TPU v7x, 512 devices: a whole 4x8x8 slice. The times are simulated.
512 devices in a mesh: dp: 128 (over y, z, core), zero: 4 (over x).
Axes of the slice: x: 4, y: 8, z: 8, core: 2. Of those that a mesh axis runs over, the one named last changes fastest.
Arguments:
- patches: bfloat16 [16384, 1280], P('dp'), may hold values from -12 to 12
- cotangent: bfloat16 [16384, 1280], P('dp'), may hold values from -6 to 6
- send_order: int32 [128, 128], P('dp'), may hold values from 0 to 127, each once within a row
- recv_order: int32 [128, 128], P('dp'), may hold values from 0 to 127, each once within a row
- segment_ids: int32 [128, 128], P('dp'), may hold values from 0 to 7, as said below
- ln_gain: float32 [1280], replicated, may hold values from 0.5 to 1.5
- ln_bias: float32 [1280], replicated, may hold values from -3 to 3
- w_qkv: bfloat16 [1280, 8, 3, 80], P(None, 'zero'), may hold values from -1 to 1
- w_out: bfloat16 [8, 80, 1280], P('zero'), may hold values from -0.25 to 0.25
Outputs:
- encoded: bfloat16 [16384, 1280], P('dp', 'zero')
- input_grad: bfloat16 [16384, 1280], P('dp', 'zero')
- w_qkv_grad: float32 [1280, 8, 3, 80], P('dp', 'zero')
- w_out_grad: float32 [8, 80, 1280], P('zero', None, 'dp')
- gain_grad: float32 [1280], P('dp')
- bias_grad: float32 [1280], P('dp')
Inputs may be any that keep to these rules, and one draw needn't show every extreme that they name: Each device's row of send_order is a permutation. Each device's row of recv_order is a permutation. `segment_ids`: numbers never fall along a device's rows; every image holds a multiple of one eighth of 128 rows; some device holds one image of all 128 rows.
All inputs are finite; a program needn't handle non-finite values.
Results may differ from a plain program's by a relative error of at most 0.025.
The roundings to bfloat16 on the way count: a program that leaves them out, or rounds other values in their place, can miss the bound.
Values may be sent and summed in bfloat16 or wider, within the bound.
No kernel may reach another device: no remote copies, remote signals or barrier semaphores. Data moves between devices by JAX's collectives and lax.ppermute only.
A program may use at most 64 MiB of HBM per device.

v0:
```python
import jax
import jax.numpy as jnp
from jax import lax
from jax.sharding import PartitionSpec as P

EPS = 1e-06


def local(patches, cotangent, send_order, recv_order, segment_ids, ln_gain, ln_bias, w_qkv, w_out):
    row_count, feature_count = patches.shape
    owners = lax.axis_size("dp")
    per_peer = row_count // owners
    shard_count = lax.axis_size("zero")
    slice_width = feature_count // shard_count
    zero_index = lax.axis_index("zero")
    send_list = send_order[0]
    recv_list = recv_order[0]
    segment_rows = segment_ids[0]
    outgoing = (
        jnp.take(patches, send_list, axis=0).reshape(owners, per_peer, feature_count),
        jnp.take(cotangent, send_list, axis=0).reshape(owners, per_peer, feature_count),
    )
    got_rows, got_grads = (
        lax.all_to_all(outgoing[0], "dp", split_axis=0, concat_axis=0, tiled=True),
        lax.all_to_all(outgoing[1], "dp", split_axis=0, concat_axis=0, tiled=True),
    )
    inputs = jnp.take(got_rows.reshape(row_count, feature_count), recv_list, axis=0)
    grads_in = jnp.take(got_grads.reshape(row_count, feature_count), recv_list, axis=0)
    heads_here = w_qkv.shape[1]
    head_dim = w_qkv.shape[3]
    score_scale = head_dim ** (-0.5)
    inputs32 = inputs.astype(jnp.float32)
    centred = inputs32 - jnp.mean(inputs32, axis=1, keepdims=True)
    inv_std = lax.rsqrt(jnp.mean(centred * centred, axis=1, keepdims=True) + EPS)
    x_hat = centred * inv_std
    normed = (x_hat * ln_gain + ln_bias).astype(jnp.bfloat16)
    flat_qkv = w_qkv.reshape(feature_count, heads_here * 3 * head_dim)
    proj_qkv = jnp.dot(normed, flat_qkv, preferred_element_type=jnp.float32).astype(jnp.bfloat16)
    proj_qkv = proj_qkv.reshape(row_count, heads_here, 3, head_dim)
    queries = proj_qkv[:, :, 0]
    key_rows = proj_qkv[:, :, 1]
    values = proj_qkv[:, :, 2]
    block_rows = min(row_count, 512)
    block_count = row_count // block_rows

    def weights_for():
        scores = (
            jnp.einsum("qhd,khd->hqk", queries, key_rows, preferred_element_type=jnp.float32)
            * score_scale
        )
        scores = jnp.where((segment_rows[:, None] == segment_rows[None, :])[None], scores, -1e30)
        row_max = jnp.max(scores, axis=2, keepdims=True)
        exponent = jnp.exp(scores - row_max)
        return (exponent / jnp.sum(exponent, axis=2, keepdims=True), queries)

    def forward_block(block_index):
        weights32, query_block = weights_for()
        return jnp.einsum(
            "hqk,khd->qhd",
            weights32.astype(jnp.bfloat16),
            values,
            preferred_element_type=jnp.float32,
        ).astype(jnp.bfloat16)

    head_out = lax.map(forward_block, jnp.arange(block_count)).reshape(
        row_count, heads_here * head_dim
    )
    wide_out = w_out.reshape(heads_here * head_dim, feature_count)
    partial_value = jnp.dot(head_out, wide_out, preferred_element_type=jnp.float32)
    head_total = lax.psum(partial_value.astype(jnp.bfloat16), "zero").astype(jnp.float32)
    encoded_rows = (inputs32 + head_total).astype(jnp.bfloat16)
    head_grad = lax.dot_general(
        grads_in, wide_out, (((1,), (1,)), ((), ())), preferred_element_type=jnp.float32
    ).astype(jnp.bfloat16)
    head_grad3 = head_grad.reshape(row_count, heads_here, head_dim)

    def backward_block(carried, block_index):
        weights32, query_block = weights_for()
        prob_grad = jnp.einsum(
            "qhd,khd->hqk", head_grad3, values, preferred_element_type=jnp.float32
        )
        row_delta = jnp.sum(prob_grad * weights32, axis=2, keepdims=True)
        score_grad = (weights32 * (prob_grad - row_delta) * score_scale).astype(jnp.bfloat16)
        query_grad = jnp.einsum(
            "hqk,khd->qhd", score_grad, key_rows, preferred_element_type=jnp.float32
        ).astype(jnp.bfloat16)
        key_grad = carried[0] + jnp.einsum(
            "hqk,qhd->khd", score_grad, query_block, preferred_element_type=jnp.float32
        )
        value_grad = carried[1] + jnp.einsum(
            "hqk,qhd->khd",
            weights32.astype(jnp.bfloat16),
            head_grad3,
            preferred_element_type=jnp.float32,
        )
        return ((key_grad, value_grad), query_grad)

    zero_block = jnp.zeros((row_count, heads_here, head_dim), jnp.float32)
    (key_grad, value_grad), query_grad = lax.scan(
        backward_block, (zero_block, zero_block), jnp.arange(block_count)
    )
    query_grad = query_grad.reshape(row_count, heads_here, head_dim)
    qkv_grad = jnp.stack(
        [query_grad, key_grad.astype(jnp.bfloat16), value_grad.astype(jnp.bfloat16)], axis=2
    )
    qkv_grad = qkv_grad.reshape(row_count, heads_here * 3 * head_dim)
    normed_part = lax.dot_general(
        qkv_grad, flat_qkv, (((1,), (1,)), ((), ())), preferred_element_type=jnp.float32
    )
    normed_grad = lax.psum(normed_part.astype(jnp.bfloat16), "zero").astype(jnp.float32)
    gain_term = jnp.sum(normed_grad * x_hat, axis=0)
    bias_term = jnp.sum(normed_grad, axis=0)
    scaled = normed_grad * ln_gain
    input_rows = (
        grads_in.astype(jnp.float32)
        + inv_std
        * (
            scaled
            - jnp.mean(scaled, axis=1, keepdims=True)
            - x_hat * jnp.mean(scaled * x_hat, axis=1, keepdims=True)
        )
    ).astype(jnp.bfloat16)
    qkv_term = lax.dot_general(
        normed, qkv_grad, (((0,), (0,)), ((), ())), preferred_element_type=jnp.float32
    )
    out_term = lax.dot_general(
        head_out, grads_in, (((0,), (0,)), ((), ())), preferred_element_type=jnp.float32
    )
    qkv_share, out_share, gain_grad, bias_grad = (
        lax.psum_scatter(qkv_term, "dp", scatter_dimension=0, tiled=True),
        lax.psum_scatter(out_term, "dp", scatter_dimension=1, tiled=True),
        lax.psum_scatter(gain_term, "dp", scatter_dimension=0, tiled=True),
        lax.psum_scatter(bias_term, "dp", scatter_dimension=0, tiled=True),
    )
    own_encoded = lax.dynamic_slice_in_dim(encoded_rows, zero_index * slice_width, slice_width, 1)
    own_inputs = lax.dynamic_slice_in_dim(input_rows, zero_index * slice_width, slice_width, 1)
    placed = (
        jnp.zeros((row_count, slice_width), jnp.bfloat16)
        .at[recv_list]
        .set(own_encoded)
        .reshape(owners, per_peer, slice_width),
        jnp.zeros((row_count, slice_width), jnp.bfloat16)
        .at[recv_list]
        .set(own_inputs)
        .reshape(owners, per_peer, slice_width),
    )
    back_encoded, back_inputs = (
        lax.all_to_all(placed[0], "dp", split_axis=0, concat_axis=0, tiled=True),
        lax.all_to_all(placed[1], "dp", split_axis=0, concat_axis=0, tiled=True),
    )
    encoded = (
        jnp.zeros((row_count, slice_width), jnp.bfloat16)
        .at[send_list]
        .set(back_encoded.reshape(row_count, slice_width))
    )
    input_grad = (
        jnp.zeros((row_count, slice_width), jnp.bfloat16)
        .at[send_list]
        .set(back_inputs.reshape(row_count, slice_width))
    )
    return (
        encoded,
        input_grad,
        qkv_share.reshape(-1, heads_here, 3, head_dim),
        out_share.reshape(heads_here, head_dim, -1),
        gain_grad,
        bias_grad,
    )


def solution(mesh):
    return jax.shard_map(
        local,
        mesh=mesh,
        in_specs=(
            P("dp", None),
            P("dp", None),
            P("dp", None),
            P("dp", None),
            P("dp", None),
            P(),
            P(),
            P(None, "zero", None, None),
            P("zero", None, None),
        ),
        out_specs=(
            P("dp", "zero"),
            P("dp", "zero"),
            P("dp", "zero", None, None),
            P("zero", None, "dp"),
            P("dp"),
            P("dp"),
        ),
        check_vma=False,
    )
```

profile of v0, /device:TPU:1, one launch (start us, length us, event | category | flops | bytes accessed | tf_op | source)
XLA Modules:
  0.0 669.3 jit_solution(16628705276009521839)
XLA Ops:
  7.2 0.8 compare_select_fusion.1
  7.9 0.7 compare_and_fusion
  8.6 2.2 gather_fusion.2
  10.9 0.9 gather_fusion
  11.8 0.1 select_bitcast_fusion
  11.9 0.5 broadcast.151
  12.4 0.8 reduce
  13.3 0.8 reshape.288
  14.1 18.6 %all-to-all-start.2 = ((bf16[128,2,640]{2,1,0:T(2,128)(2,1)}), bf16[128,2,640]{2,1,0:T(2,128)(2,1)S(1)}, u32[]{:S(2)}, u32[]{:S(2)}) async-start(bf16[128,2,640]{2,1,0:T(2,128)(2,1)} %reshape.288), calls=%async_computation.2 | async-start | bytes 655360 | tf_op jit(solution)/shard_map/all_to_all | solution.py:25
  32.6 0.8 reduce.1
  33.5 0.8 reshape.284
  34.3 13.9 %all-to-all-done.2 = bf16[128,2,640]{2,1,0:T(2,128)(2,1)S(1)} async-done(((bf16[128,2,640]{2,1,0:T(2,128)(2,1)}), bf16[128,2,640]{2,1,0:T(2,128)(2,1)S(1)}, u32[]{:S(2)}, u32[]{:S(2)}) %all-to-all-start.2) | async-done | bytes 327712 | tf_op jit(solution)/shard_map/all_to_all | solution.py:25
  48.2 7.0 %all-to-all-start = ((bf16[128,2,640]{2,1,0:T(2,128)(2,1)}), bf16[128,2,640]{2,1,0:T(2,128)(2,1)S(1)}, u32[]{:S(2)}, u32[]{:S(2)}) async-start(bf16[128,2,640]{2,1,0:T(2,128)(2,1)} %reshape.284), calls=%async_computation | async-start | bytes 655360 | tf_op jit(solution)/shard_map/all_to_all | solution.py:24
  55.4 0.3 reshape.289
  55.7 0.9 gather_fusion.3
  56.6 0.2 copy.76
  56.8 14.1 %all-to-all-done = bf16[128,2,640]{2,1,0:T(2,128)(2,1)S(1)} async-done(((bf16[128,2,640]{2,1,0:T(2,128)(2,1)}), bf16[128,2,640]{2,1,0:T(2,128)(2,1)S(1)}, u32[]{:S(2)}, u32[]{:S(2)}) %all-to-all-start) | async-done | bytes 327712 | tf_op jit(solution)/shard_map/all_to_all | solution.py:24
  70.9 0.3 reshape.285
  71.2 0.9 gather_fusion.1
  72.1 0.2 copy.66
  72.3 0.2 convert_reduce_fusion.1
  72.5 0.2 multiply_reduce_fusion.1
  72.8 0.2 copy-done.4
  73.0 0.7 convolution_convert_fusion
  73.7 0.3 fusion.55
  74.0 0.2 convolution_convert_fusion.5
  74.2 0.3 convolution_convert_fusion.1
  74.4 0.2 fusion.13
  74.6 0.2 fusion.40
  74.8 0.2 fusion.11
  75.0 0.2 fusion.12
  75.3 1.2 fusion.2
  76.4 1.4 fusion.3
  77.9 1.4 fusion.56
  79.3 2.1 fusion.54
  81.5 1.3 dynamic-slice
  83.4 40.4 %all-reduce.12.cloned.1.call-done = (bf16[128,1280]{0,1:T(8,128)(2,1)}, bf16[128,1280]{0,1:T(8,128)(2,1)}) async-done(((bf16[128,1280]{0,1:T(8,128)(2,1)}, bf16[128,1280]{0,1:T(8,128)(2,1)}), (bf16[128,1280]{0,1:T(8,128)(2,1)}, bf16[128,1280]{0,1:T(8,128)(2,1)})) %all-reduce.12.cloned.1.call-update) | async-done | bytes 655376 | tf_op jit(solution)/shard_map/psum | solution.py:70
  123.8 1.0 fusion.23
  124.8 0.1 copy.71
  124.9 1.1 scatter_custom_fusion
  126.0 0.7 reduce.2
  126.7 0.8 reshape.286
  127.4 16.3 %all-to-all-start.1 = ((bf16[128,2,160]{2,1,0:T(2,128)(2,1)}), bf16[128,2,160]{2,1,0:T(2,128)(2,1)S(1)}, u32[]{:S(2)}, u32[]{:S(2)}) async-start(bf16[128,2,160]{2,1,0:T(2,128)(2,1)} %reshape.286), calls=%async_computation.1 | async-start | bytes 262144 | tf_op jit(solution)/shard_map/all_to_all | solution.py:148
  143.7 0.6 fusion.14
  144.4 0.1 copy.82
  144.5 1.1 scatter_custom_fusion.2
  145.6 0.7 reduce.3
  146.3 0.7 reshape.290
  147.0 9.0 %all-to-all-done.1 = bf16[128,2,160]{2,1,0:T(2,128)(2,1)S(1)} async-done(((bf16[128,2,160]{2,1,0:T(2,128)(2,1)}), bf16[128,2,160]{2,1,0:T(2,128)(2,1)S(1)}, u32[]{:S(2)}, u32[]{:S(2)}) %all-to-all-start.1) | async-done | bytes 81952 | tf_op jit(solution)/shard_map/all_to_all | solution.py:148
  156.0 6.7 %all-to-all-start.3 = ((bf16[128,2,160]{2,1,0:T(2,128)(2,1)}), bf16[128,2,160]{2,1,0:T(2,128)(2,1)S(1)}, u32[]{:S(2)}, u32[]{:S(2)}) async-start(bf16[128,2,160]{2,1,0:T(2,128)(2,1)} %reshape.290), calls=%async_computation.3 | async-start | bytes 262144 | tf_op jit(solution)/shard_map/all_to_all | solution.py:149
  162.8 491.6 %all-reduce.4 = (f32[1280]{0:T(1024)S(1)}, f32[1280]{0:T(1024)S(1)}) all-reduce(f32[1280]{0:T(1024)S(1)} %get-tuple-element.76, f32[1280]{0:T(1024)S(1)} %get-tuple-element.79), channel_id=4, replica_groups=mesh['dp'=128,'zero'=4] {'dp'}, use_global_device_ids=true, to_apply=%region_16.18.clone | all-reduce | flops 2560 | bytes 20480
  654.4 0.6 dynamic-slice.5
  655.0 0.6 dynamic-slice.7
  655.6 0.2 reshape.287
  655.7 1.1 scatter_custom_fusion.1
  656.8 0.7 copy.87
  657.6 0.2 reshape.291
  657.7 1.1 scatter_custom_fusion.3
  658.8 0.7 copy.88
  659.5 0.8 constant_dynamic-slice_fusion.1
  660.4 0.7 constant_dynamic-slice_fusion
  661.1 0.7 reshape.193
  661.8 0.1 reshape.191
  661.9 0.6 copy.89
  (39 shorter events, 0.5 us)
Async XLA Ops:
  7.2 65.6 %copy-start = (bf16[1280,2,3,80]{0,3,2,1:T(8,128)(2,1)S(1)}, bf16[1280,2,3,80]{0,3,2,1:T(8,128)(2,1)}, u32[]{:S(2)}) copy-start(bf16[1280,2,3,80]{0,3,2,1:T(8,128)(2,1)} %param.18) | copy-start | bytes 3686404
  8.6 2.2 copy-start.1
  14.0 41.2 %copy-start.7 = (s32[1,128]{1,0:T(1,128)S(1)}, s32[1,128]{1,0:T(1,128)}, u32[]{:S(2)}) copy-start(s32[1,128]{1,0:T(1,128)} %param.14) | copy-start | bytes 1540
  14.0 41.2 %copy-start.6 = (s32[1,128]{1,0:T(1,128)S(1)}, s32[1,128]{1,0:T(1,128)}, u32[]{:S(2)}) copy-start(s32[1,128]{1,0:T(1,128)} %param.15) | copy-start | bytes 1540
  14.1 34.1 %all-to-all-start.2 = ((bf16[128,2,640]{2,1,0:T(2,128)(2,1)}), bf16[128,2,640]{2,1,0:T(2,128)(2,1)S(1)}, u32[]{:S(2)}, u32[]{:S(2)}) async-start(bf16[128,2,640]{2,1,0:T(2,128)(2,1)} %reshape.288), calls=%async_computation.2 | async-start | bytes 655360 | tf_op jit(solution)/shard_map/all_to_all | solution.py:25
  48.2 22.7 %all-to-all-start = ((bf16[128,2,640]{2,1,0:T(2,128)(2,1)}), bf16[128,2,640]{2,1,0:T(2,128)(2,1)S(1)}, u32[]{:S(2)}, u32[]{:S(2)}) async-start(bf16[128,2,640]{2,1,0:T(2,128)(2,1)} %reshape.284), calls=%async_computation | async-start | bytes 655360 | tf_op jit(solution)/shard_map/all_to_all | solution.py:24
  55.2 68.6 %all-reduce.12.cloned.1.call-start = ((), (), s32[]{:S(2)}) async-start(), calls=%async_computation.5 | async-start | bytes 1310720 | tf_op jit(solution)/shard_map/psum | solution.py:70
  72.3 0.7 copy-start.4
  72.3 0.7 copy-start.5
  73.0 1.1 copy-start.2
  77.9 581.7 %all-reduce.10.cloned.1.call-start = ((), (), s32[]{:S(2)}) async-start(), calls=%async_computation.4 | async-start | bytes 7864320
  123.8 19.9 %copy-start.3 = (bf16[128,1280]{0,1:T(8,128)(2,1)S(1)}, bf16[128,1280]{0,1:T(8,128)(2,1)}, u32[]{:S(2)}) copy-start(bf16[128,1280]{0,1:T(8,128)(2,1)} %get-tuple-element.85) | copy-start | bytes 983044
  127.4 28.6 %all-to-all-start.1 = ((bf16[128,2,160]{2,1,0:T(2,128)(2,1)}), bf16[128,2,160]{2,1,0:T(2,128)(2,1)S(1)}, u32[]{:S(2)}, u32[]{:S(2)}) async-start(bf16[128,2,160]{2,1,0:T(2,128)(2,1)} %reshape.286), calls=%async_computation.1 | async-start | bytes 262144 | tf_op jit(solution)/shard_map/all_to_all | solution.py:148
  143.7 19.0 %copy-start.8 = (s32[1,128]{1,0:T(1,128)S(1)}, s32[1,128]{1,0:T(1,128)}, u32[]{:S(2)}) copy-start(s32[1,128]{1,0:T(1,128)} %param.13) | copy-start | bytes 1540
  156.0 501.6 %all-to-all-start.3 = ((bf16[128,2,160]{2,1,0:T(2,128)(2,1)}), bf16[128,2,160]{2,1,0:T(2,128)(2,1)S(1)}, u32[]{:S(2)}, u32[]{:S(2)}) async-start(bf16[128,2,160]{2,1,0:T(2,128)(2,1)} %reshape.290), calls=%async_computation.3 | async-start | bytes 262144 | tf_op jit(solution)/shard_map/all_to_all | solution.py:149
Sparse Core Ops, SparseCore 0:
  78.0 45.7 all-reduce.11
  127.2 209.8 all-reduce.9
where the time goes:
time: 674 us; the launch traced here: 669 us
  blocking collectives  492 us (73%)
  waiting for transfers between devices  77.4 us (11%)
  starting transfers between devices  48.7 us (7%)
  local copies, waits for them, and re-layouts  21.5 us (3%)
  between operations  15.1 us (2%)
  matrix products  8.25 us (1%)
  other arithmetic  6.78 us (1%)
    unnamed x1, blocking collectives  492 us
    psum x1, waiting for transfers between devices, local(): lax.psum(partial_value.astype(jnp.bfloat16), 'zero').astype(jnp.float32)  40.4 us
    all_to_all x1, starting transfers between devices, local(): lax.all_to_all(outgoing[1], 'dp', split_axis=0, concat_axis=0, tiled=True)  18.6 us
    all_to_all x1, starting transfers between devices, local(): lax.all_to_all(placed[0], 'dp', split_axis=0, concat_axis=0, tiled=True)  16.3 us
    all_to_all x1, waiting for transfers between devices, local(): lax.all_to_all(outgoing[0], 'dp', split_axis=0, concat_axis=0, tiled=True)  14.1 us
    all_to_all x1, waiting for transfers between devices, local(): lax.all_to_all(outgoing[1], 'dp', split_axis=0, concat_axis=0, tiled=True)  13.9 us
  transfers between devices with their start and end apart: 6, of which 4 were waited for; matrix products, arithmetic and copies ran while one was open for 3% of the time, Pallas kernels for 0%

commit v1 on v0

v1 whole, which is shorter than its diff:
```python
import jax
import jax.numpy as jnp
import numpy as np
from jax import lax
from jax.experimental import pallas as pl
from jax.experimental.pallas import tpu as pltpu
from jax.sharding import PartitionSpec as P

EPS = 1e-06
R = 128
D = 1280
HD = 80
HG = 2
NQ = HG * 3 * HD
NO = HG * HD
QW = D // 4
QP = 384
F32 = jnp.float32
BF = jnp.bfloat16
GAIN_AT = 64
BIAS_AT = 74
MEAN_AT = 84

_cp = pltpu.CompilerParams(vmem_limit_bytes=24 * 1024 * 1024)


def dg(a, b, ca, cb):
    return lax.dot_general(a, b, (((ca,), (cb,)), ((), ())), preferred_element_type=F32)


def call(body, outs, *args, smem=(), cost=None):
    return pl.pallas_call(
        body,
        out_shape=tuple(jax.ShapeDtypeStruct(s, d) for s, d in outs),
        in_specs=[
            pl.BlockSpec(memory_space=pltpu.SMEM if i in smem else pltpu.VMEM)
            for i in range(len(args))
        ],
        out_specs=tuple(pl.BlockSpec(memory_space=pltpu.VMEM) for _ in outs),
        compiler_params=_cp,
        cost_estimate=cost,
    )(*args)


def lane(shape):
    return lax.broadcasted_iota(jnp.int32, shape, 1)


def sub(shape):
    return lax.broadcasted_iota(jnp.int32, shape, 0)


def gather_body(send_ref, x_ref, o_ref):
    pick = (sub((R, R)) == send_ref[...]).astype(F32).astype(BF)
    o_ref[...] = dg(pick, x_ref[...], 0, 0).astype(BF)


def norm_stats(x):
    mean = jnp.mean(x, axis=1, keepdims=True)
    centred = x - mean
    inv = lax.rsqrt(jnp.mean(centred * centred, axis=1, keepdims=True) + EPS)
    return mean, inv, centred * inv


def fwd_body(
    x_ref, recv_ref, seg_ref, gain_ref, bias_ref, wq_ref, wo_ref,
    p_ref, normed_ref, qkv_ref, w32_ref, ho_ref, stat_ref,
):
    x = x_ref[...].astype(F32)
    mean, inv, xh = norm_stats(x)
    stat_ref[...] = jnp.where(lane((R, R)) < 64, mean, inv)
    normed = (xh * gain_ref[...] + bias_ref[...]).astype(BF)
    normed_ref[...] = normed
    qkv = dg(wq_ref[...], normed, 1, 1).astype(BF)
    qkv_ref[...] = qkv
    place = sub((R, R)) == recv_ref[...]
    seg = jnp.sum(jnp.where(place, seg_ref[...], 0), axis=1, keepdims=True)
    group = (seg == lane((R, R))).astype(F32).astype(BF)
    same = dg(group, group, 1, 1) > 0.5
    outs = []
    for h in range(HG):
        q = qkv[h * 3 * HD : h * 3 * HD + HD]
        k = qkv[h * 3 * HD + HD : h * 3 * HD + 2 * HD]
        v = qkv[h * 3 * HD + 2 * HD : (h + 1) * 3 * HD]
        s = jnp.where(same, dg(q, k, 0, 0) * (HD**-0.5), -1e30)
        e = jnp.exp(s - jnp.max(s, axis=1, keepdims=True))
        w = e / jnp.sum(e, axis=1, keepdims=True)
        w32_ref[h] = w
        outs.append(dg(v, w.astype(BF), 1, 1).astype(BF))
    ho = jnp.concatenate(outs, axis=0)
    ho_ref[...] = ho
    p = dg(ho, wo_ref[...], 0, 0)
    pad = jnp.zeros((R, QP - QW), F32)
    for g in range(4):
        part = jnp.concatenate([p[:, g * QW : (g + 1) * QW], pad], axis=1)
        p_ref[g] = part.astype(BF)


def bwd_body(
    x_ref, g_ref, gain_ref, wq_ref, wo_ref, qkv_ref, w32_ref, sel_ref, place_ref,
    n_ref, qg_ref,
):
    _, _, xh = norm_stats(x_ref[...].astype(F32))
    dh = dg(wo_ref[...], g_ref[...], 1, 1).astype(BF)
    parts = []
    for h in range(HG):
        q = qkv_ref[h * 3 * HD : h * 3 * HD + HD]
        k = qkv_ref[h * 3 * HD + HD : h * 3 * HD + 2 * HD]
        v = qkv_ref[h * 3 * HD + 2 * HD : (h + 1) * 3 * HD]
        dhh = dh[h * HD : (h + 1) * HD]
        w = w32_ref[h]
        pg = dg(dhh, v, 0, 0)
        delta = jnp.sum(pg * w, axis=1, keepdims=True)
        sg = (w * (pg - delta) * (HD**-0.5)).astype(BF)
        parts.append(dg(k, sg, 1, 1).astype(BF))
        parts.append(dg(q, sg, 1, 0).astype(BF))
        parts.append(dg(dhh, w.astype(BF), 1, 0).astype(BF))
    qg = jnp.concatenate(parts, axis=0)
    qg_ref[...] = qg
    n = dg(qg, wq_ref[...], 0, 0)
    nx = n * xh
    u = n * gain_ref[...]
    m1 = jnp.sum(u, axis=1, keepdims=True) * (1.0 / D)
    m2 = jnp.sum(u * xh, axis=1, keepdims=True) * (1.0 / D)
    gain_row = jnp.sum(nx, axis=0, keepdims=True)
    bias_row = jnp.sum(n, axis=0, keepdims=True)
    sel = sel_ref[...].astype(F32)
    extra = dg((sel * gain_row).astype(BF), place_ref[0], 1, 0)
    extra = extra + dg((sel * bias_row).astype(BF), place_ref[1], 1, 0)
    ln = lane((R, R))
    for j, m in enumerate((m1, m2)):
        hi = m.astype(BF).astype(F32)
        extra = jnp.where(ln == MEAN_AT + 2 * j, hi, extra)
        extra = jnp.where(ln == MEAN_AT + 2 * j + 1, m - hi, extra)
    for g in range(4):
        part = jnp.concatenate([n[:, g * QW : (g + 1) * QW], extra[:, 64:]], axis=1)
        n_ref[g] = part.astype(BF)


def wgrad_body(c_ref, normed_ref, g_ref, qg_ref, ho_ref, keep_ref, send_ref):
    left = jnp.concatenate([normed_ref[...], g_ref[...]], axis=0)
    c = c_ref[0]
    for out, head in ((send_ref, 1 - c), (keep_ref, c)):
        a = qg_ref[pl.ds(pl.multiple_of(head * 3 * HD, 3 * HD), 3 * HD), :]
        b = ho_ref[pl.ds(pl.multiple_of(head * HD, HD), HD), :]
        right = jnp.concatenate(
            [
                jnp.concatenate([a, jnp.zeros((3 * HD, R), BF)], axis=1),
                jnp.concatenate([jnp.zeros((HD, R), BF), b], axis=1),
            ],
            axis=0,
        )
        out[...] = dg(left, right, 0, 1).astype(out.dtype)


def post_body(p_ref, n_ref, x_ref, g_ref, stat_ref, gain_ref, o_ref):
    ps = jnp.sum(p_ref[...].astype(F32), axis=0)
    ns = jnp.sum(n_ref[...].astype(F32), axis=0)
    x = x_ref[...].astype(F32)
    mean = stat_ref[:, 0:1]
    inv = stat_ref[:, 64:65]
    xh = (x - mean) * inv
    tile = ns[:, 256:]
    ln = lane((R, R))
    m1 = jnp.sum(jnp.where((ln == MEAN_AT) | (ln == MEAN_AT + 1), tile, 0.0), axis=1, keepdims=True)
    m2 = jnp.sum(
        jnp.where((ln == MEAN_AT + 2) | (ln == MEAN_AT + 3), tile, 0.0), axis=1, keepdims=True
    )
    o_ref[:, :QP] = (x + ps).astype(BF)
    grad = g_ref[...].astype(F32) + inv * (ns * gain_ref[...] - m1 - xh * m2)
    o_ref[:, QP : QP + 256] = grad[:, :256].astype(BF)
    o_ref[:, QP + 256 :] = jnp.where(ln < 64, grad[:, 256:], tile).astype(BF)


def final_body(send_ref, b_ref, e_ref, i_ref, s_ref):
    pick = (sub((R, R)) == send_ref[...]).astype(F32).astype(BF)
    e_ref[...] = dg(b_ref[:, :QP], pick, 0, 1)[:QW].astype(BF)
    i_ref[...] = dg(b_ref[:, QP:], pick, 0, 1)[:QW].astype(BF)
    s_ref[...] = jnp.broadcast_to(
        jnp.sum(b_ref[:, QP + 256 :].astype(F32), axis=0, keepdims=True), (8, R)
    )


_f = np.arange(D)
SEL = (_f[None, :] // 10 == np.arange(R)[:, None]).astype(np.float32)
PLACE = np.stack(
    [(_f[:, None] % 10 + at == np.arange(R)[None, :]).astype(np.float32) for at in (GAIN_AT, BIAS_AT)]
)


def local(patches, cotangent, send_order, recv_order, segment_ids, ln_gain, ln_bias, w_qkv, w_out):
    zero = lax.axis_index("zero")
    core = lax.rem(lax.axis_index("dp"), 2)
    wq = w_qkv.transpose(1, 2, 3, 0).reshape(NQ, D)
    wo = w_out.reshape(NO, D)
    gain = ln_gain.reshape(1, D)
    bias = ln_bias.reshape(1, D)
    sel = jnp.asarray(SEL, BF)
    place = jnp.asarray(PLACE, BF)

    (xs,) = call(gather_body, [((R, D), BF)], send_order, patches)
    (gs,) = call(gather_body, [((R, D), BF)], send_order, cotangent)
    x = lax.all_to_all(xs, "dp", 0, 0, tiled=True)
    g = lax.all_to_all(gs, "dp", 0, 0, tiled=True)

    p4, normed, qkv, w32, ho, stat = call(
        fwd_body,
        [
            ((4, R, QP), BF),
            ((R, D), BF),
            ((NQ, R), BF),
            ((HG, R, R), F32),
            ((NO, R), BF),
            ((R, R), F32),
        ],
        x, recv_order, segment_ids, gain, bias, wq, wo,
    )
    p4 = lax.all_to_all(p4, "zero", 0, 0, tiled=True)
    n4, qg = call(
        bwd_body,
        [((4, R, QP), BF), ((NQ, R), BF)],
        x, g, gain, wq, wo, qkv, w32, sel, place,
    )
    n4 = lax.all_to_all(n4, "zero", 0, 0, tiled=True)
    keep, send = call(
        wgrad_body,
        [((D, 4 * HD), F32), ((D, 4 * HD), BF)],
        core.reshape(1), normed, g, qg, ho,
        smem=(0,),
    )
    got = lax.ppermute(send, "dp", [(i, i ^ 1) for i in range(128)])
    wg = (keep + got.astype(F32)).astype(BF).reshape(R, 40 * HD)
    wg = lax.all_to_all(wg, "dp", 0, 0, tiled=True)

    def quarter(a):
        a = lax.dynamic_slice_in_dim(a, zero * QW, QW, 1)
        return jnp.pad(a, ((0, 0), (0, QP - QW)))

    (back,) = call(
        post_body,
        [((R, 2 * QP), BF)],
        p4, n4, quarter(x), quarter(g), stat, quarter(gain),
    )
    back = lax.all_to_all(back, "dp", 0, 0, tiled=True)
    enc, grad, sums = call(
        final_body,
        [((QW, R), BF), ((QW, R), BF), ((8, R), F32)],
        send_order, back,
    )
    wsum = jnp.sum(wg.reshape(64, 2, 10, 4 * HD).astype(F32), axis=0)
    qkv_share = wsum[:, :, : 3 * HD].reshape(2, 10, 3, HD).transpose(1, 0, 2, 3)
    out_share = wsum[:, :, 3 * HD :].transpose(0, 2, 1)
    return (
        enc.T,
        grad.T,
        qkv_share,
        out_share,
        sums[0, GAIN_AT : GAIN_AT + 10],
        sums[0, BIAS_AT : BIAS_AT + 10],
    )


def solution(mesh):
    return jax.shard_map(
        local,
        mesh=mesh,
        in_specs=(
            P("dp", None),
            P("dp", None),
            P("dp", None),
            P("dp", None),
            P("dp", None),
            P(),
            P(),
            P(None, "zero", None, None),
            P("zero", None, None),
        ),
        out_specs=(
            P("dp", "zero"),
            P("dp", "zero"),
            P("dp", "zero", None, None),
            P("zero", None, "dp"),
            P("dp"),
            P("dp"),
        ),
        check_vma=False,
    )
```

time: 674 us -> 175 us (0.26)
  blocking collectives: 492 us -> 11.7 us
  waiting for transfers between devices: 77.4 us -> 58.1 us
  between operations: 15.1 us -> 1.02 us
  other arithmetic: 6.78 us -> 15.2 us
  matrix products: 8.25 us -> 0 us
  Pallas kernels: 0 us -> 7.26 us
    unnamed x1 -> x0, blocking collectives: 492 us -> none
    psum x1 -> x0, waiting for transfers between devices: 40.4 us -> none  [local(): lax.psum(partial_value.astype(jnp.bfloat16), 'zero').astype(jnp.float32)]
    all_to_all x4 -> x5, waiting for transfers between devices: 36.9 us -> 58.1 us  [the longest x1 24.8 us: local(): wg = lax.all_to_all(wg, 'dp', 0, 0, tiled=True)]
    all_to_all x0 -> x1, blocking collectives: none -> 11.7 us  [local(): p4 = lax.all_to_all(p4, 'zero', 0, 0, tiled=True)]
    all_to_all x0 -> x4, other arithmetic: none -> 8.02 us  [the longest x1 5.61 us: local(): wg = lax.all_to_all(wg, 'dp', 0, 0, tiled=True)]
    dot_general x11 -> x0, matrix products: 7.98 us -> none  [the longest x1 2.09 us: local(): lax.dot_general(normed, qkv_grad, (((0,), (0,)), ((), ())), preferred_ele...]
    pallas_call x0 -> x7, Pallas kernels: none -> 7.26 us  [call(): pl.pallas_call(body, out_shape=tuple((jax.ShapeDtypeStruct(s, d) for s, d...]
    all_to_all x4 -> x5, starting transfers between devices: 48.6 us -> 51.5 us  [the longest x1 18.6 us: local(): x = lax.all_to_all(xs, 'dp', 0, 0, tiled=True)]
  transfers between devices with their start and end apart: 6 -> 6, of which waited for: 4 -> 4; matrix products, arithmetic and copies ran while one was open for 3% -> 9% of each run, Pallas kernels for 0% -> 1%
where the time goes in v1:
time: 175 us; the launch traced here: 174 us
  waiting for transfers between devices  58.1 us (33%)
  starting transfers between devices  55.3 us (32%)
  local copies, waits for them, and re-layouts  25.3 us (14%)
  other arithmetic  15.2 us (9%)
  blocking collectives  11.7 us (7%)
  Pallas kernels  7.26 us (4%)
    all_to_all x1, waiting for transfers between devices, local(): wg = lax.all_to_all(wg, 'dp', 0, 0, tiled=True)  24.8 us
    all_to_all x1, starting transfers between devices, local(): x = lax.all_to_all(xs, 'dp', 0, 0, tiled=True)  18.6 us
    all_to_all x1, waiting for transfers between devices, local(): g = lax.all_to_all(gs, 'dp', 0, 0, tiled=True)  14.9 us
    all_to_all x1, starting transfers between devices, local(): wg = lax.all_to_all(wg, 'dp', 0, 0, tiled=True)  13.8 us
    all_to_all x1, waiting for transfers between devices, local(): x = lax.all_to_all(xs, 'dp', 0, 0, tiled=True)  13.6 us
    unnamed x41, local copies, waits for them, and re-layouts  12 us
    all_to_all x1, blocking collectives, local(): p4 = lax.all_to_all(p4, 'zero', 0, 0, tiled=True)  11.7 us
    all_to_all x1, starting transfers between devices, local(): g = lax.all_to_all(gs, 'dp', 0, 0, tiled=True)  8.02 us
  transfers between devices with their start and end apart: 6, of which 4 were waited for; matrix products, arithmetic and copies ran while one was open for 9% of the time, Pallas kernels for 1%

profile of v1, /device:TPU:1, one launch (start us, length us, event | category | flops | bytes accessed | tf_op | source)
XLA Modules:
  0.0 173.8 jit_solution(8455707755001704374)
XLA Ops:
  0.6 0.0 copy-start.4
  0.6 1.0 copy-done.4
  1.6 0.7 copy-done.6
  2.3 0.3 shard_map.154
  2.6 0.5 broadcast.8
  3.1 0.8 reduce.2
  3.9 0.8 reshape.55
  4.7 18.6 %all-to-all-start = ((bf16[128,2,640]{2,1,0:T(2,128)(2,1)}), bf16[128,2,640]{2,1,0:T(2,128)(2,1)S(1)}, u32[]{:S(2)}, u32[]{:S(2)}) async-start(bf16[128,2,640]{2,1,0:T(2,128)(2,1)} %reshape.55), calls=%async_computation | async-start | bytes 655360 | tf_op jit(solution)/shard_map/all_to_all | solution.py:203
  23.3 0.0 copy-done.5
  23.3 0.0 copy-done.7
  23.3 0.3 shard_map.156
  23.6 0.8 reduce.3
  24.4 0.8 reshape.57
  25.2 13.6 %all-to-all-done = bf16[128,2,640]{2,1,0:T(2,128)(2,1)S(1)} async-done(((bf16[128,2,640]{2,1,0:T(2,128)(2,1)}), bf16[128,2,640]{2,1,0:T(2,128)(2,1)S(1)}, u32[]{:S(2)}, u32[]{:S(2)}) %all-to-all-start) | async-done | bytes 327712 | tf_op jit(solution)/shard_map/all_to_all | solution.py:203
  38.8 8.0 %all-to-all-start.2 = ((bf16[128,2,640]{2,1,0:T(2,128)(2,1)}), bf16[128,2,640]{2,1,0:T(2,128)(2,1)}, u32[]{:S(2)}, u32[]{:S(2)}) async-start(bf16[128,2,640]{2,1,0:T(2,128)(2,1)} %reshape.57), calls=%async_computation.2 | async-start | bytes 655360 | tf_op jit(solution)/shard_map/all_to_all | solution.py:204
  46.9 0.0 copy-done.12
  46.9 0.0 copy-done.13
  46.9 0.3 reshape.56
  47.2 0.0 copy-start.10
  47.2 0.0 copy-start
  47.2 0.0 copy-start.1
  47.2 0.0 copy-start.8
  47.2 0.0 copy-start.9
  47.3 14.9 %all-to-all-done.2 = bf16[128,2,640]{2,1,0:T(2,128)(2,1)} async-done(((bf16[128,2,640]{2,1,0:T(2,128)(2,1)}), bf16[128,2,640]{2,1,0:T(2,128)(2,1)}, u32[]{:S(2)}, u32[]{:S(2)}) %all-to-all-start.2) | async-done | bytes 327712 | tf_op jit(solution)/shard_map/all_to_all | solution.py:204
  62.2 2.5 %reshape.58 = bf16[128,1,1280]{2,1,0:T(2,128)(2,1)S(1)} reshape(bf16[128,2,640]{2,1,0:T(2,128)(2,1)} %all-to-all-done.2) | data formatting | bytes 655360
  64.7 0.0 copy-start.11
  64.7 0.0 copy-start.2
  64.7 0.0 copy-start.3
  64.8 0.8 copy-done.11
  65.6 0.0 copy-done.8
  65.6 2.0 %shard_map.155 = (bf16[4,128,384]{2,1,0:T(8,128)(2,1)S(1)}, bf16[128,1280]{1,0:T(8,128)(2,1)S(1)}, bf16[480,128]{1,0:T(8,128)(2,1)S(1)}, f32[2,128,128]{2,1,0:T(...) custom-call(bf16[128,1280]{1,0:T(8,128)(2,1)S(1)} %bitcast.40, s32[1,128]{1,0:T(1,128)S(1)} %copy-done.8, ...), custom_call_target="tpu_custom_call" | custom-call | tf_op jit(solution)/shard_map/pallas_call | solution.py:32
  67.6 2.7 %shard_map.157 = (bf16[4,128,384]{2,1,0:T(8,128)(2,1)}, bf16[480,128]{1,0:T(8,128)(2,1)S(1)}) custom-call(bf16[128,1280]{1,0:T(8,128)(2,1)S(1)} %bitcast.41, bf16[128,1280]{1,0:T(8,128)(2,1)S(1)} %bitcast.38, f32[1,1280]{1,0:T(1,128)S(1)} %reshape.47.gain_ref, bf16[480,1280]{1,0:T(8,128)(2,1)S(1)} %bitcast.37, bf16[160,1280]{1,0:T(8,128)(2,1)S(1)} %bitcast.43, ...), custom_call_target="tpu_custom_call" | custom-call | tf_op jit(solution)/shard_map/pallas_call | solution.py:32
  70.3 0.9 shard_map.160
  71.2 1.3 copy.35
  72.5 3.7 %collective-permute-start = (bf16[1280,320]{0,1:T(8,128)(2,1)}, bf16[1280,320]{0,1:T(8,128)(2,1)}, u32[]{:S(2)}, u32[]{:S(2)}) collective-permute-start(bf16[1280,320]{0,1:T(8,128)(2,1)} %copy.35), channel_id=1, source_target_pairs={{0,4},{4,0},{8,12},{12,8},{16,20},{20,16},{24,28},{28,24},{32,36},... | collective-permute-start | bytes 2457608 | tf_op jit(solution)/shard_map/ppermute | solution.py:231
  76.2 11.7 %all_to_all.53.p_ref = bf16[4,128,384]{2,1,0:T(8,128)(2,1)S(1)} all-to-all(bf16[4,128,384]{2,1,0:T(8,128)(2,1)S(1)} %get-tuple-element.19), channel_id=1, replica_groups=mesh['dp'=128,'zero'=4] {'zero'}, dimensions={0} | all-to-all | bytes 786432 | tf_op jit(solution)/shard_map/all_to_all | solution.py:218
  88.0 3.5 %all-to-all-start.3 = ((bf16[4,128,384]{2,1,0:T(8,128)(2,1)}), bf16[4,128,384]{2,1,0:T(8,128)(2,1)S(1)}, u32[]{:S(2)}, u32[]{:S(2)}) async-start(bf16[4,128,384]{2,1,0:T(8,128)(2,1)} %get-tuple-element.22), calls=%async_computation.3 | async-start | bytes 786432 | tf_op jit(solution)/shard_map/all_to_all | solution.py:224
  91.5 0.1 dynamic-slice.5
  91.5 1.8 %constant_dynamic-slice_fusion = (bf16[128,1,320]{2,1,0:T(2,128)(2,1)S(1)}, bf16[128,1,320]{2,1,0:T(2,128)(2,1)S(1)}) fusion(bf16[128,1,1280]{2,1,0:T(2,128)(2,1)} %copy-done.11, s32[]{:T(128)S(6)} %select_n.2, bf16[128,1,1280]{2,1,0:T(2,128)(2,1)} %copy-done.10), kind=kLoop, calls=%fused_computation.10 | loop fusion | bytes 327684 | tf_op jit(solution)/shard_map/dynamic_slice | solution.py:236
  93.4 4.7 %all-to-all-done.3.n_ref = bf16[4,128,384]{2,1,0:T(8,128)(2,1)S(1)} async-done(((bf16[4,128,384]{2,1,0:T(8,128)(2,1)}), bf16[4,128,384]{2,1,0:T(8,128)(2,1)S(1)}, u32[]{:S(2)}, u32[]{:S(2)}) %all-to-all-start.3) | async-done | bytes 393248 | tf_op jit(solution)/shard_map/all_to_all | solution.py:224
  98.1 0.2 shard_map.158
  98.3 0.7 reduce.4
  99.0 0.7 reshape.59
  99.8 7.7 %all-to-all-start.4 = ((bf16[128,2,384]{2,1,0:T(2,128)(2,1)}), bf16[128,2,384]{2,1,0:T(2,128)(2,1)S(1)}, u32[]{:S(2)}, u32[]{:S(2)}) async-start(bf16[128,2,384]{2,1,0:T(2,128)(2,1)} %reshape.59), calls=%async_computation.4 | async-start | bytes 393216 | tf_op jit(solution)/shard_map/all_to_all | solution.py:244
  107.5 0.0 collective-permute-done
  107.5 1.6 copy.36
  109.0 1.1 add_convert_fusion
  110.2 4.9 %all_to_all.46 = bf16[128,1,3200]{2,1,0:T(2,128)(2,1)S(1)} reshape(bf16[1280,320]{1,0:T(8,128)(2,1)} %add_convert_fusion) | data formatting | bytes 1638400 | tf_op jit(solution)/shard_map/all_to_all | solution.py:233
  115.0 5.6 %reduce.5 = bf16[128,3200]{1,0:T(8,128)(2,1)S(1)} reduce(bf16[128,1,3200]{2,1,0:T(2,128)(2,1)S(1)} %all_to_all.46, bf16[]{:T(256)} %broadcast.8), dimensions={1}, to_apply=%all_to_all.46.reduce_sub_computation | reduce | bytes 1638402 | tf_op jit(solution)/shard_map/all_to_all | solution.py:233
  120.7 1.9 %reshape.61 = bf16[128,2,1600]{2,1,0:T(2,128)(2,1)} reshape(bf16[128,3200]{1,0:T(8,128)(2,1)S(1)} %reduce.5) | data formatting | bytes 1638400
  122.5 0.0 all-to-all-done.4
  122.5 13.8 %all-to-all-start.5 = ((bf16[128,2,1600]{2,1,0:T(2,128)(2,1)}), bf16[128,2,1600]{2,1,0:T(2,128)(2,1)S(1)}, u32[]{:S(2)}, u32[]{:S(2)}) async-start(bf16[128,2,1600]{2,1,0:T(2,128)(2,1)} %reshape.61), calls=%async_computation.5 | async-start | bytes 1703936 | tf_op jit(solution)/shard_map/all_to_all | solution.py:233
  136.4 0.1 reshape.60
  136.6 0.9 shard_map.159
  137.5 0.6 slice_bitcast_fusion.1
  138.0 24.8 %all-to-all-done.5 = bf16[128,2,1600]{2,1,0:T(2,128)(2,1)S(1)} async-done(((bf16[128,2,1600]{2,1,0:T(2,128)(2,1)}), bf16[128,2,1600]{2,1,0:T(2,128)(2,1)S(1)}, u32[]{:S(2)}, u32[]{:S(2)}) %all-to-all-start.5) | async-done | bytes 819232 | tf_op jit(solution)/shard_map/all_to_all | solution.py:233
  162.9 1.2 reshape.62
  164.1 5.8 %convert_reduce_fusion = f32[128,3200]{1,0:T(8,128)} fusion(bf16[128,1,3200]{2,1,0:T(2,128)(2,1)S(1)} %reshape.62), kind=kLoop, calls=%fused_computation.1 | loop fusion | flops 409600 | bytes 2457600 | tf_op jit(solution)/shard_map/convert_element_type | solution.py:250
  169.9 2.3 %reshape.53 = f32[64,2,10,320]{3,2,1,0:T(8,128)S(1)} reshape(f32[128,3200]{1,0:T(8,128)} %convert_reduce_fusion) | data formatting | bytes 3276800 | tf_op jit(solution)/shard_map/convert_element_type | solution.py:250
  172.2 0.2 reduce_sum.9
  172.4 0.1 slice_bitcast_fusion
  172.5 0.6 copy.40
  173.1 0.1 reshape.52
  173.2 0.6 copy.39
  (24 shorter events, 0.2 us)
Async XLA Ops:
  0.6 1.0 copy-start.4
  1.6 0.7 copy-start.6
  2.3 21.0 %copy-start.5 = (bf16[128,1280]{1,0:T(8,128)(2,1)S(1)}, bf16[128,1280]{1,0:T(8,128)(2,1)}, u32[]{:S(2)}) copy-start(bf16[128,1280]{1,0:T(8,128)(2,1)} %x_ref.3) | copy-start | bytes 983044
  2.3 21.0 %copy-start.7 = (s32[1,128]{1,0:T(1,128)S(1)}, s32[1,128]{1,0:T(1,128)}, u32[]{:S(2)}) copy-start(s32[1,128]{1,0:T(1,128)} %send_ref.5) | copy-start | bytes 1540
  4.7 42.1 %copy-start.12 = (f32[1280]{0:T(1024)S(1)}, f32[1280]{0:T(1024)}, u32[]{:S(2)}) copy-start(f32[1280]{0:T(1024)} %param.16) | copy-start | bytes 15364
  4.7 42.2 %copy-start.13 = (f32[1280]{0:T(1024)S(1)}, f32[1280]{0:T(1024)}, u32[]{:S(2)}) copy-start(f32[1280]{0:T(1024)} %param.17) | copy-start | bytes 15364
  4.7 34.1 %all-to-all-start = ((bf16[128,2,640]{2,1,0:T(2,128)(2,1)}), bf16[128,2,640]{2,1,0:T(2,128)(2,1)S(1)}, u32[]{:S(2)}, u32[]{:S(2)}) async-start(bf16[128,2,640]{2,1,0:T(2,128)(2,1)} %reshape.55), calls=%async_computation | async-start | bytes 655360 | tf_op jit(solution)/shard_map/all_to_all | solution.py:203
  38.8 23.4 %all-to-all-start.2 = ((bf16[128,2,640]{2,1,0:T(2,128)(2,1)}), bf16[128,2,640]{2,1,0:T(2,128)(2,1)}, u32[]{:S(2)}, u32[]{:S(2)}) async-start(bf16[128,2,640]{2,1,0:T(2,128)(2,1)} %reshape.57), calls=%async_computation.2 | async-start | bytes 655360 | tf_op jit(solution)/shard_map/all_to_all | solution.py:204
  47.2 23.1 %copy-start.10 = (bf16[128,1,1280]{2,1,0:T(2,128)(2,1)}, bf16[128,1,1280]{2,1,0:T(2,128)(2,1)S(1)}, u32[]{:S(2)}) copy-start(bf16[128,1,1280]{2,1,0:T(2,128)(2,1)S(1)} %reshape.56) | copy-start | bytes 983044
  47.2 18.4 %copy-start = (bf16[1280,2,3,80]{0,3,2,1:T(8,128)(2,1)S(1)}, bf16[1280,2,3,80]{0,3,2,1:T(8,128)(2,1)}, u32[]{:S(2)}) copy-start(bf16[1280,2,3,80]{0,3,2,1:T(8,128)(2,1)} %param.18) | copy-start | bytes 3686404
  47.2 18.3 %copy-start.1 = (bf16[2,80,1280]{2,1,0:T(8,128)(2,1)S(1)}, bf16[2,80,1280]{2,1,0:T(8,128)(2,1)}, u32[]{:S(2)}) copy-start(bf16[2,80,1280]{2,1,0:T(8,128)(2,1)} %param.19) | copy-start | bytes 1228804
  47.2 18.3 %copy-start.8 = (s32[1,128]{1,0:T(1,128)S(1)}, s32[1,128]{1,0:T(1,128)}, u32[]{:S(2)}) copy-start(s32[1,128]{1,0:T(1,128)} %recv_ref.1) | copy-start | bytes 1540
  47.2 18.3 %copy-start.9 = (s32[1,128]{1,0:T(1,128)S(1)}, s32[1,128]{1,0:T(1,128)}, u32[]{:S(2)}) copy-start(s32[1,128]{1,0:T(1,128)} %seg_ref.1) | copy-start | bytes 1540
  64.7 0.8 copy-start.11
  64.7 2.9 %copy-start.2 = (bf16[2,1280,128]{2,1,0:T(8,128)(2,1)S(1)}, bf16[2,1280,128]{2,1,0:T(8,128)(2,1)}, u32[]{:S(2)}) copy-start(bf16[2,1280,128]{2,1,0:T(8,128)(2,1)} %constant.31.clone.place_ref) | copy-start | bytes 1966084
  64.7 2.9 %copy-start.3 = (bf16[128,1280]{1,0:T(8,128)(2,1)S(1)}, bf16[128,1280]{1,0:T(8,128)(2,1)}, u32[]{:S(2)}) copy-start(bf16[128,1280]{1,0:T(8,128)(2,1)} %constant.30.clone.sel_ref) | copy-start | bytes 983044
  72.5 34.9 %collective-permute-start = (bf16[1280,320]{0,1:T(8,128)(2,1)}, bf16[1280,320]{0,1:T(8,128)(2,1)}, u32[]{:S(2)}, u32[]{:S(2)}) collective-permute-start(bf16[1280,320]{0,1:T(8,128)(2,1)} %copy.35), channel_id=1, source_target_pairs={{0,4},{4,0},{8,12},{12,8},{16,20},{20,16},{24,28},{28,24},{32,36},... | collective-permute-start | bytes 2457608 | tf_op jit(solution)/shard_map/ppermute | solution.py:231
  88.0 10.1 %all-to-all-start.3 = ((bf16[4,128,384]{2,1,0:T(8,128)(2,1)}), bf16[4,128,384]{2,1,0:T(8,128)(2,1)S(1)}, u32[]{:S(2)}, u32[]{:S(2)}) async-start(bf16[4,128,384]{2,1,0:T(8,128)(2,1)} %get-tuple-element.22), calls=%async_computation.3 | async-start | bytes 786432 | tf_op jit(solution)/shard_map/all_to_all | solution.py:224
  99.8 22.7 %all-to-all-start.4 = ((bf16[128,2,384]{2,1,0:T(2,128)(2,1)}), bf16[128,2,384]{2,1,0:T(2,128)(2,1)S(1)}, u32[]{:S(2)}, u32[]{:S(2)}) async-start(bf16[128,2,384]{2,1,0:T(2,128)(2,1)} %reshape.59), calls=%async_computation.4 | async-start | bytes 393216 | tf_op jit(solution)/shard_map/all_to_all | solution.py:244
  122.5 40.4 %all-to-all-start.5 = ((bf16[128,2,1600]{2,1,0:T(2,128)(2,1)}), bf16[128,2,1600]{2,1,0:T(2,128)(2,1)S(1)}, u32[]{:S(2)}, u32[]{:S(2)}) async-start(bf16[128,2,1600]{2,1,0:T(2,128)(2,1)} %reshape.61), calls=%async_computation.5 | async-start | bytes 1703936 | tf_op jit(solution)/shard_map/all_to_all | solution.py:233

commit v2 on v1

v2 whole, which is shorter than its diff:
```python
import jax
import jax.numpy as jnp
import numpy as np
from jax import lax
from jax.experimental import pallas as pl
from jax.experimental.pallas import tpu as pltpu
from jax.sharding import PartitionSpec as P

EPS = 1e-06
R = 128
D = 1280
HD = 80
HG = 2
NQ = HG * 3 * HD
NO = HG * HD
QW = D // 4
QP = 384
F32 = jnp.float32
BF = jnp.bfloat16
GAIN_AT = 64
BIAS_AT = 74
MEAN_AT = 84
WG = 1664

_cp = pltpu.CompilerParams(vmem_limit_bytes=24 * 1024 * 1024)


def dg(a, b, ca, cb):
    return lax.dot_general(a, b, (((ca,), (cb,)), ((), ())), preferred_element_type=F32)


def call(body, outs, *args, smem=(), cost=None):
    return pl.pallas_call(
        body,
        out_shape=tuple(jax.ShapeDtypeStruct(s, d) for s, d in outs),
        in_specs=[
            pl.BlockSpec(memory_space=pltpu.SMEM if i in smem else pltpu.VMEM)
            for i in range(len(args))
        ],
        out_specs=tuple(pl.BlockSpec(memory_space=pltpu.VMEM) for _ in outs),
        compiler_params=_cp,
        cost_estimate=cost,
    )(*args)


def lane(shape):
    return lax.broadcasted_iota(jnp.int32, shape, 1)


def sub(shape):
    return lax.broadcasted_iota(jnp.int32, shape, 0)


def gather_body(send_ref, x_ref, g_ref, o_ref):
    pick = (sub((R, R)) == send_ref[...]).astype(F32).astype(BF)
    o_ref[:, :D] = dg(pick, x_ref[...], 0, 0).astype(BF)
    o_ref[:, D:] = dg(pick, g_ref[...], 0, 0).astype(BF)


def norm_stats(x):
    mean = jnp.mean(x, axis=1, keepdims=True)
    centred = x - mean
    inv = lax.rsqrt(jnp.mean(centred * centred, axis=1, keepdims=True) + EPS)
    return mean, inv, centred * inv


def block_body(
    xg_ref, recv_ref, seg_ref, gain_ref, bias_ref, wq_ref, wo_ref, sel_ref, place_ref,
    pn_ref, normed_ref, qg_ref, ho_ref, stat_ref,
):
    x = xg_ref[:, :D].astype(F32)
    g = xg_ref[:, D:]
    mean, inv, xh = norm_stats(x)
    stat_ref[...] = jnp.where(lane((R, R)) < 64, mean, inv)
    normed = (xh * gain_ref[...] + bias_ref[...]).astype(BF)
    normed_ref[...] = normed
    qkv = dg(wq_ref[...], normed, 1, 1).astype(BF)
    dh = dg(wo_ref[...], g, 1, 1).astype(BF)
    place = sub((R, R)) == recv_ref[...]
    seg = jnp.sum(jnp.where(place, seg_ref[...], 0), axis=1, keepdims=True)
    group = (seg == lane((R, R))).astype(F32).astype(BF)
    same = dg(group, group, 1, 1) > 0.5
    outs, parts = [], []
    for h in range(HG):
        q = qkv[h * 3 * HD : h * 3 * HD + HD]
        k = qkv[h * 3 * HD + HD : h * 3 * HD + 2 * HD]
        v = qkv[h * 3 * HD + 2 * HD : (h + 1) * 3 * HD]
        dhh = dh[h * HD : (h + 1) * HD]
        s = jnp.where(same, dg(q, k, 0, 0) * (HD**-0.5), -1e30)
        e = jnp.exp(s - jnp.max(s, axis=1, keepdims=True))
        w = e / jnp.sum(e, axis=1, keepdims=True)
        w16 = w.astype(BF)
        outs.append(dg(v, w16, 1, 1).astype(BF))
        pg = dg(dhh, v, 0, 0)
        delta = jnp.sum(pg * w, axis=1, keepdims=True)
        sg = (w * (pg - delta) * (HD**-0.5)).astype(BF)
        parts.append(dg(k, sg, 1, 1).astype(BF))
        parts.append(dg(q, sg, 1, 0).astype(BF))
        parts.append(dg(dhh, w16, 1, 0).astype(BF))
    ho = jnp.concatenate(outs, axis=0)
    ho_ref[...] = ho
    qg = jnp.concatenate(parts, axis=0)
    qg_ref[...] = qg
    p = dg(ho, wo_ref[...], 0, 0)
    n = dg(qg, wq_ref[...], 0, 0)
    u = n * gain_ref[...]
    m1 = jnp.sum(u, axis=1, keepdims=True) * (1.0 / D)
    m2 = jnp.sum(u * xh, axis=1, keepdims=True) * (1.0 / D)
    gain_row = jnp.sum(n * xh, axis=0, keepdims=True)
    bias_row = jnp.sum(n, axis=0, keepdims=True)
    sel = sel_ref[...].astype(F32)
    extra = dg((sel * gain_row).astype(BF), place_ref[0], 1, 0)
    extra = extra + dg((sel * bias_row).astype(BF), place_ref[1], 1, 0)
    ln = lane((R, R))
    for j, m in enumerate((m1, m2)):
        hi = m.astype(BF).astype(F32)
        extra = jnp.where(ln == MEAN_AT + 2 * j, hi, extra)
        extra = jnp.where(ln == MEAN_AT + 2 * j + 1, m - hi, extra)
    pad = jnp.zeros((R, QP - QW), F32)
    for i in range(4):
        part = jnp.concatenate([p[:, i * QW : (i + 1) * QW], pad], axis=1)
        pn_ref[i, :, :QP] = part.astype(BF)
        part = jnp.concatenate([n[:, i * QW : (i + 1) * QW], extra[:, 64:]], axis=1)
        pn_ref[i, :, QP:] = part.astype(BF)


def wgrad_body(c_ref, normed_ref, xg_ref, qg_ref, ho_ref, keep_ref, send_ref):
    c = c_ref[0]
    for out, head in ((send_ref, 1 - c), (keep_ref, c)):
        a = qg_ref[pl.ds(pl.multiple_of(head * 3 * HD, 3 * HD), 3 * HD), :]
        b = ho_ref[pl.ds(pl.multiple_of(head * HD, HD), HD), :]
        out[: 3 * HD, :] = dg(a, normed_ref[...], 1, 0).astype(out.dtype)
        out[3 * HD :, :] = dg(b, xg_ref[:, D:], 1, 0).astype(out.dtype)


def pair_body(c_ref, keep_ref, got_ref, own_ref, sz_ref, sy_ref):
    z = c_ref[1]
    y = c_ref[2]

    def rows(j):
        at = pl.ds(pl.multiple_of(j * HD, HD), HD)
        return keep_ref[at, :] + got_ref[at, :].astype(F32)

    sz_ref[...] = rows(1 - z).astype(BF)
    sy_ref[...] = rows(3 - y).astype(BF)
    own_ref[:HD, :] = rows(z)
    own_ref[HD:, :] = rows(2 + y)


def post_body(
    pn_ref, x_ref, g_ref, stat_ref, gain_ref, own_ref, gz_ref, gy_ref, order_ref, o_ref
):
    pn = jnp.sum(pn_ref[...].astype(F32), axis=0)
    ps = pn[:, :QP]
    ns = pn[:, QP:]
    x = x_ref[...].astype(F32)
    mean = stat_ref[:, 0:1]
    inv = stat_ref[:, 64:65]
    xh = (x - mean) * inv
    tile = ns[:, 256:]
    ln = lane((R, R))
    m1 = jnp.sum(jnp.where((ln == MEAN_AT) | (ln == MEAN_AT + 1), tile, 0.0), axis=1, keepdims=True)
    m2 = jnp.sum(
        jnp.where((ln == MEAN_AT + 2) | (ln == MEAN_AT + 3), tile, 0.0), axis=1, keepdims=True
    )
    enc = x + ps
    grad = g_ref[...].astype(F32) + inv * (ns * gain_ref[...] - m1 - xh * m2)
    got = jnp.concatenate([gz_ref[...], gy_ref[...]], axis=0).astype(F32)
    wg = (own_ref[...] + got).astype(BF)
    wg = dg(order_ref[...], wg, 1, 1)
    slabs = [wg[i * R : (i + 1) * R] for i in range(10)]
    o_ref[...] = jnp.concatenate(
        slabs + [tile[:, 64:], enc[:, :QW], grad[:, :QW]], axis=1
    ).astype(BF)


def final_body(send_ref, b_ref, e_ref, i_ref, a_ref, w_ref, gain_ref, bias_ref):
    pick = (sub((R, R)) == send_ref[...]).astype(F32).astype(BF)
    rows = dg(b_ref[:, WG:], pick, 0, 1).astype(BF)
    e_ref[...] = rows[:QW]
    i_ref[...] = rows[QW:]
    row = sub((16, R))
    src = lane((16, R))
    half = (row // 2) % 2
    c_ok = src % 2 == row % 2
    z_ok = (src // 2) % 2 == half
    y_ok = (src // 16) % 2 == half
    mask = ((row < 4) & c_ok & z_ok) | ((row >= 4) & (row < 8) & c_ok & y_ok) | (row == 8)
    sums = dg(mask.astype(F32).astype(BF), b_ref[:, :WG], 1, 0)
    for i in range(10):
        at = i * 2 * HD
        a_ref[i, 0] = sums[0:2, at : at + HD]
        a_ref[i, 1] = sums[2:4, at : at + HD]
        a_ref[i, 2] = sums[4:6, at + HD : at + 2 * HD]
        w_ref[i] = sums[6:8, at + HD : at + 2 * HD]
    gain_ref[...] = sums[8:9, WG - 64 : WG - 54]
    bias_ref[...] = sums[8:9, WG - 54 : WG - 44]


_f = np.arange(D)
SEL = (_f[None, :] // 10 == np.arange(R)[:, None]).astype(np.float32)
PLACE = np.stack(
    [(_f[:, None] % 10 + at == np.arange(R)[None, :]).astype(np.float32) for at in (GAIN_AT, BIAS_AT)]
)


ORDER = np.zeros((D, D), np.float32)
ORDER[np.arange(D), (np.arange(D) % R) * 10 + np.arange(D) // R] = 1.0


def local(patches, cotangent, send_order, recv_order, segment_ids, ln_gain, ln_bias, w_qkv, w_out):
    zero = lax.axis_index("zero")
    dp = lax.axis_index("dp")
    bits = jnp.stack([dp & 1, (dp >> 1) & 1, (dp >> 4) & 1])
    wq = w_qkv.transpose(1, 2, 3, 0).reshape(NQ, D)
    wo = w_out.reshape(NO, D)
    gain = ln_gain.reshape(1, D)
    bias = ln_bias.reshape(1, D)
    sel = jnp.asarray(SEL, BF)
    place = jnp.asarray(PLACE, BF)
    order = jnp.asarray(ORDER, BF)

    def swap(a, bit):
        return lax.ppermute(a, "dp", [(i, i ^ bit) for i in range(128)])

    (xg,) = call(gather_body, [((R, 2 * D), BF)], send_order, patches, cotangent)
    xg = lax.all_to_all(xg, "dp", 0, 0, tiled=True)
    pn, normed, qg, ho, stat = call(
        block_body,
        [((4, R, 2 * QP), BF), ((R, D), BF), ((NQ, R), BF), ((NO, R), BF), ((R, R), F32)],
        xg, recv_order, segment_ids, gain, bias, wq, wo, sel, place,
    )
    pn = lax.all_to_all(pn, "zero", 0, 0, tiled=True)
    keep, send = call(
        wgrad_body,
        [((4 * HD, D), F32), ((4 * HD, D), BF)],
        bits, normed, xg, qg, ho,
        smem=(0,),
    )
    own, sz, sy = call(
        pair_body,
        [((2 * HD, D), F32), ((HD, D), BF), ((HD, D), BF)],
        bits, keep, swap(send, 1),
        smem=(0,),
    )
    gz = swap(sz, 2)
    gy = swap(sy, 16)

    def quarter(a, at=0):
        a = lax.dynamic_slice_in_dim(a, at + zero * QW, QW, 1)
        return jnp.pad(a, ((0, 0), (0, QP - QW)))

    (back,) = call(
        post_body,
        [((R, WG + 2 * QW), BF)],
        pn, quarter(xg), quarter(xg, D), stat, quarter(gain), own, gz, gy, order,
    )
    back = lax.all_to_all(back, "dp", 0, 0, tiled=True)
    enc, grad, qkv_share, out_share, gain_grad, bias_grad = call(
        final_body,
        [
            ((QW, R), BF),
            ((QW, R), BF),
            ((10, 3, 2, HD), F32),
            ((10, 2, HD), F32),
            ((1, 10), F32),
            ((1, 10), F32),
        ],
        send_order, back,
    )
    return (
        enc.T,
        grad.T,
        qkv_share.transpose(0, 2, 1, 3),
        out_share.transpose(1, 2, 0),
        gain_grad.reshape(10),
        bias_grad.reshape(10),
    )


def solution(mesh):
    return jax.shard_map(
        local,
        mesh=mesh,
        in_specs=(
            P("dp", None),
            P("dp", None),
            P("dp", None),
            P("dp", None),
            P("dp", None),
            P(),
            P(),
            P(None, "zero", None, None),
            P("zero", None, None),
        ),
        out_specs=(
            P("dp", "zero"),
            P("dp", "zero"),
            P("dp", "zero", None, None),
            P("zero", None, "dp"),
            P("dp"),
            P("dp"),
        ),
        check_vma=False,
    )
```

time: 175 us -> 118 us (0.67)
  waiting for transfers between devices: 58.1 us -> 27.9 us
  starting transfers between devices: 55.3 us -> 31.2 us
  blocking collectives: 11.7 us -> 27.6 us
  other arithmetic: 15.2 us -> 3.27 us
  local copies, waits for them, and re-layouts: 25.3 us -> 15.9 us
  Pallas kernels: 7.26 us -> 10.2 us
    all_to_all x5 -> x2, waiting for transfers between devices: 58.1 us -> 23 us  [the longest x1 22.2 us: local(): xg = lax.all_to_all(xg, 'dp', 0, 0, tiled=True)]
    all_to_all x5 -> x2, starting transfers between devices: 51.5 us -> 22.6 us  [the longest x1 18.4 us: local(): xg = lax.all_to_all(xg, 'dp', 0, 0, tiled=True)]
    all_to_all x1, blocking collectives: 11.7 us -> 27.6 us  [local(): back = lax.all_to_all(back, 'dp', 0, 0, tiled=True)]
    convert_element_type x2 -> x0, other arithmetic: 6.96 us -> none  [the longest x1 5.81 us: local(): wsum = jnp.sum(wg.reshape(64, 2, 10, 4 * HD).astype(F32), axis=0)]
    all_to_all x3 -> x1, other arithmetic: 7.3 us -> 1.1 us  [local(): xg = lax.all_to_all(xg, 'dp', 0, 0, tiled=True)]
    ppermute x1 -> x3, waiting for transfers between devices: 0.01 us -> 4.96 us  [swap(): return lax.ppermute(a, 'dp', [(i, i ^ bit) for i in range(128)])]
    all_to_all x2 -> x1, local copies, waits for them, and re-layouts: 5.38 us -> 0.51 us  [local(): xg = lax.all_to_all(xg, 'dp', 0, 0, tiled=True)]
    ppermute x1 -> x3, starting transfers between devices: 3.73 us -> 8.52 us  [swap(): return lax.ppermute(a, 'dp', [(i, i ^ bit) for i in range(128)])]
  transfers between devices with their start and end apart: 6 -> 5, of which waited for: 4 -> 4; matrix products, arithmetic and copies ran while one was open for 9% -> 1% of each run, Pallas kernels for 1% -> 1%
where the time goes in v2:
time: 118 us; the launch traced here: 117 us
  starting transfers between devices  31.2 us (26%)
  waiting for transfers between devices  27.9 us (24%)
  blocking collectives  27.6 us (23%)
  local copies, waits for them, and re-layouts  15.9 us (13%)
  Pallas kernels  10.2 us (9%)
  other arithmetic  3.27 us (3%)
    all_to_all x1, blocking collectives, local(): back = lax.all_to_all(back, 'dp', 0, 0, tiled=True)  27.6 us
    all_to_all x1, waiting for transfers between devices, local(): xg = lax.all_to_all(xg, 'dp', 0, 0, tiled=True)  22.2 us
    all_to_all x1, starting transfers between devices, local(): xg = lax.all_to_all(xg, 'dp', 0, 0, tiled=True)  18.4 us
    unnamed x46, local copies, waits for them, and re-layouts  14.5 us
    pallas_call x6, Pallas kernels, call(): pl.pallas_call(body, out_shape=tuple((jax.ShapeDtypeStruct(s, d) for s, d...  10.2 us
    ppermute x3, starting transfers between devices, swap(): return lax.ppermute(a, 'dp', [(i, i ^ bit) for i in range(128)])  8.52 us
    ppermute x3, waiting for transfers between devices, swap(): return lax.ppermute(a, 'dp', [(i, i ^ bit) for i in range(128)])  4.96 us
    all_to_all x1, starting transfers between devices, local(): pn = lax.all_to_all(pn, 'zero', 0, 0, tiled=True)  4.22 us
  transfers between devices with their start and end apart: 5, of which 4 were waited for; matrix products, arithmetic and copies ran while one was open for 1% of the time, Pallas kernels for 1%

profile of v2, /device:TPU:1, one launch (start us, length us, event | category | flops | bytes accessed | tf_op | source)
XLA Modules:
  0.0 117.0 jit_solution(3704749088433627443)
XLA Ops:
  0.6 0.0 copy-start.11
  0.6 1.0 copy-done.11
  1.6 0.0 copy-start.12
  1.6 1.0 copy-done.12
  2.6 0.0 copy-start.14
  2.6 0.7 copy-done.14
  3.2 0.4 shard_map.163
  3.6 0.5 broadcast.6
  4.1 1.1 reduce
  5.2 0.0 copy-start.19
  5.2 0.0 copy-start.18
  5.2 1.0 reshape.43
  6.2 18.4 %all-to-all-start = ((bf16[128,2,1280]{2,1,0:T(2,128)(2,1)}), bf16[128,2,1280]{2,1,0:T(2,128)(2,1)S(1)}, u32[]{:S(2)}, u32[]{:S(2)}) async-start(bf16[128,2,1280]{2,1,0:T(2,128)(2,1)} %reshape.43), calls=%async_computation | async-start | bytes 1310720 | tf_op jit(solution)/shard_map/all_to_all | solution.py:227
  24.7 0.0 copy-done.19
  24.7 0.0 copy-done.18
  24.7 0.1 pad_add_fusion.c_ref
  24.8 22.2 %all-to-all-done = bf16[128,2,1280]{2,1,0:T(2,128)(2,1)S(1)} async-done(((bf16[128,2,1280]{2,1,0:T(2,128)(2,1)}), bf16[128,2,1280]{2,1,0:T(2,128)(2,1)S(1)}, u32[]{:S(2)}, u32[]{:S(2)}) %all-to-all-start) | async-done | bytes 655392 | tf_op jit(solution)/shard_map/all_to_all | solution.py:227
  47.0 0.0 copy-start.10
  47.0 0.0 copy-start.13
  47.0 0.5 reshape.44
  47.5 0.0 copy-start.4
  47.5 0.0 copy-start.9
  47.6 0.0 copy-start.16
  47.6 0.0 copy-start.17
  47.6 0.1 copy.36
  47.7 0.3 copy-done.10
  48.0 0.1 copy-done.13
  48.1 0.8 copy-done.4
  48.9 0.2 copy-done.9
  49.1 0.0 copy-done.16
  49.1 0.0 copy-done.17
  49.1 4.0 %shard_map.164 = (bf16[4,128,768]{2,1,0:T(8,128)(2,1)}, bf16[128,1280]{1,0:T(8,128)(2,1)S(1)}, bf16[480,128]{1,0:T(8,128)(2,1)S(1)}, bf16[160,128]{1,0:T(8,128)(2,1)S(1)}, f32[128,128]{1,0:T(8,128)S(1)}) custom-call(bf16[128,2560]{1,0:T(8,128)(2,1)S(1)} %bitcast.27, s32[1,128]{1,0:T(1,128)S(1)} %copy-done.16, s32[1,128]{1,0:T(1,128)S(1)} %copy-done.17, ...), custom_call_target="tpu_custom_call" | custom-call | tf_op jit(solution)/shard_map/pallas_call | solution.py:33
  53.1 1.1 shard_map.165
  54.2 0.0 copy-start.2
  54.2 1.2 %copy-done.2 = f32[320,1280]{1,0:T(8,128)} copy-done((f32[320,1280]{1,0:T(8,128)}, f32[320,1280]{1,0:T(8,128)S(1)}, u32[]{:S(2)}) %copy-start.2) | copy-done | bytes 1638424
  55.4 3.8 %collective-permute-start = (bf16[320,1280]{1,0:T(8,128)(2,1)S(1)}, bf16[320,1280]{1,0:T(8,128)(2,1)S(1)}, u32[]{:S(2)}, u32[]{:S(2)}) collective-permute-start(bf16[320,1280]{1,0:T(8,128)(2,1)S(1)} %get-tuple-element.28), channel_id=1, source_target_pairs={{0,4},{4,0},{8,12},{12,8},{16,20},{20,16},{24,28},{28,24},{32,36},... | collective-permute-start | bytes 2457608 | tf_op jit(solution)/shard_map/ppermute | solution.py:224
  59.2 4.2 %all-to-all-start.1 = ((bf16[4,128,768]{2,1,0:T(8,128)(2,1)}), bf16[4,128,768]{2,1,0:T(8,128)(2,1)}, u32[]{:S(2)}, u32[]{:S(2)}) async-start(bf16[4,128,768]{2,1,0:T(8,128)(2,1)} %get-tuple-element.22), calls=%async_computation.1 | async-start | bytes 1572864 | tf_op jit(solution)/shard_map/all_to_all | solution.py:233
  63.4 0.1 dynamic-slice.5
  63.5 0.8 constant_dynamic-slice_fusion
  64.3 0.0 collective-permute-done.got_ref
  64.3 0.0 copy-start.5
  64.3 0.9 copy-done.5
  65.2 1.4 %copy-done.3 = f32[320,1280]{1,0:T(8,128)S(1)} copy-done((f32[320,1280]{1,0:T(8,128)S(1)}, f32[320,1280]{1,0:T(8,128)}, u32[]{:S(2)}) %copy-start.3) | copy-done | bytes 1638424
  66.6 1.1 copy-done.6
  67.8 1.4 %shard_map.166 = (f32[160,1280]{1,0:T(8,128)S(1)}, bf16[80,1280]{1,0:T(8,128)(2,1)}, bf16[80,1280]{1,0:T(8,128)(2,1)}) custom-call(s32[3]{0:T(128)S(1)} %pad_add_fusion.c_ref, f32[320,1280]{1,0:T(8,128)S(1)} %copy-done.3, bf16[320,1280]{1,0:T(8,128)(2,1)S(1)} %copy-done.6), custom_call_target="tpu_custom_call" | custom-call | tf_op jit(solution)/shard_map/pallas_call | solution.py:33
  69.2 0.9 copy-done.7
  70.1 2.0 %collective-permute-start.1 = (bf16[80,1280]{1,0:T(8,128)(2,1)}, bf16[80,1280]{1,0:T(8,128)(2,1)}, u32[]{:S(2)}, u32[]{:S(2)}) collective-permute-start(bf16[80,1280]{1,0:T(8,128)(2,1)} %get-tuple-element.30), channel_id=1, source_target_pairs={{0,8},{4,12},{8,0},{12,4},{16,24},{20,28},{24,16},{28,20},{32,40},... | collective-permute-start | bytes 614408 | tf_op jit(solution)/shard_map/ppermute | solution.py:224
  72.2 2.7 %collective-permute-start.2 = (bf16[80,1280]{1,0:T(8,128)(2,1)}, bf16[80,1280]{1,0:T(8,128)(2,1)}, u32[]{:S(2)}, u32[]{:S(2)}) collective-permute-start(bf16[80,1280]{1,0:T(8,128)(2,1)} %get-tuple-element.31), channel_id=1, source_target_pairs={{0,64},{4,68},{8,72},{12,76},{16,80},{20,84},{24,88},{28,92},{32,9... | collective-permute-start | bytes 614408 | tf_op jit(solution)/shard_map/ppermute | solution.py:224
  75.0 0.8 all-to-all-done.1.pn_ref
  75.7 3.2 %collective-permute-done.1.gz_ref = bf16[80,1280]{1,0:T(8,128)(2,1)} collective-permute-done((bf16[80,1280]{1,0:T(8,128)(2,1)}, bf16[80,1280]{1,0:T(8,128)(2,1)}, u32[]{:S(2)}, u32[]{:S(2)}) %collective-permute-start.1) | collective-permute-done | bytes 204832 | tf_op jit(solution)/shard_map/ppermute | solution.py:224
  79.0 1.7 %collective-permute-done.2.gy_ref = bf16[80,1280]{1,0:T(8,128)(2,1)} collective-permute-done((bf16[80,1280]{1,0:T(8,128)(2,1)}, bf16[80,1280]{1,0:T(8,128)(2,1)}, u32[]{:S(2)}, u32[]{:S(2)}) %collective-permute-start.2) | collective-permute-done | bytes 204832 | tf_op jit(solution)/shard_map/ppermute | solution.py:224
  80.7 0.0 copy-done
  80.7 1.1 copy-done.8
  81.9 2.4 %shard_map.167 = bf16[128,2304]{1,0:T(8,128)(2,1)S(1)} custom-call(bf16[4,128,768]{2,1,0:T(8,128)(2,1)} %all-to-all-done.1.pn_ref, bf16[128,384]{1,0:T(8,128)(2,1)S(1)} %pad.11.x_ref, bf16[128,384]{1,0:T(8,128)(2,1)S(1)} %pad.12.g_ref, f32[128,128]{1,0:T(8,128)S(1)} %get-tuple-element.23.stat_ref, f32[1,384]{1,0:T(1,128)S(1)} %pad.13.gain_ref, ...), custom_call_target="tpu_custom_call" | custom-call | tf_op jit(solution)/shard_map/pallas_call | solution.py:33
  84.2 0.0 copy-start.1
  84.3 0.8 copy-done.1
  85.1 2.1 %reduce.1 = bf16[128,2304]{1,0:T(8,128)(2,1)S(1)} reduce(bf16[128,1,2304]{2,0,1:T(8,128)(2,1)} %bitcast.31, bf16[]{:T(256)} %broadcast.6), dimensions={1}, to_apply=%copy.25.reduce_sub_computation | reduce | bytes 1179650 | tf_op jit(solution)/shard_map/all_to_all | solution.py:258
  87.2 0.1 reshape.45
  87.3 27.6 %all_to_all.27 = bf16[128,2,1152]{2,1,0:T(2,128)(2,1)S(1)} all-to-all(bf16[128,2,1152]{2,1,0:T(2,128)(2,1)S(1)} %reshape.45), channel_id=1, replica_groups=mesh['dp'=128,'zero'=4] {'dp'}, dimensions={0} | all-to-all | bytes 1179648 | tf_op jit(solution)/shard_map/all_to_all | solution.py:258
  114.9 0.5 reshape.46
  115.4 0.0 copy-start.15
  115.4 0.1 copy.37
  115.5 0.6 copy-done.15
  116.1 0.9 shard_map.168
  (12 shorter events, 0.1 us)
Async XLA Ops:
  0.6 1.0 copy-start.11
  1.6 1.0 copy-start.12
  2.6 0.7 copy-start.14
  5.2 19.5 %copy-start.19 = (f32[1280]{0:T(1024)S(1)}, f32[1280]{0:T(1024)}, u32[]{:S(2)}) copy-start(f32[1280]{0:T(1024)} %param.18) | copy-start | bytes 15364
  5.2 19.5 %copy-start.18 = (f32[1280]{0:T(1024)S(1)}, f32[1280]{0:T(1024)}, u32[]{:S(2)}) copy-start(f32[1280]{0:T(1024)} %param.17) | copy-start | bytes 15364
  6.2 40.8 %all-to-all-start = ((bf16[128,2,1280]{2,1,0:T(2,128)(2,1)}), bf16[128,2,1280]{2,1,0:T(2,128)(2,1)S(1)}, u32[]{:S(2)}, u32[]{:S(2)}) async-start(bf16[128,2,1280]{2,1,0:T(2,128)(2,1)} %reshape.43), calls=%async_computation | async-start | bytes 1310720 | tf_op jit(solution)/shard_map/all_to_all | solution.py:227
  47.0 1.0 copy-start.10
  47.0 1.1 copy-start.13
  47.5 1.3 %copy-start.4 = (bf16[1280,2,3,80]{0,3,2,1:T(8,128)(2,1)S(1)}, bf16[1280,2,3,80]{0,3,2,1:T(8,128)(2,1)}, u32[]{:S(2)}) copy-start(bf16[1280,2,3,80]{0,3,2,1:T(8,128)(2,1)} %param.19) | copy-start | bytes 3686404
  47.5 1.5 %copy-start.9 = (bf16[2,1280,128]{2,1,0:T(8,128)(2,1)S(1)}, bf16[2,1280,128]{2,1,0:T(8,128)(2,1)}, u32[]{:S(2)}) copy-start(bf16[2,1280,128]{2,1,0:T(8,128)(2,1)} %constant.36.clone.place_ref) | copy-start | bytes 1966084
  47.6 1.5 %copy-start.16 = (s32[1,128]{1,0:T(1,128)S(1)}, s32[1,128]{1,0:T(1,128)}, u32[]{:S(2)}) copy-start(s32[1,128]{1,0:T(1,128)} %recv_ref.1) | copy-start | bytes 1540
  47.6 1.5 %copy-start.17 = (s32[1,128]{1,0:T(1,128)S(1)}, s32[1,128]{1,0:T(1,128)}, u32[]{:S(2)}) copy-start(s32[1,128]{1,0:T(1,128)} %seg_ref.1) | copy-start | bytes 1540
  54.2 1.2 %copy-start.2 = (f32[320,1280]{1,0:T(8,128)}, f32[320,1280]{1,0:T(8,128)S(1)}, u32[]{:S(2)}) copy-start(f32[320,1280]{1,0:T(8,128)S(1)} %get-tuple-element.27.keep_ref) | copy-start | bytes 4915204
  55.4 8.9 %collective-permute-start = (bf16[320,1280]{1,0:T(8,128)(2,1)S(1)}, bf16[320,1280]{1,0:T(8,128)(2,1)S(1)}, u32[]{:S(2)}, u32[]{:S(2)}) collective-permute-start(bf16[320,1280]{1,0:T(8,128)(2,1)S(1)} %get-tuple-element.28), channel_id=1, source_target_pairs={{0,4},{4,0},{8,12},{12,8},{16,20},{20,16},{24,28},{28,24},{32,36},... | collective-permute-start | bytes 2457608 | tf_op jit(solution)/shard_map/ppermute | solution.py:224
  59.2 16.6 %all-to-all-start.1 = ((bf16[4,128,768]{2,1,0:T(8,128)(2,1)}), bf16[4,128,768]{2,1,0:T(8,128)(2,1)}, u32[]{:S(2)}, u32[]{:S(2)}) async-start(bf16[4,128,768]{2,1,0:T(8,128)(2,1)} %get-tuple-element.22), calls=%async_computation.1 | async-start | bytes 1572864 | tf_op jit(solution)/shard_map/all_to_all | solution.py:233
  64.3 0.9 copy-start.5
  65.2 1.4 %copy-start.3 = (f32[320,1280]{1,0:T(8,128)S(1)}, f32[320,1280]{1,0:T(8,128)}, u32[]{:S(2)}) copy-start(f32[320,1280]{1,0:T(8,128)} %copy-done.2) | copy-start | bytes 4915204
  66.6 1.1 copy-start.6
  67.8 12.9 %copy-start = (bf16[1280,1280]{1,0:T(8,128)(2,1)S(1)}, bf16[1280,1280]{1,0:T(8,128)(2,1)}, u32[]{:S(2)}) copy-start(bf16[1280,1280]{1,0:T(8,128)(2,1)} %constant.37.clone.order_ref) | copy-start | bytes 9830404
  69.2 0.9 copy-start.7
  70.1 8.8 %collective-permute-start.1 = (bf16[80,1280]{1,0:T(8,128)(2,1)}, bf16[80,1280]{1,0:T(8,128)(2,1)}, u32[]{:S(2)}, u32[]{:S(2)}) collective-permute-start(bf16[80,1280]{1,0:T(8,128)(2,1)} %get-tuple-element.30), channel_id=1, source_target_pairs={{0,8},{4,12},{8,0},{12,4},{16,24},{20,28},{24,16},{28,20},{32,40},... | collective-permute-start | bytes 614408 | tf_op jit(solution)/shard_map/ppermute | solution.py:224
  72.2 8.5 %collective-permute-start.2 = (bf16[80,1280]{1,0:T(8,128)(2,1)}, bf16[80,1280]{1,0:T(8,128)(2,1)}, u32[]{:S(2)}, u32[]{:S(2)}) collective-permute-start(bf16[80,1280]{1,0:T(8,128)(2,1)} %get-tuple-element.31), channel_id=1, source_target_pairs={{0,64},{4,68},{8,72},{12,76},{16,80},{20,84},{24,88},{28,92},{32,9... | collective-permute-start | bytes 614408 | tf_op jit(solution)/shard_map/ppermute | solution.py:224
  80.7 1.1 copy-start.8
  84.2 0.8 copy-start.1
  115.4 0.7 copy-start.15

commit v3 on v2

--- a/solution.py
+++ b/solution.py
@@ -21,26 +21,37 @@
 BIAS_AT = 74
 MEAN_AT = 84
 WG = 1664
-
-_cp = pltpu.CompilerParams(vmem_limit_bytes=24 * 1024 * 1024)
+HALF = (WG + 2 * QW) // 2
+
+_cp = pltpu.CompilerParams(vmem_limit_bytes=16 * 1024 * 1024)
 
 
 def dg(a, b, ca, cb):
     return lax.dot_general(a, b, (((ca,), (cb,)), ((), ())), preferred_element_type=F32)
 
 
-def call(body, outs, *args, smem=(), cost=None):
+def call(body, outs, *args, smem=(), hbm=()):
+    def space(i):
+        return pltpu.SMEM if i in smem else pltpu.HBM if i in hbm else pltpu.VMEM
+
+    scratch = [pltpu.VMEM(args[i].shape, args[i].dtype) for i in hbm]
+    if hbm:
+        scratch.append(pltpu.SemaphoreType.DMA((len(hbm),)))
     return pl.pallas_call(
         body,
         out_shape=tuple(jax.ShapeDtypeStruct(s, d) for s, d in outs),
-        in_specs=[
-            pl.BlockSpec(memory_space=pltpu.SMEM if i in smem else pltpu.VMEM)
-            for i in range(len(args))
-        ],
+        in_specs=[pl.BlockSpec(memory_space=space(i)) for i in range(len(args))],
         out_specs=tuple(pl.BlockSpec(memory_space=pltpu.VMEM) for _ in outs),
+        scratch_shapes=scratch,
         compiler_params=_cp,
-        cost_estimate=cost,
     )(*args)
+
+
+def fetch(sems, *pairs):
+    copies = [pltpu.make_async_copy(a, b, sems.at[i]) for i, (a, b) in enumerate(pairs)]
+    for copy in copies:
+        copy.start()
+    return copies
 
 
 def lane(shape):
@@ -51,10 +62,27 @@
     return lax.broadcasted_iota(jnp.int32, shape, 0)
 
 
-def gather_body(send_ref, x_ref, g_ref, o_ref):
-    pick = (sub((R, R)) == send_ref[...]).astype(F32).astype(BF)
-    o_ref[:, :D] = dg(pick, x_ref[...], 0, 0).astype(BF)
-    o_ref[:, D:] = dg(pick, g_ref[...], 0, 0).astype(BF)
+def one_hot(cond):
+    return cond.astype(F32).astype(BF)
+
+
+def pair_picks(send_ref):
+    spread = one_hot(lane((R, 2 * R)) // 2 == sub((R, 2 * R)))
+    rows = jnp.broadcast_to(send_ref[...], (8, R)).astype(F32).astype(BF)
+    target = dg(rows, spread, 1, 0)[0:1].astype(jnp.int32)
+    hit = sub((R, 2 * R)) == target
+    odd = lane((R, 2 * R)) % 2
+    return one_hot(hit & (odd == 0)), one_hot(hit & (odd == 1))
+
+
+def gather_body(send_ref, x_ref, g_ref, o_ref, x_buf, g_buf, sems):
+    copies = fetch(sems, (x_ref, x_buf), (g_ref, g_buf))
+    even, odd = pair_picks(send_ref)
+    copies[0].wait()
+    rows = dg(even, x_buf[...], 0, 0)
+    copies[1].wait()
+    rows = rows + dg(odd, g_buf[...], 0, 0)
+    o_ref[...] = rows.astype(BF).reshape(R, 2, D)
 
 
 def norm_stats(x):
@@ -65,15 +93,35 @@
 
 
 def block_body(
-    xg_ref, recv_ref, seg_ref, gain_ref, bias_ref, wq_ref, wo_ref, sel_ref, place_ref,
-    pn_ref, normed_ref, qg_ref, ho_ref, stat_ref,
+    bits_ref, xg_ref, recv_ref, seg_ref, gain_ref, bias_ref, wq_ref, wo_ref, sel_ref, place_ref,
+    pn_ref, send_ref, normed_ref, g_out_ref, qg_ref, ho_ref, stat_ref, xq_ref, gq_ref, gainq_ref,
+    wq_buf, wo_buf, sel_buf, place_buf, sems,
 ):
-    x = xg_ref[:, :D].astype(F32)
-    g = xg_ref[:, D:]
+    copies = fetch(
+        sems, (wq_ref, wq_buf), (wo_ref, wo_buf), (sel_ref, sel_buf), (place_ref, place_buf)
+    )
+    xg = xg_ref[...].reshape(2 * R, D)
+    at = lane((R, 2 * R)) - 2 * sub((R, 2 * R))
+    x = dg(one_hot(at == 0), xg, 1, 0)
+    g32 = dg(one_hot(at == 1), xg, 1, 0)
+    g = g32.astype(BF)
+    g_out_ref[...] = g
     mean, inv, xh = norm_stats(x)
     stat_ref[...] = jnp.where(lane((R, R)) < 64, mean, inv)
     normed = (xh * gain_ref[...] + bias_ref[...]).astype(BF)
     normed_ref[...] = normed
+    for i in range(4):
+
+        @pl.when(bits_ref[3] == i)
+        def _(i=i):
+            cols = slice(i * QW, (i + 1) * QW)
+            xq_ref[...] = x[:, cols]
+            gq_ref[...] = g32[:, cols]
+            gainq_ref[...] = gain_ref[:, cols]
+
+    copies[0].wait()
+    copies[1].wait()
+    wq_ref, wo_ref, sel_ref, place_ref = wq_buf, wo_buf, sel_buf, place_buf
     qkv = dg(wq_ref[...], normed, 1, 1).astype(BF)
     dh = dg(wo_ref[...], g, 1, 1).astype(BF)
     place = sub((R, R)) == recv_ref[...]
@@ -101,6 +149,11 @@
     ho_ref[...] = ho
     qg = jnp.concatenate(parts, axis=0)
     qg_ref[...] = qg
+    other = 1 - bits_ref[0]
+    a = qg_ref[pl.ds(pl.multiple_of(other * 3 * HD, 3 * HD), 3 * HD), :]
+    b = ho_ref[pl.ds(pl.multiple_of(other * HD, HD), HD), :]
+    send_ref[: 3 * HD, :] = dg(a, normed, 1, 0).astype(BF)
+    send_ref[3 * HD :, :] = dg(b, g, 1, 0).astype(BF)
     p = dg(ho, wo_ref[...], 0, 0)
     n = dg(qg, wq_ref[...], 0, 0)
     u = n * gain_ref[...]
@@ -108,6 +161,8 @@
     m2 = jnp.sum(u * xh, axis=1, keepdims=True) * (1.0 / D)
     gain_row = jnp.sum(n * xh, axis=0, keepdims=True)
     bias_row = jnp.sum(n, axis=0, keepdims=True)
+    copies[2].wait()
+    copies[3].wait()
     sel = sel_ref[...].astype(F32)
     extra = dg((sel * gain_row).astype(BF), place_ref[0], 1, 0)
     extra = extra + dg((sel * bias_row).astype(BF), place_ref[1], 1, 0)
@@ -124,69 +179,96 @@
         pn_ref[i, :, QP:] = part.astype(BF)
 
 
-def wgrad_body(c_ref, normed_ref, xg_ref, qg_ref, ho_ref, keep_ref, send_ref):
-    c = c_ref[0]
-    for out, head in ((send_ref, 1 - c), (keep_ref, c)):
-        a = qg_ref[pl.ds(pl.multiple_of(head * 3 * HD, 3 * HD), 3 * HD), :]
-        b = ho_ref[pl.ds(pl.multiple_of(head * HD, HD), HD), :]
-        out[: 3 * HD, :] = dg(a, normed_ref[...], 1, 0).astype(out.dtype)
-        out[3 * HD :, :] = dg(b, xg_ref[:, D:], 1, 0).astype(out.dtype)
-
-
-def pair_body(c_ref, keep_ref, got_ref, own_ref, sz_ref, sy_ref):
-    z = c_ref[1]
-    y = c_ref[2]
-
-    def rows(j):
-        at = pl.ds(pl.multiple_of(j * HD, HD), HD)
-        return keep_ref[at, :] + got_ref[at, :].astype(F32)
-
-    sz_ref[...] = rows(1 - z).astype(BF)
-    sy_ref[...] = rows(3 - y).astype(BF)
-    own_ref[:HD, :] = rows(z)
-    own_ref[HD:, :] = rows(2 + y)
+def own_rows(c, part, normed, g, qg_ref, ho_ref):
+    first, choose_out = part
+    a = qg_ref[pl.ds(pl.multiple_of((c * 3 + first) * HD, HD), HD), :]
+    if choose_out is None:
+        return dg(a, normed, 1, 0)
+    b = ho_ref[pl.ds(pl.multiple_of(c * HD, HD), HD), :]
+    pick = choose_out.astype(F32)
+    left = jnp.concatenate([a.astype(F32) * (1.0 - pick), b.astype(F32) * pick], axis=1).astype(BF)
+    return dg(left, jnp.concatenate([normed, g], axis=0), 1, 0)
+
+
+def part_rows(ref, j):
+    return ref[pl.ds(pl.multiple_of(j * HD, HD), HD), :].astype(F32)
+
+
+def pair_body(bits_ref, normed_ref, g_ref, qg_ref, ho_ref, got_ref, sz_ref, sy_ref, got, sems):
+    copies = fetch(sems, (got_ref, got))
+    c, z, y = bits_ref[0], bits_ref[1], bits_ref[2]
+    normed, g = normed_ref[...], g_ref[...]
+    a = own_rows(c, (1 - z, None), normed, g, qg_ref, ho_ref)
+    b = own_rows(c, (2, 1 - y), normed, g, qg_ref, ho_ref)
+    copies[0].wait()
+    sz_ref[...] = (a + part_rows(got, 1 - z)).astype(BF)
+    sy_ref[...] = (b + part_rows(got, 3 - y)).astype(BF)
 
 
 def post_body(
-    pn_ref, x_ref, g_ref, stat_ref, gain_ref, own_ref, gz_ref, gy_ref, order_ref, o_ref
+    bits_ref, pn_ref, x_ref, g_ref, stat_ref, gain_ref,
+    normed_ref, gall_ref, qg_ref, ho_ref, order_ref, got_ref, gz_ref, gy_ref,
+    o_ref,
+    got, gz, gy, sems,
 ):
+    copies = fetch(sems, (got_ref, got), (gz_ref, gz), (gy_ref, gy))
+    c, z, y = bits_ref[0], bits_ref[1], bits_ref[2]
+    normed, gall = normed_ref[...], gall_ref[...]
+    own_a = own_rows(c, (z, None), normed, gall, qg_ref, ho_ref)
+    own_b = own_rows(c, (2, y), normed, gall, qg_ref, ho_ref)
     pn = jnp.sum(pn_ref[...].astype(F32), axis=0)
-    ps = pn[:, :QP]
-    ns = pn[:, QP:]
-    x = x_ref[...].astype(F32)
+    ps = pn[:, :QW]
+    ns = pn[:, QP : QP + QW]
+    x = x_ref[...]
     mean = stat_ref[:, 0:1]
     inv = stat_ref[:, 64:65]
     xh = (x - mean) * inv
-    tile = ns[:, 256:]
+    tile = pn[:, QP + 256 :]
     ln = lane((R, R))
     m1 = jnp.sum(jnp.where((ln == MEAN_AT) | (ln == MEAN_AT + 1), tile, 0.0), axis=1, keepdims=True)
     m2 = jnp.sum(
         jnp.where((ln == MEAN_AT + 2) | (ln == MEAN_AT + 3), tile, 0.0), axis=1, keepdims=True
     )
     enc = x + ps
-    grad = g_ref[...].astype(F32) + inv * (ns * gain_ref[...] - m1 - xh * m2)
-    got = jnp.concatenate([gz_ref[...], gy_ref[...]], axis=0).astype(F32)
-    wg = (own_ref[...] + got).astype(BF)
+    grad = g_ref[...] + inv * (ns * gain_ref[...] - m1 - xh * m2)
+    for copy in copies:
+        copy.wait()
+    wg = jnp.concatenate(
+        [
+            own_a + part_rows(got, z) + gz[...].astype(F32),
+            own_b + part_rows(got, 2 + y) + gy[...].astype(F32),
+        ],
+        axis=0,
+    ).astype(BF)
     wg = dg(order_ref[...], wg, 1, 1)
     slabs = [wg[i * R : (i + 1) * R] for i in range(10)]
-    o_ref[...] = jnp.concatenate(
-        slabs + [tile[:, 64:], enc[:, :QW], grad[:, :QW]], axis=1
-    ).astype(BF)
+    row = jnp.concatenate(slabs + [tile[:, 64:], enc, grad], axis=1).astype(BF)
+    at = sub((2 * R, R)) - 2 * lane((2 * R, R))
+    both = dg(one_hot(at == 0), row[:, :HALF], 1, 0) + dg(one_hot(at == 1), row[:, HALF:], 1, 0)
+    o_ref[...] = both.astype(BF).reshape(R, 2, HALF)
 
 
 def final_body(send_ref, b_ref, e_ref, i_ref, a_ref, w_ref, gain_ref, bias_ref):
-    pick = (sub((R, R)) == send_ref[...]).astype(F32).astype(BF)
-    rows = dg(b_ref[:, WG:], pick, 0, 1).astype(BF)
+    _, odd = pair_picks(send_ref)
+    back = b_ref[...].reshape(2 * R, HALF)
+    rows = dg(back[:, WG - HALF :], odd, 0, 1).astype(BF)
     e_ref[...] = rows[:QW]
     i_ref[...] = rows[QW:]
-    row = sub((16, R))
-    src = lane((16, R))
+    row = sub((16, 2 * R))
+    src = lane((16, 2 * R)) // 2
     half = (row // 2) % 2
     c_ok = src % 2 == row % 2
     z_ok = (src // 2) % 2 == half
     y_ok = (src // 16) % 2 == half
     mask = ((row < 4) & c_ok & z_ok) | ((row >= 4) & (row < 8) & c_ok & y_ok) | (row == 8)
-    sums = dg(mask.astype(F32).astype(BF), b_ref[:, :WG], 1, 0)
+    first = lane((16, 2 * R)) % 2 == 0
+    sums = jnp.concatenate(
+        [
+            dg(one_hot(mask & first), back, 1, 0),
+            dg(one_hot(mask & ~first), back[:, : WG - HALF], 1, 0),
+        ],
+        axis=1,
+    )
     for i in range(10):
         at = i * 2 * HD
         a_ref[i, 0] = sums[0:2, at : at + HD]
@@ -211,7 +293,7 @@
 def local(patches, cotangent, send_order, recv_order, segment_ids, ln_gain, ln_bias, w_qkv, w_out):
     zero = lax.axis_index("zero")
     dp = lax.axis_index("dp")
-    bits = jnp.stack([dp & 1, (dp >> 1) & 1, (dp >> 4) & 1])
+    bits = jnp.stack([dp & 1, (dp >> 1) & 1, (dp >> 4) & 1, zero])
     wq = w_qkv.transpose(1, 2, 3, 0).reshape(NQ, D)
     wo = w_out.reshape(NO, D)
     gain = ln_gain.reshape(1, D)
@@ -223,37 +305,43 @@
     def swap(a, bit):
         return lax.ppermute(a, "dp", [(i, i ^ bit) for i in range(128)])
 
-    (xg,) = call(gather_body, [((R, 2 * D), BF)], send_order, patches, cotangent)
+    (xg,) = call(gather_body, [((R, 2, D), BF)], send_order, patches, cotangent, hbm=(1, 2))
     xg = lax.all_to_all(xg, "dp", 0, 0, tiled=True)
-    pn, normed, qg, ho, stat = call(
+    pn, send, normed, g, qg, ho, stat, xq, gq, gainq = call(
         block_body,
-        [((4, R, 2 * QP), BF), ((R, D), BF), ((NQ, R), BF), ((NO, R), BF), ((R, R), F32)],
-        xg, recv_order, segment_ids, gain, bias, wq, wo, sel, place,
-    )
+        [
+            ((4, R, 2 * QP), BF),
+            ((4 * HD, D), BF),
+            ((R, D), BF),
+            ((R, D), BF),
+            ((NQ, R), BF),
+            ((NO, R), BF),
+            ((R, R), F32),
+            ((R, QW), F32),
+            ((R, QW), F32),
+            ((1, QW), F32),
+        ],
+        bits, xg, recv_order, segment_ids, gain, bias, wq, wo, sel, place,
+        smem=(0,),
+        hbm=(6, 7, 8, 9),
+    )
+    got = swap(send, 1)
     pn = lax.all_to_all(pn, "zero", 0, 0, tiled=True)
-    keep, send = call(
-        wgrad_body,
-        [((4 * HD, D), F32), ((4 * HD, D), BF)],
-        bits, normed, xg, qg, ho,
+    sz, sy = call(
+        pair_body,
+        [((HD, D), BF), ((HD, D), BF)],
+        bits, normed, g, qg, ho, got,
         smem=(0,),
-    )
-    own, sz, sy = call(
-        pair_body,
-        [((2 * HD, D), F32), ((HD, D), BF), ((HD, D), BF)],
-        bits, keep, swap(send, 1),
-        smem=(0,),
+        hbm=(5,),
     )
     gz = swap(sz, 2)
     gy = swap(sy, 16)
-
-    def quarter(a, at=0):
-        a = lax.dynamic_slice_in_dim(a, at + zero * QW, QW, 1)
-        return jnp.pad(a, ((0, 0), (0, QP - QW)))
-
     (back,) = call(
         post_body,
-        [((R, WG + 2 * QW), BF)],
-        pn, quarter(xg), quarter(xg, D), stat, quarter(gain), own, gz, gy, order,
+        [((R, 2, HALF), BF)],
+        bits, pn, xq, gq, stat, gainq, normed, g, qg, ho, order, got, gz, gy,
+        smem=(0,),
+        hbm=(11, 12, 13),
     )
     back = lax.all_to_all(back, "dp", 0, 0, tiled=True)
     enc, grad, qkv_share, out_share, gain_grad, bias_grad = call(

time: 118 us -> 124 us (1.051)
  Pallas kernels: 10.2 us -> 16.8 us
  local copies, waits for them, and re-layouts: 15.9 us -> 19.2 us
  other arithmetic: 3.27 us -> 0.08 us
  waiting for transfers between devices: 27.9 us -> 26.2 us
    pallas_call x6 -> x5, Pallas kernels: 10.2 us -> 16.8 us  [call(): pl.pallas_call(body, out_shape=tuple((jax.ShapeDtypeStruct(s, d) for s, d...]
    all_to_all x2 -> x0, other arithmetic: 3.2 us -> none  [the longest x1 2.1 us: local(): back = lax.all_to_all(back, 'dp', 0, 0, tiled=True)]
    unnamed x46 -> x44, local copies, waits for them, and re-layouts: 14.5 us -> 17.7 us
    all_to_all x1, waiting for transfers between devices: 0.78 us -> 2.95 us  [local(): pn = lax.all_to_all(pn, 'zero', 0, 0, tiled=True)]
    ppermute x3, waiting for transfers between devices: 4.96 us -> 2.86 us  [swap(): return lax.ppermute(a, 'dp', [(i, i ^ bit) for i in range(128)])]
    all_to_all x1, waiting for transfers between devices: 22.2 us -> 20.4 us  [local(): xg = lax.all_to_all(xg, 'dp', 0, 0, tiled=True)]
  transfers between devices with their start and end apart: 5 -> 5, of which waited for: 4 -> 4; matrix products, arithmetic and copies ran while one was open for 1% -> 1% of each run, Pallas kernels for 1% -> 2%
where the time goes in v3:
time: 124 us; the launch traced here: 122 us
  starting transfers between devices  31.6 us (25%)
  blocking collectives  27.6 us (22%)
  waiting for transfers between devices  26.2 us (21%)
  local copies, waits for them, and re-layouts  19.2 us (15%)
  Pallas kernels  16.8 us (14%)
    all_to_all x1, blocking collectives, local(): back = lax.all_to_all(back, 'dp', 0, 0, tiled=True)  27.6 us
    all_to_all x1, waiting for transfers between devices, local(): xg = lax.all_to_all(xg, 'dp', 0, 0, tiled=True)  20.4 us
    all_to_all x1, starting transfers between devices, local(): xg = lax.all_to_all(xg, 'dp', 0, 0, tiled=True)  18.8 us
    unnamed x44, local copies, waits for them, and re-layouts  17.7 us
    pallas_call x5, Pallas kernels, call(): pl.pallas_call(body, out_shape=tuple((jax.ShapeDtypeStruct(s, d) for s, d...  16.8 us
    ppermute x3, starting transfers between devices, swap(): return lax.ppermute(a, 'dp', [(i, i ^ bit) for i in range(128)])  8.54 us
    all_to_all x1, starting transfers between devices, local(): pn = lax.all_to_all(pn, 'zero', 0, 0, tiled=True)  4.21 us
    all_to_all x1, waiting for transfers between devices, local(): pn = lax.all_to_all(pn, 'zero', 0, 0, tiled=True)  2.95 us
  transfers between devices with their start and end apart: 5, of which 4 were waited for; matrix products, arithmetic and copies ran while one was open for 1% of the time, Pallas kernels for 2%

profile of v3, /device:TPU:1, one launch (start us, length us, event | category | flops | bytes accessed | tf_op | source)
XLA Modules:
  0.0 122.2 jit_solution(14575800207029341085)
XLA Ops:
  0.6 0.0 copy-start.12
  0.6 1.0 copy-done.12
  1.6 0.0 copy-start.13
  1.6 1.0 copy-done.13
  2.6 0.0 copy-start.18
  2.6 0.7 copy-done.18
  3.2 1.8 %shard_map.163 = bf16[128,2,1280]{2,1,0:T(2,128)(2,1)} custom-call(s32[1,128]{1,0:T(1,128)S(1)} %copy-done.18, bf16[128,1280]{1,0:T(8,128)(2,1)S(1)} %copy-done.12, bf16[128,1280]{1,0:T(8,128)(2,1)S(1)} %copy-done.13), custom_call_target="tpu_custom_call" | custom-call | tf_op jit(solution)/shard_map/pallas_call | solution.py:40
  5.1 18.8 %all-to-all-start = ((bf16[128,2,1280]{2,1,0:T(2,128)(2,1)}), bf16[128,2,1280]{2,1,0:T(2,128)(2,1)}, u32[]{:S(2)}, u32[]{:S(2)}) async-start(bf16[128,2,1280]{2,1,0:T(2,128)(2,1)} %shard_map.163), calls=%async_computation | async-start | bytes 1310720 | tf_op jit(solution)/shard_map/all_to_all | solution.py:309
  23.9 0.7 reshape.30.gain_ref
  24.6 0.0 copy-start
  24.6 0.9 reshape.31.bias_ref
  25.5 0.1 pad_add_fusion.bits_ref
  25.6 20.4 %all-to-all-done.xg_ref = bf16[128,2,1280]{2,1,0:T(2,128)(2,1)} async-done(((bf16[128,2,1280]{2,1,0:T(2,128)(2,1)}), bf16[128,2,1280]{2,1,0:T(2,128)(2,1)}, u32[]{:S(2)}, u32[]{:S(2)}) %all-to-all-start) | async-done | bytes 655392 | tf_op jit(solution)/shard_map/all_to_all | solution.py:309
  46.0 0.0 copy-start.7
  46.0 1.3 %copy-done.7 = bf16[1280,2,3,80]{0,3,2,1:T(8,128)(2,1)S(1)} copy-done((bf16[1280,2,3,80]{0,3,2,1:T(8,128)(2,1)S(1)}, bf16[1280,2,3,80]{0,3,2,1:T(8,128)(2,1)}, u32[]{:S(2)}) %copy-start.7) | copy-done | bytes 1228824
  47.3 0.0 copy-start.9
  47.3 1.1 copy-done.9
  48.3 0.0 copy-start.10
  48.3 1.0 copy-done.10
  49.3 0.0 copy-start.11
  49.3 1.0 copy-done.11
  50.3 0.0 copy-start.20
  50.3 0.7 copy-done.20
  51.0 0.0 copy-start.21
  51.0 0.7 copy-done.21
  51.6 6.4 %shard_map.164 = (bf16[4,128,768]{2,1,0:T(8,128)(2,1)S(1)}, bf16[320,1280]{1,0:T(8,128)(2,1)}, bf16[128,1280]{1,0:T(8,128)(2,1)S(1)}, bf16[128,1280]{1,0:T(8,128...) custom-call(s32[4]{0:T(128)S(1)} %pad_add_fusion.bits_ref, ...), custom_call_target="tpu_custom_call" | custom-call | tf_op jit(solution)/shard_map/pallas_call | solution.py:40
  58.0 0.0 copy-start.1
  58.0 0.7 copy-done.1
  58.8 0.0 copy-start.4
  58.8 0.7 copy-done.4
  59.5 0.0 copy-start.8
  59.5 0.9 copy-done.8
  60.4 0.0 copy-start.14
  60.4 0.7 copy-done.14
  61.1 0.0 copy-start.16
  61.1 0.7 copy-done.16
  61.7 3.8 %collective-permute-start = (bf16[320,1280]{1,0:T(8,128)(2,1)}, bf16[320,1280]{1,0:T(8,128)(2,1)}, u32[]{:S(2)}, u32[]{:S(2)}) collective-permute-start(bf16[320,1280]{1,0:T(8,128)(2,1)} %get-tuple-element.33), channel_id=1, source_target_pairs={{0,4},{4,0},{8,12},{12,8},{16,20},{20,16},{24,28},{28,24},{32,36},... | collective-permute-start | bytes 2457608 | tf_op jit(solution)/shard_map/ppermute | solution.py:306
  65.5 4.2 %all-to-all-start.1 = ((bf16[4,128,768]{2,1,0:T(8,128)(2,1)}), bf16[4,128,768]{2,1,0:T(8,128)(2,1)}, u32[]{:S(2)}, u32[]{:S(2)}) async-start(bf16[4,128,768]{2,1,0:T(8,128)(2,1)} %copy-done.8), calls=%async_computation.1 | async-start | bytes 1572864 | tf_op jit(solution)/shard_map/all_to_all | solution.py:329
  69.7 0.0 collective-permute-done.got_ref
  69.7 0.0 copy-start.2
  69.8 1.0 copy-done.2
  70.7 0.0 copy-start.5
  70.7 1.0 copy-done.5
  71.7 2.7 %shard_map.165 = (bf16[80,1280]{1,0:T(8,128)(2,1)}, bf16[80,1280]{1,0:T(8,128)(2,1)}) custom-call(s32[4]{0:T(128)S(1)} %pad_add_fusion.bits_ref, bf16[128,1280]{1,0:T(8,128)(2,1)S(1)} %copy-done.2, bf16[128,1280]{1,0:T(8,128)(2,1)S(1)} %copy-done.5, bf16[480,128]{1,0:T(8,128)(2,1)S(1)} %get-tuple-element.31.qg_ref, ...), custom_call_target="tpu_custom_call" | custom-call | tf_op jit(solution)/shard_map/pallas_call | solution.py:40
  74.4 2.1 %collective-permute-start.1 = (bf16[80,1280]{1,0:T(8,128)(2,1)}, bf16[80,1280]{1,0:T(8,128)(2,1)}, u32[]{:S(2)}, u32[]{:S(2)}) collective-permute-start(bf16[80,1280]{1,0:T(8,128)(2,1)} %get-tuple-element.34), channel_id=1, source_target_pairs={{0,8},{4,12},{8,0},{12,4},{16,24},{20,28},{24,16},{28,20},{32,40},... | collective-permute-start | bytes 614408 | tf_op jit(solution)/shard_map/ppermute | solution.py:306
  76.4 2.7 %collective-permute-start.2 = (bf16[80,1280]{1,0:T(8,128)(2,1)}, bf16[80,1280]{1,0:T(8,128)(2,1)}, u32[]{:S(2)}, u32[]{:S(2)}) collective-permute-start(bf16[80,1280]{1,0:T(8,128)(2,1)} %get-tuple-element.35), channel_id=1, source_target_pairs={{0,64},{4,68},{8,72},{12,76},{16,80},{20,84},{24,88},{28,92},{32,9... | collective-permute-start | bytes 614408 | tf_op jit(solution)/shard_map/ppermute | solution.py:306
  79.1 2.9 %all-to-all-done.1.pn_ref = bf16[4,128,768]{2,1,0:T(8,128)(2,1)} async-done(((bf16[4,128,768]{2,1,0:T(8,128)(2,1)}), bf16[4,128,768]{2,1,0:T(8,128)(2,1)}, u32[]{:S(2)}, u32[]{:S(2)}) %all-to-all-start.1) | async-done | bytes 786464 | tf_op jit(solution)/shard_map/all_to_all | solution.py:329
  82.1 1.1 collective-permute-done.1.gz_ref
  83.2 1.7 %collective-permute-done.2.gy_ref = bf16[80,1280]{1,0:T(8,128)(2,1)} collective-permute-done((bf16[80,1280]{1,0:T(8,128)(2,1)}, bf16[80,1280]{1,0:T(8,128)(2,1)}, u32[]{:S(2)}, u32[]{:S(2)}) %collective-permute-start.2) | collective-permute-done | bytes 204832 | tf_op jit(solution)/shard_map/ppermute | solution.py:306
  84.9 0.0 copy-done
  84.9 0.0 copy-start.3
  84.9 1.0 copy-done.3
  85.9 0.0 copy-start.6
  85.9 1.0 copy-done.6
  86.9 0.0 copy-start.15
  86.9 0.9 copy-done.15
  87.8 0.0 copy-start.17
  87.8 0.9 copy-done.17
  88.7 0.0 copy-start.19
  88.7 4.7 %shard_map.166 = bf16[128,2,1152]{2,1,0:T(2,128)(2,1)S(1)} custom-call(s32[4]{0:T(128)S(1)} %pad_add_fusion.bits_ref, bf16[4,128,768]{2,1,0:T(8,128)(2,1)} %all-to-all-done.1.pn_ref, f32[128,320]{1,0:T(8,128)S(1)} %copy-done.15, f32[128,320]{1,0:T(8,128)S(1)} %copy-done.17, f32[128,128]{1,0:T(8,128)S(1)} %get-tuple-element.27.stat_ref, ...), custom_call_target="tpu_custom_call" | custom-call | tf_op jit(solution)/shard_map/pallas_call | solution.py:40
  93.5 27.6 %all_to_all.15.b_ref = bf16[128,2,1152]{2,1,0:T(2,128)(2,1)S(1)} all-to-all(bf16[128,2,1152]{2,1,0:T(2,128)(2,1)S(1)} %shard_map.166), channel_id=1, replica_groups=mesh['dp'=128,'zero'=4] {'dp'}, dimensions={0} | all-to-all | bytes 1179648 | tf_op jit(solution)/shard_map/all_to_all | solution.py:346
  121.0 0.0 copy-done.19
  121.0 1.1 shard_map.167
Async XLA Ops:
  0.6 1.0 copy-start.12
  1.6 1.0 copy-start.13
  2.6 0.7 copy-start.18
  5.1 40.9 %all-to-all-start = ((bf16[128,2,1280]{2,1,0:T(2,128)(2,1)}), bf16[128,2,1280]{2,1,0:T(2,128)(2,1)}, u32[]{:S(2)}, u32[]{:S(2)}) async-start(bf16[128,2,1280]{2,1,0:T(2,128)(2,1)} %shard_map.163), calls=%async_computation | async-start | bytes 1310720 | tf_op jit(solution)/shard_map/all_to_all | solution.py:309
  24.6 60.3 %copy-start = (bf16[1280,1280]{1,0:T(8,128)(2,1)S(1)}, bf16[1280,1280]{1,0:T(8,128)(2,1)}, u32[]{:S(2)}) copy-start(bf16[1280,1280]{1,0:T(8,128)(2,1)} %constant.21.clone.order_ref) | copy-start | bytes 9830404
  46.0 1.3 %copy-start.7 = (bf16[1280,2,3,80]{0,3,2,1:T(8,128)(2,1)S(1)}, bf16[1280,2,3,80]{0,3,2,1:T(8,128)(2,1)}, u32[]{:S(2)}) copy-start(bf16[1280,2,3,80]{0,3,2,1:T(8,128)(2,1)} %param.19) | copy-start | bytes 3686404
  47.3 1.1 copy-start.9
  48.3 1.0 copy-start.10
  49.3 1.0 copy-start.11
  50.3 0.7 copy-start.20
  51.0 0.7 copy-start.21
  58.0 0.7 copy-start.1
  58.8 0.7 copy-start.4
  59.5 0.9 copy-start.8
  60.4 0.7 copy-start.14
  61.1 0.7 copy-start.16
  61.7 8.0 %collective-permute-start = (bf16[320,1280]{1,0:T(8,128)(2,1)}, bf16[320,1280]{1,0:T(8,128)(2,1)}, u32[]{:S(2)}, u32[]{:S(2)}) collective-permute-start(bf16[320,1280]{1,0:T(8,128)(2,1)} %get-tuple-element.33), channel_id=1, source_target_pairs={{0,4},{4,0},{8,12},{12,8},{16,20},{20,16},{24,28},{28,24},{32,36},... | collective-permute-start | bytes 2457608 | tf_op jit(solution)/shard_map/ppermute | solution.py:306
  65.5 16.6 %all-to-all-start.1 = ((bf16[4,128,768]{2,1,0:T(8,128)(2,1)}), bf16[4,128,768]{2,1,0:T(8,128)(2,1)}, u32[]{:S(2)}, u32[]{:S(2)}) async-start(bf16[4,128,768]{2,1,0:T(8,128)(2,1)} %copy-done.8), calls=%async_computation.1 | async-start | bytes 1572864 | tf_op jit(solution)/shard_map/all_to_all | solution.py:329
  69.7 1.0 copy-start.2
  70.7 1.0 copy-start.5
  74.4 8.9 %collective-permute-start.1 = (bf16[80,1280]{1,0:T(8,128)(2,1)}, bf16[80,1280]{1,0:T(8,128)(2,1)}, u32[]{:S(2)}, u32[]{:S(2)}) collective-permute-start(bf16[80,1280]{1,0:T(8,128)(2,1)} %get-tuple-element.34), channel_id=1, source_target_pairs={{0,8},{4,12},{8,0},{12,4},{16,24},{20,28},{24,16},{28,20},{32,40},... | collective-permute-start | bytes 614408 | tf_op jit(solution)/shard_map/ppermute | solution.py:306
  76.4 8.5 %collective-permute-start.2 = (bf16[80,1280]{1,0:T(8,128)(2,1)}, bf16[80,1280]{1,0:T(8,128)(2,1)}, u32[]{:S(2)}, u32[]{:S(2)}) collective-permute-start(bf16[80,1280]{1,0:T(8,128)(2,1)} %get-tuple-element.35), channel_id=1, source_target_pairs={{0,64},{4,68},{8,72},{12,76},{16,80},{20,84},{24,88},{28,92},{32,9... | collective-permute-start | bytes 614408 | tf_op jit(solution)/shard_map/ppermute | solution.py:306
  84.9 1.0 copy-start.3
  85.9 1.0 copy-start.6
  86.9 0.9 copy-start.15
  87.8 0.9 copy-start.17
  88.7 32.3 %copy-start.19 = (s32[1,128]{1,0:T(1,128)S(1)}, s32[1,128]{1,0:T(1,128)}, u32[]{:S(2)}) copy-start(s32[1,128]{1,0:T(1,128)} %send_ref.3) | copy-start | bytes 1540

commit v4 on v3

v4 whole, which is shorter than its diff:
```python
import jax
import jax.numpy as jnp
from jax import lax
from jax.experimental import pallas as pl
from jax.experimental.pallas import tpu as pltpu
from jax.sharding import PartitionSpec as P

EPS = 1e-06
R = 128
D = 1280
HD = 80
HG = 2
NQ = HG * 3 * HD
NO = HG * HD
QW = D // 4
QP = 384
F32 = jnp.float32
BF = jnp.bfloat16
GAIN_AT = 64
BIAS_AT = 74
MEAN_AT = 84
WG = 1664
HALF = (WG + 2 * QW) // 2

MIB = 1024 * 1024
MIB_HOLD, MIB_BLOCK, MIB_PAIR, MIB_POST = 16, 50, 50, 50


def dg(a, b, ca, cb):
    return lax.dot_general(a, b, (((ca,), (cb,)), ((), ())), preferred_element_type=F32)


def call(body, outs, *args, smem=(), hbm=(), scratch=(), mib=50):
    def space(i):
        return pltpu.SMEM if i in smem else pltpu.HBM if i in hbm else pltpu.VMEM

    scratch = list(scratch) + [pltpu.VMEM(args[i].shape, args[i].dtype) for i in hbm]
    if hbm:
        scratch.append(pltpu.SemaphoreType.DMA((len(hbm),)))
    return pl.pallas_call(
        body,
        out_shape=tuple(jax.ShapeDtypeStruct(s, d) for s, d in outs),
        in_specs=[pl.BlockSpec(memory_space=space(i)) for i in range(len(args))],
        out_specs=tuple(pl.BlockSpec(memory_space=pltpu.VMEM) for _ in outs),
        scratch_shapes=scratch,
        compiler_params=pltpu.CompilerParams(vmem_limit_bytes=mib * MIB),
    )(*args)


def fetch(sems, *pairs):
    copies = [pltpu.make_async_copy(a, b, sems.at[i]) for i, (a, b) in enumerate(pairs)]
    for copy in copies:
        copy.start()
    return copies


def lane(shape):
    return lax.broadcasted_iota(jnp.int32, shape, 1)


def sub(shape):
    return lax.broadcasted_iota(jnp.int32, shape, 0)


def one_hot(cond):
    return cond.astype(F32).astype(BF)


def pair_picks(send_ref):
    spread = one_hot(lane((R, 2 * R)) // 2 == sub((R, 2 * R)))
    rows = jnp.broadcast_to(send_ref[...], (8, R)).astype(F32).astype(BF)
    target = dg(rows, spread, 1, 0)[0:1].astype(jnp.int32)
    hit = sub((R, 2 * R)) == target
    odd = lane((R, 2 * R)) % 2
    return one_hot(hit & (odd == 0)), one_hot(hit & (odd == 1))


def gather_body(send_ref, x_ref, g_ref, o_ref, x_buf, g_buf, sems):
    copies = fetch(sems, (x_ref, x_buf), (g_ref, g_buf))
    even, odd = pair_picks(send_ref)
    copies[0].wait()
    rows = dg(even, x_buf[...], 0, 0)
    copies[1].wait()
    rows = rows + dg(odd, g_buf[...], 0, 0)
    o_ref[...] = rows.astype(BF).reshape(R, 2, D)


def norm_stats(x):
    mean = jnp.mean(x, axis=1, keepdims=True)
    centred = x - mean
    inv = lax.rsqrt(jnp.mean(centred * centred, axis=1, keepdims=True) + EPS)
    return mean, inv, centred * inv


def hold_body(
    recv_ref, seg_ref, gain_ref, bias_ref, wo_ref, same_ref, gain_out, bias_out, wo_out
):
    hit = sub((R, R)) == recv_ref[...]
    seg = jnp.sum(jnp.where(hit, seg_ref[...], 0), axis=1, keepdims=True)
    group = one_hot(seg == lane((R, R)))
    same_ref[...] = dg(group, group, 1, 1)
    gain_out[...] = gain_ref[...]
    bias_out[...] = bias_ref[...]
    wo_out[...] = wo_ref[...]


def block_body(
    bits_ref, xg_ref, same_ref, gain_ref, bias_ref, wo_ref, wq_hbm,
    pn_ref, send_ref, ng_ref, heads_ref, aux_ref,
    wq_ref, sems,
):
    copies = fetch(sems, (wq_hbm, wq_ref))
    xg = xg_ref[...].reshape(2 * R, D)
    at = lane((R, 2 * R)) - 2 * sub((R, 2 * R))
    x = dg(one_hot(at == 0), xg, 1, 0)
    g32 = dg(one_hot(at == 1), xg, 1, 0)
    g = g32.astype(BF)
    ng_ref[R:, :] = g
    mean, inv, xh = norm_stats(x)
    normed = (xh * gain_ref[...] + bias_ref[...]).astype(BF)
    ng_ref[:R, :] = normed
    for i in range(4):

        @pl.when(bits_ref[3] == i)
        def _(i=i):
            cols = slice(i * QW, (i + 1) * QW)
            tail = (R, QP - QW)
            rows = [
                x[:, cols], jnp.broadcast_to(mean, tail),
                g32[:, cols], jnp.broadcast_to(inv, tail),
                jnp.broadcast_to(gain_ref[:, cols], (R, QW)), jnp.zeros(tail, F32),
            ]
            aux_ref[...] = jnp.concatenate(rows, axis=1)

    copies[0].wait()
    qkv = dg(wq_ref[...], normed, 1, 1).astype(BF)
    dh = dg(wo_ref[...], g, 1, 1).astype(BF)
    same = same_ref[...] > 0.5
    rows = []
    for h in range(HG):
        q = qkv[h * 3 * HD : h * 3 * HD + HD]
        k = qkv[h * 3 * HD + HD : h * 3 * HD + 2 * HD]
        v = qkv[h * 3 * HD + 2 * HD : (h + 1) * 3 * HD]
        dhh = dh[h * HD : (h + 1) * HD]
        s = jnp.where(same, dg(q, k, 0, 0) * (HD**-0.5), -1e30)
        e = jnp.exp(s - jnp.max(s, axis=1, keepdims=True))
        w = e / jnp.sum(e, axis=1, keepdims=True)
        w16 = w.astype(BF)
        pg = dg(dhh, v, 0, 0)
        delta = jnp.sum(pg * w, axis=1, keepdims=True)
        sg = (w * (pg - delta) * (HD**-0.5)).astype(BF)
        rows.append(dg(k, sg, 1, 1).astype(BF))
        rows.append(dg(q, sg, 1, 0).astype(BF))
        rows.append(dg(dhh, w16, 1, 0).astype(BF))
        rows.append(dg(v, w16, 1, 1).astype(BF))
    heads_ref[...] = jnp.concatenate(rows, axis=0)
    qg = jnp.concatenate(rows[0:3] + rows[4:7], axis=0)
    ho = jnp.concatenate([rows[3], rows[7]], axis=0)
    other = (1 - bits_ref[0]) * 4 * HD
    a = heads_ref[pl.ds(pl.multiple_of(other, 4 * HD), 3 * HD), :]
    b = heads_ref[pl.ds(pl.multiple_of(other + 3 * HD, HD), HD), :]
    send_ref[: 3 * HD, :] = dg(a, normed, 1, 0).astype(BF)
    send_ref[3 * HD :, :] = dg(b, g, 1, 0).astype(BF)
    p = dg(ho, wo_ref[...], 0, 0)
    n = dg(qg, wq_ref[...], 0, 0)
    u = n * gain_ref[...]
    m1 = jnp.sum(u, axis=1, keepdims=True) * (1.0 / D)
    m2 = jnp.sum(u * xh, axis=1, keepdims=True) * (1.0 / D)
    gain_row = jnp.sum(n * xh, axis=0, keepdims=True)
    bias_row = jnp.sum(n, axis=0, keepdims=True)
    first = lane((R, D)) - 10 * sub((R, D))
    sel = (first >= 0) & (first < 10)
    both = jnp.concatenate(
        [jnp.where(sel, gain_row, 0.0).astype(BF), jnp.where(sel, bias_row, 0.0).astype(BF)], axis=0
    )
    f = sub((D, R)).astype(F32)
    k = f - 10.0 * jnp.floor((f + 0.5) * 0.1)
    both = dg(both, one_hot(k == (lane((D, R)) - GAIN_AT).astype(F32)), 1, 0)
    extra = both[:R] + pltpu.roll(both[R:], BIAS_AT - GAIN_AT, 1)
    ln = lane((R, R))
    for j, m in enumerate((m1, m2)):
        hi = m.astype(BF).astype(F32)
        extra = jnp.where(ln == MEAN_AT + 2 * j, hi, extra)
        extra = jnp.where(ln == MEAN_AT + 2 * j + 1, m - hi, extra)
    pad = jnp.zeros((R, QP - QW), F32)
    for i in range(4):
        part = jnp.concatenate([p[:, i * QW : (i + 1) * QW], pad], axis=1)
        pn_ref[i, :, :QP] = part.astype(BF)
        part = jnp.concatenate([n[:, i * QW : (i + 1) * QW], extra[:, 64:]], axis=1)
        pn_ref[i, :, QP:] = part.astype(BF)


def own_rows(c, first, choose_out, ng_ref, heads_ref):
    a = heads_ref[pl.ds(pl.multiple_of((c * 4 + first) * HD, HD), HD), :]
    if choose_out is None:
        return dg(a, ng_ref[:R, :], 1, 0)
    b = heads_ref[pl.ds(pl.multiple_of((c * 4 + 3) * HD, HD), HD), :]
    pick = choose_out.astype(F32)
    left = jnp.concatenate([a.astype(F32) * (1.0 - pick), b.astype(F32) * pick], axis=1).astype(BF)
    return dg(left, ng_ref[...], 1, 0)


def part_rows(ref, j):
    return ref[pl.ds(pl.multiple_of(j * HD, HD), HD), :].astype(F32)


def pair_body(bits_ref, ng_ref, heads_ref, got_ref, sz_ref, sy_ref):
    c, z, y = bits_ref[0], bits_ref[1], bits_ref[2]
    a = own_rows(c, 1 - z, None, ng_ref, heads_ref)
    b = own_rows(c, 2, 1 - y, ng_ref, heads_ref)
    sz_ref[...] = (a + part_rows(got_ref, 1 - z)).astype(BF)
    sy_ref[...] = (b + part_rows(got_ref, 3 - y)).astype(BF)


def post_body(
    bits_ref, pn_ref, aux_ref, ng_ref, heads_ref, got_ref, gz_ref, gy_ref, o_ref, wz_ref, wy_ref
):
    c, z, y = bits_ref[0], bits_ref[1], bits_ref[2]
    wz = own_rows(c, z, None, ng_ref, heads_ref) + part_rows(got_ref, z)
    wz_ref[:, :HD] = (wz + gz_ref[...].astype(F32)).T
    wy = own_rows(c, 2, y, ng_ref, heads_ref) + part_rows(got_ref, 2 + y)
    wy_ref[:, :HD] = (wy + gy_ref[...].astype(F32)).T
    slabs = []
    for i in range(10):
        for ref in (wz_ref, wy_ref):
            slabs.append(ref[pl.ds(i, R, stride=10), :][:, :HD])
    pn = jnp.sum(pn_ref[...].astype(F32), axis=0)
    ps = pn[:, :QW]
    ns = pn[:, QP : QP + QW]
    x = aux_ref[:, :QW]
    mean = aux_ref[:, QW : QW + 1]
    inv = aux_ref[:, QP + QW : QP + QW + 1]
    xh = (x - mean) * inv
    tile = pn[:, QP + 256 :]
    ln = lane((R, R))
    m1 = jnp.sum(jnp.where((ln == MEAN_AT) | (ln == MEAN_AT + 1), tile, 0.0), axis=1, keepdims=True)
    m2 = jnp.sum(
        jnp.where((ln == MEAN_AT + 2) | (ln == MEAN_AT + 3), tile, 0.0), axis=1, keepdims=True
    )
    enc = x + ps
    grad = aux_ref[:, QP : QP + QW] + inv * (ns * aux_ref[:, 2 * QP : 2 * QP + QW] - m1 - xh * m2)
    row = jnp.concatenate(slabs + [tile[:, 64:], enc, grad], axis=1).astype(BF)
    at = sub((2 * R, R)) - 2 * lane((2 * R, R))
    both = dg(one_hot(at == 0), row[:, :HALF], 1, 0) + dg(one_hot(at == 1), row[:, HALF:], 1, 0)
    o_ref[...] = both.astype(BF).reshape(R, 2, HALF)


def final_body(send_ref, b_ref, e_ref, i_ref, a_ref, w_ref, gain_ref, bias_ref):
    _, odd = pair_picks(send_ref)
    back = b_ref[...].reshape(2 * R, HALF)
    rows = dg(back[:, WG - HALF :], odd, 0, 1).astype(BF)
    e_ref[...] = rows[:QW]
    i_ref[...] = rows[QW:]
    row = sub((16, 2 * R))
    src = lane((16, 2 * R)) // 2
    half = (row // 2) % 2
    c_ok = src % 2 == row % 2
    z_ok = (src // 2) % 2 == half
    y_ok = (src // 16) % 2 == half
    mask = ((row < 4) & c_ok & z_ok) | ((row >= 4) & (row < 8) & c_ok & y_ok) | (row == 8)
    first = lane((16, 2 * R)) % 2 == 0
    sums = jnp.concatenate(
        [
            dg(one_hot(mask & first), back, 1, 0),
            dg(one_hot(mask & ~first), back[:, : WG - HALF], 1, 0),
        ],
        axis=1,
    )
    for i in range(10):
        at = i * 2 * HD
        a_ref[i, 0] = sums[0:2, at : at + HD]
        a_ref[i, 1] = sums[2:4, at : at + HD]
        a_ref[i, 2] = sums[4:6, at + HD : at + 2 * HD]
        w_ref[i] = sums[6:8, at + HD : at + 2 * HD]
    gain_ref[...] = sums[8:9, WG - 64 : WG - 54]
    bias_ref[...] = sums[8:9, WG - 54 : WG - 44]


def local(patches, cotangent, send_order, recv_order, segment_ids, ln_gain, ln_bias, w_qkv, w_out):
    zero = lax.axis_index("zero")
    dp = lax.axis_index("dp")
    bits = jnp.stack([dp & 1, (dp >> 1) & 1, (dp >> 4) & 1, zero])
    wq = w_qkv.transpose(1, 2, 3, 0).reshape(NQ, D)
    wo = w_out.reshape(NO, D)
    gain = ln_gain.reshape(1, D)
    bias = ln_bias.reshape(1, D)

    def swap(a, bit):
        return lax.ppermute(a, "dp", [(i, i ^ bit) for i in range(128)])

    (xg,) = call(gather_body, [((R, 2, D), BF)], send_order, patches, cotangent, hbm=(1, 2), mib=58)
    same, gain, bias, wo = call(
        hold_body,
        [((R, R), F32), ((1, D), F32), ((1, D), F32), ((NO, D), BF)],
        recv_order, segment_ids, gain, bias, wo,
        mib=MIB_HOLD,
    )
    xg = lax.all_to_all(xg, "dp", 0, 0, tiled=True)
    pn, send, ng, heads, aux = call(
        block_body,
        [
            ((4, R, 2 * QP), BF),
            ((4 * HD, D), BF),
            ((2 * R, D), BF),
            ((8 * HD, R), BF),
            ((R, 3 * QP), F32),
        ],
        bits, xg, same, gain, bias, wo, wq,
        smem=(0,),
        hbm=(6,),
        mib=MIB_BLOCK,
    )
    got = swap(send, 1)
    pn = lax.all_to_all(pn, "zero", 0, 0, tiled=True)
    sz, sy = call(
        pair_body,
        [((HD, D), BF), ((HD, D), BF)],
        bits, ng, heads, got,
        smem=(0,),
        mib=MIB_PAIR,
    )
    gz = swap(sz, 2)
    gy = swap(sy, 16)
    (back,) = call(
        post_body,
        [((R, 2, HALF), BF)],
        bits, pn, aux, ng, heads, got, gz, gy,
        smem=(0,),
        scratch=[pltpu.VMEM((D, R), F32)] * 2,
        mib=MIB_POST,
    )
    back = lax.all_to_all(back, "dp", 0, 0, tiled=True)
    enc, grad, qkv_share, out_share, gain_grad, bias_grad = call(
        final_body,
        [
            ((QW, R), BF),
            ((QW, R), BF),
            ((10, 3, 2, HD), F32),
            ((10, 2, HD), F32),
            ((1, 10), F32),
            ((1, 10), F32),
        ],
        send_order, back,
    )
    return (
        enc.T,
        grad.T,
        qkv_share.transpose(0, 2, 1, 3),
        out_share.transpose(1, 2, 0),
        gain_grad.reshape(10),
        bias_grad.reshape(10),
    )


def solution(mesh):
    return jax.shard_map(
        local,
        mesh=mesh,
        in_specs=(
            P("dp", None),
            P("dp", None),
            P("dp", None),
            P("dp", None),
            P("dp", None),
            P(),
            P(),
            P(None, "zero", None, None),
            P("zero", None, None),
        ),
        out_specs=(
            P("dp", "zero"),
            P("dp", "zero"),
            P("dp", "zero", None, None),
            P("zero", None, "dp"),
            P("dp"),
            P("dp"),
        ),
        check_vma=False,
    )
```

time: 124 us -> 102 us (0.82)
  local copies, waits for them, and re-layouts: 19.2 us -> 0.04 us
  Pallas kernels: 16.8 us -> 14 us
  waiting for transfers between devices: 26.2 us -> 27.8 us
    unnamed x44 -> x12, local copies, waits for them, and re-layouts: 17.7 us -> 0.02 us
    all_to_all x1, waiting for transfers between devices: 2.95 us -> 5.86 us  [local(): pn = lax.all_to_all(pn, 'zero', 0, 0, tiled=True)]
    ppermute x3, waiting for transfers between devices: 2.86 us -> 0.01 us  [swap(): return lax.ppermute(a, 'dp', [(i, i ^ bit) for i in range(128)])]
    pallas_call x5 -> x6, Pallas kernels: 16.8 us -> 14 us  [call(): pl.pallas_call(body, out_shape=tuple((jax.ShapeDtypeStruct(s, d) for s, d...]
    all_to_all x1, waiting for transfers between devices: 20.4 us -> 21.9 us  [local(): xg = lax.all_to_all(xg, 'dp', 0, 0, tiled=True)]
  transfers between devices with their start and end apart: 5 -> 5, of which waited for: 4 -> 2; matrix products, arithmetic and copies ran while one was open for 1% -> 0% of each run, Pallas kernels for 2% -> 2%
where the time goes in v4:
time: 102 us; the launch traced here: 101 us
  starting transfers between devices  31 us (30%)
  waiting for transfers between devices  27.8 us (27%)
  blocking collectives  27.4 us (27%)
  Pallas kernels  14 us (14%)
    all_to_all x1, blocking collectives, local(): back = lax.all_to_all(back, 'dp', 0, 0, tiled=True)  27.4 us
    all_to_all x1, waiting for transfers between devices, local(): xg = lax.all_to_all(xg, 'dp', 0, 0, tiled=True)  21.9 us
    all_to_all x1, starting transfers between devices, local(): xg = lax.all_to_all(xg, 'dp', 0, 0, tiled=True)  18.4 us
    pallas_call x6, Pallas kernels, call(): pl.pallas_call(body, out_shape=tuple((jax.ShapeDtypeStruct(s, d) for s, d...  14 us
    ppermute x3, starting transfers between devices, swap(): return lax.ppermute(a, 'dp', [(i, i ^ bit) for i in range(128)])  8.51 us
    all_to_all x1, waiting for transfers between devices, local(): pn = lax.all_to_all(pn, 'zero', 0, 0, tiled=True)  5.86 us
    all_to_all x1, starting transfers between devices, local(): pn = lax.all_to_all(pn, 'zero', 0, 0, tiled=True)  4.02 us
  transfers between devices with their start and end apart: 5, of which 2 were waited for; matrix products, arithmetic and copies ran while one was open for 0% of the time, Pallas kernels for 2%

profile of v4, /device:TPU:1, one launch (start us, length us, event | category | flops | bytes accessed | tf_op | source)
XLA Modules:
  0.0 101.1 jit_solution(9021111541412625016)
XLA Ops:
  0.6 0.0 copy-start.4
  0.6 0.0 copy-start.5
  0.7 0.0 copy-start
  0.7 0.0 copy-start.3
  0.7 0.0 copy-start.2
  0.7 3.2 %shard_map.136 = bf16[128,2,1280]{2,1,0:T(2,128)(2,1)} custom-call(s32[1,128]{1,0:T(1,128)} %send_ref.3, bf16[128,1280]{1,0:T(8,128)(2,1)} %x_ref.1, bf16[128,1280]{1,0:T(8,128)(2,1)} %g_ref.1), custom_call_target="tpu_custom_call" | custom-call | tf_op jit(solution)/shard_map/pallas_call | solution.py:40
  3.9 18.4 %all-to-all-start = ((bf16[128,2,1280]{2,1,0:T(2,128)(2,1)}), bf16[128,2,1280]{2,1,0:T(2,128)(2,1)S(1)}, u32[]{:S(2)}, u32[]{:S(2)}) async-start(bf16[128,2,1280]{2,1,0:T(2,128)(2,1)} %shard_map.136), calls=%async_computation | async-start | bytes 1310720 | tf_op jit(solution)/shard_map/all_to_all | solution.py:298
  22.3 0.0 copy-done.4
  22.4 0.0 copy-done.5
  22.4 0.0 copy-done
  22.4 0.0 copy-done.3
  22.4 0.0 copy-done.2
  22.4 0.2 shard_map.137
  22.7 0.1 pad_add_fusion.bits_ref
  22.7 21.9 %all-to-all-done.xg_ref = bf16[128,2,1280]{2,1,0:T(2,128)(2,1)S(1)} async-done(((bf16[128,2,1280]{2,1,0:T(2,128)(2,1)}), bf16[128,2,1280]{2,1,0:T(2,128)(2,1)S(1)}, u32[]{:S(2)}, u32[]{:S(2)}) %all-to-all-start) | async-done | bytes 655392 | tf_op jit(solution)/shard_map/all_to_all | solution.py:298
  44.7 6.1 %shard_map.138 = (bf16[4,128,768]{2,1,0:T(8,128)(2,1)}, bf16[320,1280]{1,0:T(8,128)(2,1)}, bf16[256,1280]{1,0:T(8,128)(2,1)S(1)}, bf16[640,128]{1,0:T(8,128)(2,1)S(1)}, f32[128,1152]{1,0:T(8,128)S(1)}) custom-call(s32[4]{0:T(128)S(1)} %pad_add_fusion.bits_ref, bf16[128,2,1280]{2,1,0:T(2,128)(2,1)S(1)} %all-to-all-done.xg_ref, ...), custom_call_target="tpu_custom_call" | custom-call | tf_op jit(solution)/shard_map/pallas_call | solution.py:40
  50.7 3.8 %collective-permute-start = (bf16[320,1280]{1,0:T(8,128)(2,1)}, bf16[320,1280]{1,0:T(8,128)(2,1)S(1)}, u32[]{:S(2)}, u32[]{:S(2)}) collective-permute-start(bf16[320,1280]{1,0:T(8,128)(2,1)} %get-tuple-element.31), channel_id=1, source_target_pairs={{0,4},{4,0},{8,12},{12,8},{16,20},{20,16},{24,28},{28,24},{32,36},... | collective-permute-start | bytes 2457608 | tf_op jit(solution)/shard_map/ppermute | solution.py:289
  54.5 4.0 %all-to-all-start.1 = ((bf16[4,128,768]{2,1,0:T(8,128)(2,1)}), bf16[4,128,768]{2,1,0:T(8,128)(2,1)S(1)}, u32[]{:S(2)}, u32[]{:S(2)}) async-start(bf16[4,128,768]{2,1,0:T(8,128)(2,1)} %get-tuple-element.27), calls=%async_computation.1 | async-start | bytes 1572864 | tf_op jit(solution)/shard_map/all_to_all | solution.py:314
  58.6 0.0 collective-permute-done.got_ref
  58.6 1.5 %shard_map.139 = (bf16[80,1280]{1,0:T(8,128)(2,1)}, bf16[80,1280]{1,0:T(8,128)(2,1)}) custom-call(s32[4]{0:T(128)S(1)} %pad_add_fusion.bits_ref, bf16[256,1280]{1,0:T(8,128)(2,1)S(1)} %get-tuple-element.29.ng_ref, bf16[640,128]{1,0:T(8,128)(2,1)S(1)} %get-tuple-element.30.heads_ref, bf16[320,1280]{1,0:T(8,128)(2,1)S(1)} %collective-permute-done.got_ref), custom_call_target="tpu_custom_call" | custom-call | tf_op jit(solution)/shard_map/pallas_call | solution.py:40
  60.1 2.0 %collective-permute-start.1 = (bf16[80,1280]{1,0:T(8,128)(2,1)}, bf16[80,1280]{1,0:T(8,128)(2,1)S(1)}, u32[]{:S(2)}, u32[]{:S(2)}) collective-permute-start(bf16[80,1280]{1,0:T(8,128)(2,1)} %get-tuple-element.32), channel_id=1, source_target_pairs={{0,8},{4,12},{8,0},{12,4},{16,24},{20,28},{24,16},{28,20},{32,40},... | collective-permute-start | bytes 614408 | tf_op jit(solution)/shard_map/ppermute | solution.py:289
  62.1 2.7 %collective-permute-start.2 = (bf16[80,1280]{1,0:T(8,128)(2,1)}, bf16[80,1280]{1,0:T(8,128)(2,1)S(1)}, u32[]{:S(2)}, u32[]{:S(2)}) collective-permute-start(bf16[80,1280]{1,0:T(8,128)(2,1)} %get-tuple-element.33), channel_id=1, source_target_pairs={{0,64},{4,68},{8,72},{12,76},{16,80},{20,84},{24,88},{28,92},{32,9... | collective-permute-start | bytes 614408 | tf_op jit(solution)/shard_map/ppermute | solution.py:289
  64.8 5.9 %all-to-all-done.1.pn_ref = bf16[4,128,768]{2,1,0:T(8,128)(2,1)S(1)} async-done(((bf16[4,128,768]{2,1,0:T(8,128)(2,1)}), bf16[4,128,768]{2,1,0:T(8,128)(2,1)S(1)}, u32[]{:S(2)}, u32[]{:S(2)}) %all-to-all-start.1) | async-done | bytes 786464 | tf_op jit(solution)/shard_map/all_to_all | solution.py:314
  70.7 0.0 collective-permute-done.1.gz_ref
  70.7 0.0 collective-permute-done.2.gy_ref
  70.7 0.0 copy-start.1
  70.7 1.8 %shard_map.140 = bf16[128,2,1152]{2,1,0:T(2,128)(2,1)S(1)} custom-call(s32[4]{0:T(128)S(1)} %pad_add_fusion.bits_ref, bf16[4,128,768]{2,1,0:T(8,128)(2,1)S(1)} %all-to-all-done.1.pn_ref, f32[128,1152]{1,0:T(8,128)S(1)} %get-tuple-element.28.aux_ref, bf16[256,1280]{1,0:T(8,128)(2,1)S(1)} %get-tuple-element.29.ng_ref, ...), custom_call_target="tpu_custom_call" | custom-call | tf_op jit(solution)/shard_map/pallas_call | solution.py:40
  72.5 27.4 %all_to_all.15.b_ref = bf16[128,2,1152]{2,1,0:T(2,128)(2,1)S(1)} all-to-all(bf16[128,2,1152]{2,1,0:T(2,128)(2,1)S(1)} %shard_map.140), channel_id=1, replica_groups=mesh['dp'=128,'zero'=4] {'dp'}, dimensions={0} | all-to-all | bytes 1179648 | tf_op jit(solution)/shard_map/all_to_all | solution.py:332
  99.9 0.0 copy-done.1
  99.9 1.1 %shard_map.141 = (bf16[320,128]{1,0:T(8,128)(2,1)}, bf16[320,128]{1,0:T(8,128)(2,1)}, f32[10,3,2,80]{3,2,1,0:T(2,128)}, f32[10,2,80]{2,1,0:T(2,128)}, f32[1,10]{1,0:T(1,128)}, /*index=5*/f32[1,10]{1,0:T(1,128)}) custom-call(s32[1,128]{1,0:T(1,128)S(1)} %copy-done.1, bf16[128,2,1152]{2,1,0:T(2,128)(2,1)S(1)} %all_to_all.15.b_ref), custom_call_target="tpu_custom_call" | custom-call | tf_op jit(solution)/shard_map/pallas_call | solution.py:40
  (2 shorter events, 0.0 us)
Async XLA Ops:
  0.6 21.7 %copy-start.4 = (f32[1280]{0:T(1024)S(1)}, f32[1280]{0:T(1024)}, u32[]{:S(2)}) copy-start(f32[1280]{0:T(1024)} %param.14) | copy-start | bytes 15364
  0.6 21.7 %copy-start.5 = (f32[1280]{0:T(1024)S(1)}, f32[1280]{0:T(1024)}, u32[]{:S(2)}) copy-start(f32[1280]{0:T(1024)} %param.15) | copy-start | bytes 15364
  0.7 21.7 %copy-start = (bf16[2,80,1280]{2,1,0:T(8,128)(2,1)S(1)}, bf16[2,80,1280]{2,1,0:T(8,128)(2,1)}, u32[]{:S(2)}) copy-start(bf16[2,80,1280]{2,1,0:T(8,128)(2,1)} %param.17) | copy-start | bytes 1228804
  0.7 21.7 %copy-start.3 = (s32[1,128]{1,0:T(1,128)S(1)}, s32[1,128]{1,0:T(1,128)}, u32[]{:S(2)}) copy-start(s32[1,128]{1,0:T(1,128)} %seg_ref.1) | copy-start | bytes 1540
  0.7 21.7 %copy-start.2 = (s32[1,128]{1,0:T(1,128)S(1)}, s32[1,128]{1,0:T(1,128)}, u32[]{:S(2)}) copy-start(s32[1,128]{1,0:T(1,128)} %recv_ref.1) | copy-start | bytes 1540
  3.9 40.8 %all-to-all-start = ((bf16[128,2,1280]{2,1,0:T(2,128)(2,1)}), bf16[128,2,1280]{2,1,0:T(2,128)(2,1)S(1)}, u32[]{:S(2)}, u32[]{:S(2)}) async-start(bf16[128,2,1280]{2,1,0:T(2,128)(2,1)} %shard_map.136), calls=%async_computation | async-start | bytes 1310720 | tf_op jit(solution)/shard_map/all_to_all | solution.py:298
  50.7 7.8 %collective-permute-start = (bf16[320,1280]{1,0:T(8,128)(2,1)}, bf16[320,1280]{1,0:T(8,128)(2,1)S(1)}, u32[]{:S(2)}, u32[]{:S(2)}) collective-permute-start(bf16[320,1280]{1,0:T(8,128)(2,1)} %get-tuple-element.31), channel_id=1, source_target_pairs={{0,4},{4,0},{8,12},{12,8},{16,20},{20,16},{24,28},{28,24},{32,36},... | collective-permute-start | bytes 2457608 | tf_op jit(solution)/shard_map/ppermute | solution.py:289
  54.5 16.1 %all-to-all-start.1 = ((bf16[4,128,768]{2,1,0:T(8,128)(2,1)}), bf16[4,128,768]{2,1,0:T(8,128)(2,1)S(1)}, u32[]{:S(2)}, u32[]{:S(2)}) async-start(bf16[4,128,768]{2,1,0:T(8,128)(2,1)} %get-tuple-element.27), calls=%async_computation.1 | async-start | bytes 1572864 | tf_op jit(solution)/shard_map/all_to_all | solution.py:314
  60.1 10.6 %collective-permute-start.1 = (bf16[80,1280]{1,0:T(8,128)(2,1)}, bf16[80,1280]{1,0:T(8,128)(2,1)S(1)}, u32[]{:S(2)}, u32[]{:S(2)}) collective-permute-start(bf16[80,1280]{1,0:T(8,128)(2,1)} %get-tuple-element.32), channel_id=1, source_target_pairs={{0,8},{4,12},{8,0},{12,4},{16,24},{20,28},{24,16},{28,20},{32,40},... | collective-permute-start | bytes 614408 | tf_op jit(solution)/shard_map/ppermute | solution.py:289
  62.1 8.6 %collective-permute-start.2 = (bf16[80,1280]{1,0:T(8,128)(2,1)}, bf16[80,1280]{1,0:T(8,128)(2,1)S(1)}, u32[]{:S(2)}, u32[]{:S(2)}) collective-permute-start(bf16[80,1280]{1,0:T(8,128)(2,1)} %get-tuple-element.33), channel_id=1, source_target_pairs={{0,64},{4,68},{8,72},{12,76},{16,80},{20,84},{24,88},{28,92},{32,9... | collective-permute-start | bytes 614408 | tf_op jit(solution)/shard_map/ppermute | solution.py:289
  70.7 29.2 %copy-start.1 = (s32[1,128]{1,0:T(1,128)S(1)}, s32[1,128]{1,0:T(1,128)}, u32[]{:S(2)}) copy-start(s32[1,128]{1,0:T(1,128)} %send_ref.3) | copy-start | bytes 1540

commit v5 on v4

--- a/solution.py
+++ b/solution.py
@@ -19,10 +19,11 @@
 GAIN_AT = 64
 BIAS_AT = 74
 MEAN_AT = 84
-WG = 1664
+WG = 896
 HALF = (WG + 2 * QW) // 2
 
 MIB = 1024 * 1024
+GATHER_PARTS = 2
 MIB_HOLD, MIB_BLOCK, MIB_PAIR, MIB_POST = 16, 50, 50, 50
 
 
@@ -30,28 +31,31 @@
     return lax.dot_general(a, b, (((ca,), (cb,)), ((), ())), preferred_element_type=F32)
 
 
-def call(body, outs, *args, smem=(), hbm=(), scratch=(), mib=50):
+def call(body, outs, *args, smem=(), hbm=(), out_hbm=(), scratch=(), mib=50):
     def space(i):
         return pltpu.SMEM if i in smem else pltpu.HBM if i in hbm else pltpu.VMEM
 
     scratch = list(scratch) + [pltpu.VMEM(args[i].shape, args[i].dtype) for i in hbm]
-    if hbm:
-        scratch.append(pltpu.SemaphoreType.DMA((len(hbm),)))
+    scratch += [pltpu.VMEM(*outs[i]) for i in out_hbm]
+    if hbm or out_hbm:
+        scratch.append(pltpu.SemaphoreType.DMA((8,)))
     return pl.pallas_call(
         body,
         out_shape=tuple(jax.ShapeDtypeStruct(s, d) for s, d in outs),
         in_specs=[pl.BlockSpec(memory_space=space(i)) for i in range(len(args))],
-        out_specs=tuple(pl.BlockSpec(memory_space=pltpu.VMEM) for _ in outs),
+        out_specs=tuple(
+            pl.BlockSpec(memory_space=pltpu.HBM if i in out_hbm else pltpu.VMEM)
+            for i in range(len(outs))
+        ),
         scratch_shapes=scratch,
         compiler_params=pltpu.CompilerParams(vmem_limit_bytes=mib * MIB),
     )(*args)
 
 
-def fetch(sems, *pairs):
-    copies = [pltpu.make_async_copy(a, b, sems.at[i]) for i, (a, b) in enumerate(pairs)]
-    for copy in copies:
-        copy.start()
-    return copies
+def start(sem, a, b):
+    copy = pltpu.make_async_copy(a, b, sem)
+    copy.start()
+    return copy
 
 
 def lane(shape):
@@ -75,14 +79,21 @@
     return one_hot(hit & (odd == 0)), one_hot(hit & (odd == 1))
 
 
-def gather_body(send_ref, x_ref, g_ref, o_ref, x_buf, g_buf, sems):
-    copies = fetch(sems, (x_ref, x_buf), (g_ref, g_buf))
+def gather_body(send_ref, x_hbm, g_hbm, o_hbm, x_ref, g_ref, o_ref, sems):
+    copies = [start(sems.at[0], x_hbm, x_ref), start(sems.at[1], g_hbm, g_ref)]
     even, odd = pair_picks(send_ref)
-    copies[0].wait()
-    rows = dg(even, x_buf[...], 0, 0)
-    copies[1].wait()
-    rows = rows + dg(odd, g_buf[...], 0, 0)
-    o_ref[...] = rows.astype(BF).reshape(R, 2, D)
+    for copy in copies:
+        copy.wait()
+    copies = []
+    step = R // GATHER_PARTS
+    for i in range(GATHER_PARTS):
+        rows = slice(2 * step * i, 2 * step * (i + 1))
+        part = dg(even[:, rows], x_ref[...], 0, 0) + dg(odd[:, rows], g_ref[...], 0, 0)
+        at = pl.ds(step * i, step)
+        o_ref[at] = part.astype(BF).reshape(step, 2, D)
+        copies.append(start(sems.at[2 + i], o_ref.at[at], o_hbm.at[at]))
+    for copy in copies:
+        copy.wait()
 
 
 def norm_stats(x):
@@ -106,10 +117,10 @@
 
 def block_body(
     bits_ref, xg_ref, same_ref, gain_ref, bias_ref, wo_ref, wq_hbm,
-    pn_ref, send_ref, ng_ref, heads_ref, aux_ref,
-    wq_ref, sems,
+    pn_hbm, send_hbm, ng_ref, heads_ref, aux_ref,
+    wq_ref, pn_ref, send_ref, sems,
 ):
-    copies = fetch(sems, (wq_hbm, wq_ref))
+    copies = [start(sems.at[0], wq_hbm, wq_ref)]
     xg = xg_ref[...].reshape(2 * R, D)
     at = lane((R, 2 * R)) - 2 * sub((R, 2 * R))
     x = dg(one_hot(at == 0), xg, 1, 0)
@@ -161,6 +172,7 @@
     b = heads_ref[pl.ds(pl.multiple_of(other + 3 * HD, HD), HD), :]
     send_ref[: 3 * HD, :] = dg(a, normed, 1, 0).astype(BF)
     send_ref[3 * HD :, :] = dg(b, g, 1, 0).astype(BF)
+    copies[0] = start(sems.at[1], send_ref, send_hbm)
     p = dg(ho, wo_ref[...], 0, 0)
     n = dg(qg, wq_ref[...], 0, 0)
     u = n * gain_ref[...]
@@ -188,6 +200,9 @@
         pn_ref[i, :, :QP] = part.astype(BF)
         part = jnp.concatenate([n[:, i * QW : (i + 1) * QW], extra[:, 64:]], axis=1)
         pn_ref[i, :, QP:] = part.astype(BF)
+        copies.append(start(sems.at[2 + i], pn_ref.at[i], pn_hbm.at[i]))
+    for copy in copies:
+        copy.wait()
 
 
 def own_rows(c, first, choose_out, ng_ref, heads_ref):
@@ -212,18 +227,26 @@
     sy_ref[...] = (b + part_rows(got_ref, 3 - y)).astype(BF)
 
 
-def post_body(
-    bits_ref, pn_ref, aux_ref, ng_ref, heads_ref, got_ref, gz_ref, gy_ref, o_ref, wz_ref, wy_ref
+def second_body(
+    bits_ref, ng_ref, heads_ref, got_ref, gz_ref, gy_ref, keep_ref, sy_ref, sz_ref
 ):
     c, z, y = bits_ref[0], bits_ref[1], bits_ref[2]
     wz = own_rows(c, z, None, ng_ref, heads_ref) + part_rows(got_ref, z)
-    wz_ref[:, :HD] = (wz + gz_ref[...].astype(F32)).T
+    wz = wz + gz_ref[...].astype(F32)
     wy = own_rows(c, 2, y, ng_ref, heads_ref) + part_rows(got_ref, 2 + y)
-    wy_ref[:, :HD] = (wy + gy_ref[...].astype(F32)).T
-    slabs = []
-    for i in range(10):
-        for ref in (wz_ref, wy_ref):
-            slabs.append(ref[pl.ds(i, R, stride=10), :][:, :HD])
+    wy = wy + gy_ref[...].astype(F32)
+    low, high = slice(0, HD // 2), slice(HD // 2, HD)
+    keep_ref[low] = jnp.where(y == 0, wz[low], wz[high])
+    keep_ref[high] = jnp.where(z == 0, wy[low], wy[high])
+    sy_ref[...] = jnp.where(y == 0, wz[high], wz[low]).astype(BF)
+    sz_ref[...] = jnp.where(z == 0, wy[high], wy[low]).astype(BF)
+
+
+def post_body(pn_ref, aux_ref, keep_ref, gy_ref, gz_ref, o_ref, w_ref):
+    got = jnp.concatenate([gy_ref[...].astype(F32), gz_ref[...].astype(F32)], axis=0)
+    w_ref[:, :HD] = (keep_ref[...] + got).T
+    slabs = [w_ref[pl.ds(i, R, stride=10), :][:, :HD] for i in range(10)]
+    slabs.append(jnp.zeros((R, WG - 64 - 10 * HD), F32))
     pn = jnp.sum(pn_ref[...].astype(F32), axis=0)
     ps = pn[:, :QW]
     ns = pn[:, QP : QP + QW]
@@ -253,11 +276,8 @@
     i_ref[...] = rows[QW:]
     row = sub((16, 2 * R))
     src = lane((16, 2 * R)) // 2
-    half = (row // 2) % 2
-    c_ok = src % 2 == row % 2
-    z_ok = (src // 2) % 2 == half
-    y_ok = (src // 16) % 2 == half
-    mask = ((row < 4) & c_ok & z_ok) | ((row >= 4) & (row < 8) & c_ok & y_ok) | (row == 8)
+    bits = ((src // 2) % 2) * 4 + ((src // 16) % 2) * 2 + src % 2
+    mask = (row == bits) | (row == 8)
     first = lane((16, 2 * R)) % 2 == 0
     sums = jnp.concatenate(
         [
@@ -267,11 +287,12 @@
         axis=1,
     )
     for i in range(10):
-        at = i * 2 * HD
-        a_ref[i, 0] = sums[0:2, at : at + HD]
-        a_ref[i, 1] = sums[2:4, at : at + HD]
-        a_ref[i, 2] = sums[4:6, at + HD : at + 2 * HD]
-        w_ref[i] = sums[6:8, at + HD : at + 2 * HD]
+        a = sums[:, i * HD : i * HD + HD // 2]
+        b = sums[:, i * HD + HD // 2 : (i + 1) * HD]
+        a_ref[i, 0] = jnp.concatenate([a[0:2], a[2:4]], axis=1)
+        a_ref[i, 1] = jnp.concatenate([a[4:6], a[6:8]], axis=1)
+        a_ref[i, 2] = jnp.concatenate([b[0:2], b[4:6]], axis=1)
+        w_ref[i] = jnp.concatenate([b[2:4], b[6:8]], axis=1)
     gain_ref[...] = sums[8:9, WG - 64 : WG - 54]
     bias_ref[...] = sums[8:9, WG - 54 : WG - 44]
 
@@ -288,7 +309,7 @@
     def swap(a, bit):
         return lax.ppermute(a, "dp", [(i, i ^ bit) for i in range(128)])
 
-    (xg,) = call(gather_body, [((R, 2, D), BF)], send_order, patches, cotangent, hbm=(1, 2), mib=58)
+    (xg,) = call(gather_body, [((R, 2, D), BF)], send_order, patches, cotangent, hbm=(1, 2), out_hbm=(0,), mib=58)
     same, gain, bias, wo = call(
         hold_body,
         [((R, R), F32), ((1, D), F32), ((1, D), F32), ((NO, D), BF)],
@@ -308,6 +329,7 @@
         bits, xg, same, gain, bias, wo, wq,
         smem=(0,),
         hbm=(6,),
+        out_hbm=(0, 1),
         mib=MIB_BLOCK,
     )
     got = swap(send, 1)
@@ -321,12 +343,18 @@
     )
     gz = swap(sz, 2)
     gy = swap(sy, 16)
+    keep, sy, sz = call(
+        second_body,
+        [((HD, D), F32), ((HD // 2, D), BF), ((HD // 2, D), BF)],
+        bits, ng, heads, got, gz, gy,
+        smem=(0,),
+        mib=MIB_PAIR,
+    )
     (back,) = call(
         post_body,
         [((R, 2, HALF), BF)],
-        bits, pn, aux, ng, heads, got, gz, gy,
-        smem=(0,),
-        scratch=[pltpu.VMEM((D, R), F32)] * 2,
+        pn, aux, keep, swap(sy, 16), swap(sz, 2),
+        scratch=[pltpu.VMEM((D, R), F32)],
         mib=MIB_POST,
     )
     back = lax.all_to_all(back, "dp", 0, 0, tiled=True)

time: 102 us -> 107 us (1.049)
  starting transfers between devices: 31 us -> 36.8 us
  blocking collectives: 27.4 us -> 25.4 us
  waiting for transfers between devices: 27.8 us -> 29.5 us
    ppermute x3 -> x5, waiting for transfers between devices: 0.01 us -> 7.55 us  [swap(): return lax.ppermute(a, 'dp', [(i, i ^ bit) for i in range(128)])]
    all_to_all x1, waiting for transfers between devices: 5.86 us -> 0.01 us  [local(): pn = lax.all_to_all(pn, 'zero', 0, 0, tiled=True)]
    ppermute x3 -> x5, starting transfers between devices: 8.51 us -> 14.3 us  [swap(): return lax.ppermute(a, 'dp', [(i, i ^ bit) for i in range(128)])]
    all_to_all x1, blocking collectives: 27.4 us -> 25.4 us  [local(): back = lax.all_to_all(back, 'dp', 0, 0, tiled=True)]
    pallas_call x6 -> x7, Pallas kernels: 14 us -> 13.6 us  [call(): pl.pallas_call(body, out_shape=tuple((jax.ShapeDtypeStruct(s, d) for s, d...]
  transfers between devices with their start and end apart: 5 -> 7, of which waited for: 2 -> 4; matrix products, arithmetic and copies ran while one was open for 0% -> 0% of each run, Pallas kernels for 2% -> 2%
where the time goes in v5:
time: 107 us; the launch traced here: 106 us
  starting transfers between devices  36.8 us (34%)
  waiting for transfers between devices  29.5 us (28%)
  blocking collectives  25.4 us (24%)
  Pallas kernels  13.6 us (13%)
    all_to_all x1, blocking collectives, local(): back = lax.all_to_all(back, 'dp', 0, 0, tiled=True)  25.4 us
    all_to_all x1, waiting for transfers between devices, local(): xg = lax.all_to_all(xg, 'dp', 0, 0, tiled=True)  21.9 us
    all_to_all x1, starting transfers between devices, local(): xg = lax.all_to_all(xg, 'dp', 0, 0, tiled=True)  18.4 us
    ppermute x5, starting transfers between devices, swap(): return lax.ppermute(a, 'dp', [(i, i ^ bit) for i in range(128)])  14.3 us
    pallas_call x7, Pallas kernels, call(): pl.pallas_call(body, out_shape=tuple((jax.ShapeDtypeStruct(s, d) for s, d...  13.6 us
    ppermute x5, waiting for transfers between devices, swap(): return lax.ppermute(a, 'dp', [(i, i ^ bit) for i in range(128)])  7.55 us
    all_to_all x1, starting transfers between devices, local(): pn = lax.all_to_all(pn, 'zero', 0, 0, tiled=True)  4.03 us
  transfers between devices with their start and end apart: 7, of which 4 were waited for; matrix products, arithmetic and copies ran while one was open for 0% of the time, Pallas kernels for 2%

profile of v5, /device:TPU:1, one launch (start us, length us, event | category | flops | bytes accessed | tf_op | source)
XLA Modules:
  0.0 106.2 jit_solution(10286113616052778361)
XLA Ops:
  0.6 0.0 copy-start.4
  0.6 0.0 copy-start.5
  0.7 0.0 copy-start
  0.7 0.0 copy-start.3
  0.7 0.0 copy-start.2
  0.7 3.1 %shard_map.136 = bf16[128,2,1280]{2,1,0:T(2,128)(2,1)} custom-call(s32[1,128]{1,0:T(1,128)} %send_ref.3, bf16[128,1280]{1,0:T(8,128)(2,1)} %x_hbm.1, bf16[128,1280]{1,0:T(8,128)(2,1)} %g_hbm.1), custom_call_target="tpu_custom_call" | custom-call | tf_op jit(solution)/shard_map/pallas_call | solution.py:42
  3.8 18.4 %all-to-all-start = ((bf16[128,2,1280]{2,1,0:T(2,128)(2,1)}), bf16[128,2,1280]{2,1,0:T(2,128)(2,1)S(1)}, u32[]{:S(2)}, u32[]{:S(2)}) async-start(bf16[128,2,1280]{2,1,0:T(2,128)(2,1)} %shard_map.136), calls=%async_computation | async-start | bytes 1310720 | tf_op jit(solution)/shard_map/all_to_all | solution.py:319
  22.3 0.0 copy-done.4
  22.3 0.0 copy-done.5
  22.3 0.0 copy-done
  22.3 0.0 copy-done.3
  22.3 0.0 copy-done.2
  22.3 0.2 shard_map.137
  22.6 0.1 pad_add_fusion.bits_ref
  22.6 21.9 %all-to-all-done.xg_ref = bf16[128,2,1280]{2,1,0:T(2,128)(2,1)S(1)} async-done(((bf16[128,2,1280]{2,1,0:T(2,128)(2,1)}), bf16[128,2,1280]{2,1,0:T(2,128)(2,1)S(1)}, u32[]{:S(2)}, u32[]{:S(2)}) %all-to-all-start) | async-done | bytes 655392 | tf_op jit(solution)/shard_map/all_to_all | solution.py:319
  44.6 6.1 %shard_map.138 = (bf16[4,128,768]{2,1,0:T(8,128)(2,1)}, bf16[320,1280]{1,0:T(8,128)(2,1)}, bf16[256,1280]{1,0:T(8,128)(2,1)S(1)}, bf16[640,128]{1,0:T(8,128)(2,1)S(1)}, f32[128,1152]{1,0:T(8,128)S(1)}) custom-call(s32[4]{0:T(128)S(1)} %pad_add_fusion.bits_ref, bf16[128,2,1280]{2,1,0:T(2,128)(2,1)S(1)} %all-to-all-done.xg_ref, ...), custom_call_target="tpu_custom_call" | custom-call | tf_op jit(solution)/shard_map/pallas_call | solution.py:42
  50.7 3.8 %collective-permute-start = (bf16[320,1280]{1,0:T(8,128)(2,1)}, bf16[320,1280]{1,0:T(8,128)(2,1)S(1)}, u32[]{:S(2)}, u32[]{:S(2)}) collective-permute-start(bf16[320,1280]{1,0:T(8,128)(2,1)} %get-tuple-element.34), channel_id=1, source_target_pairs={{0,4},{4,0},{8,12},{12,8},{16,20},{20,16},{24,28},{28,24},{32,36},... | collective-permute-start | bytes 2457608 | tf_op jit(solution)/shard_map/ppermute | solution.py:310
  54.5 4.0 %all-to-all-start.1 = ((bf16[4,128,768]{2,1,0:T(8,128)(2,1)}), bf16[4,128,768]{2,1,0:T(8,128)(2,1)S(1)}, u32[]{:S(2)}, u32[]{:S(2)}) async-start(bf16[4,128,768]{2,1,0:T(8,128)(2,1)} %get-tuple-element.30), calls=%async_computation.1 | async-start | bytes 1572864 | tf_op jit(solution)/shard_map/all_to_all | solution.py:336
  58.5 0.0 collective-permute-done.got_ref
  58.5 0.8 shard_map.139
  59.3 2.0 %collective-permute-start.1 = (bf16[80,1280]{1,0:T(8,128)(2,1)S(1)}, bf16[80,1280]{1,0:T(8,128)(2,1)S(1)}, u32[]{:S(2)}, u32[]{:S(2)}) collective-permute-start(bf16[80,1280]{1,0:T(8,128)(2,1)S(1)} %get-tuple-element.35), channel_id=1, source_target_pairs={{0,8},{4,12},{8,0},{12,4},{16,24},{20,28},{24,16},{28,20},{32,40},... | collective-permute-start | bytes 614408 | tf_op jit(solution)/shard_map/ppermute | solution.py:310
  61.4 2.7 %collective-permute-start.2 = (bf16[80,1280]{1,0:T(8,128)(2,1)S(1)}, bf16[80,1280]{1,0:T(8,128)(2,1)S(1)}, u32[]{:S(2)}, u32[]{:S(2)}) collective-permute-start(bf16[80,1280]{1,0:T(8,128)(2,1)S(1)} %get-tuple-element.36), channel_id=1, source_target_pairs={{0,64},{4,68},{8,72},{12,76},{16,80},{20,84},{24,88},{28,92},{32,9... | collective-permute-start | bytes 614408 | tf_op jit(solution)/shard_map/ppermute | solution.py:310
  64.1 3.5 %collective-permute-done.1.gz_ref = bf16[80,1280]{1,0:T(8,128)(2,1)S(1)} collective-permute-done((bf16[80,1280]{1,0:T(8,128)(2,1)S(1)}, bf16[80,1280]{1,0:T(8,128)(2,1)S(1)}, u32[]{:S(2)}, u32[]{:S(2)}) %collective-permute-start.1) | collective-permute-done | bytes 204832 | tf_op jit(solution)/shard_map/ppermute | solution.py:310
  67.6 1.7 %collective-permute-done.2.gy_ref = bf16[80,1280]{1,0:T(8,128)(2,1)S(1)} collective-permute-done((bf16[80,1280]{1,0:T(8,128)(2,1)S(1)}, bf16[80,1280]{1,0:T(8,128)(2,1)S(1)}, u32[]{:S(2)}, u32[]{:S(2)}) %collective-permute-start.2) | collective-permute-done | bytes 204832 | tf_op jit(solution)/shard_map/ppermute | solution.py:310
  69.3 1.4 %shard_map.140 = (f32[80,1280]{1,0:T(8,128)S(1)}, bf16[40,1280]{1,0:T(8,128)(2,1)}, bf16[40,1280]{1,0:T(8,128)(2,1)S(1)}) custom-call(s32[4]{0:T(128)S(1)} %pad_add_fusion.bits_ref, bf16[256,1280]{1,0:T(8,128)(2,1)S(1)} %get-tuple-element.32.ng_ref, bf16[640,128]{1,0:T(8,128)(2,1)S(1)} %get-tuple-element.33.heads_ref, ...), custom_call_target="tpu_custom_call" | custom-call | tf_op jit(solution)/shard_map/pallas_call | solution.py:42
  70.8 2.7 %collective-permute-start.3 = (bf16[40,1280]{1,0:T(8,128)(2,1)}, bf16[40,1280]{1,0:T(8,128)(2,1)S(1)}, u32[]{:S(2)}, u32[]{:S(2)}) collective-permute-start(bf16[40,1280]{1,0:T(8,128)(2,1)} %get-tuple-element.38), channel_id=1, source_target_pairs={{0,64},{4,68},{8,72},{12,76},{16,80},{20,84},{24,88},{28,92},{32,9... | collective-permute-start | bytes 307208 | tf_op jit(solution)/shard_map/ppermute | solution.py:310
  73.5 3.1 %collective-permute-start.4 = (bf16[40,1280]{1,0:T(8,128)(2,1)S(1)}, bf16[40,1280]{1,0:T(8,128)(2,1)S(1)}, u32[]{:S(2)}, u32[]{:S(2)}) collective-permute-start(bf16[40,1280]{1,0:T(8,128)(2,1)S(1)} %get-tuple-element.39), channel_id=1, source_target_pairs={{0,8},{4,12},{8,0},{12,4},{16,24},{20,28},{24,16},{28,20},{32,40},... | collective-permute-start | bytes 307208 | tf_op jit(solution)/shard_map/ppermute | solution.py:310
  76.5 0.0 all-to-all-done.1.pn_ref
  76.6 0.0 collective-permute-done.3.gy_ref
  76.6 2.3 %collective-permute-done.4.gz_ref = bf16[40,1280]{1,0:T(8,128)(2,1)S(1)} collective-permute-done((bf16[40,1280]{1,0:T(8,128)(2,1)S(1)}, bf16[40,1280]{1,0:T(8,128)(2,1)S(1)}, u32[]{:S(2)}, u32[]{:S(2)}) %collective-permute-start.4) | collective-permute-done | bytes 102432 | tf_op jit(solution)/shard_map/ppermute | solution.py:310
  78.9 0.0 copy-start.1
  78.9 0.8 shard_map.141
  79.7 25.4 %all_to_all.15.b_ref = bf16[128,2,768]{2,1,0:T(2,128)(2,1)S(1)} all-to-all(bf16[128,2,768]{2,1,0:T(2,128)(2,1)S(1)} %shard_map.141), channel_id=1, replica_groups=mesh['dp'=128,'zero'=4] {'dp'}, dimensions={0} | all-to-all | bytes 786432 | tf_op jit(solution)/shard_map/all_to_all | solution.py:360
  105.0 0.0 copy-done.1
  105.0 1.1 %shard_map.142 = (bf16[320,128]{1,0:T(8,128)(2,1)}, bf16[320,128]{1,0:T(8,128)(2,1)}, f32[10,3,2,80]{3,2,1,0:T(2,128)}, f32[10,2,80]{2,1,0:T(2,128)}, f32[1,10]{1,0:T(1,128)}, /*index=5*/f32[1,10]{1,0:T(1,128)}) custom-call(s32[1,128]{1,0:T(1,128)S(1)} %copy-done.1, bf16[128,2,768]{2,1,0:T(2,128)(2,1)S(1)} %all_to_all.15.b_ref), custom_call_target="tpu_custom_call" | custom-call | tf_op jit(solution)/shard_map/pallas_call | solution.py:42
  (2 shorter events, 0.0 us)
Async XLA Ops:
  0.6 21.6 %copy-start.4 = (f32[1280]{0:T(1024)S(1)}, f32[1280]{0:T(1024)}, u32[]{:S(2)}) copy-start(f32[1280]{0:T(1024)} %param.14) | copy-start | bytes 15364
  0.6 21.6 %copy-start.5 = (f32[1280]{0:T(1024)S(1)}, f32[1280]{0:T(1024)}, u32[]{:S(2)}) copy-start(f32[1280]{0:T(1024)} %param.15) | copy-start | bytes 15364
  0.7 21.7 %copy-start = (bf16[2,80,1280]{2,1,0:T(8,128)(2,1)S(1)}, bf16[2,80,1280]{2,1,0:T(8,128)(2,1)}, u32[]{:S(2)}) copy-start(bf16[2,80,1280]{2,1,0:T(8,128)(2,1)} %param.17) | copy-start | bytes 1228804
  0.7 21.7 %copy-start.3 = (s32[1,128]{1,0:T(1,128)S(1)}, s32[1,128]{1,0:T(1,128)}, u32[]{:S(2)}) copy-start(s32[1,128]{1,0:T(1,128)} %seg_ref.1) | copy-start | bytes 1540
  0.7 21.7 %copy-start.2 = (s32[1,128]{1,0:T(1,128)S(1)}, s32[1,128]{1,0:T(1,128)}, u32[]{:S(2)}) copy-start(s32[1,128]{1,0:T(1,128)} %recv_ref.1) | copy-start | bytes 1540
  3.8 40.8 %all-to-all-start = ((bf16[128,2,1280]{2,1,0:T(2,128)(2,1)}), bf16[128,2,1280]{2,1,0:T(2,128)(2,1)S(1)}, u32[]{:S(2)}, u32[]{:S(2)}) async-start(bf16[128,2,1280]{2,1,0:T(2,128)(2,1)} %shard_map.136), calls=%async_computation | async-start | bytes 1310720 | tf_op jit(solution)/shard_map/all_to_all | solution.py:319
  50.7 7.8 %collective-permute-start = (bf16[320,1280]{1,0:T(8,128)(2,1)}, bf16[320,1280]{1,0:T(8,128)(2,1)S(1)}, u32[]{:S(2)}, u32[]{:S(2)}) collective-permute-start(bf16[320,1280]{1,0:T(8,128)(2,1)} %get-tuple-element.34), channel_id=1, source_target_pairs={{0,4},{4,0},{8,12},{12,8},{16,20},{20,16},{24,28},{28,24},{32,36},... | collective-permute-start | bytes 2457608 | tf_op jit(solution)/shard_map/ppermute | solution.py:310
  54.5 22.1 %all-to-all-start.1 = ((bf16[4,128,768]{2,1,0:T(8,128)(2,1)}), bf16[4,128,768]{2,1,0:T(8,128)(2,1)S(1)}, u32[]{:S(2)}, u32[]{:S(2)}) async-start(bf16[4,128,768]{2,1,0:T(8,128)(2,1)} %get-tuple-element.30), calls=%async_computation.1 | async-start | bytes 1572864 | tf_op jit(solution)/shard_map/all_to_all | solution.py:336
  59.3 8.3 %collective-permute-start.1 = (bf16[80,1280]{1,0:T(8,128)(2,1)S(1)}, bf16[80,1280]{1,0:T(8,128)(2,1)S(1)}, u32[]{:S(2)}, u32[]{:S(2)}) collective-permute-start(bf16[80,1280]{1,0:T(8,128)(2,1)S(1)} %get-tuple-element.35), channel_id=1, source_target_pairs={{0,8},{4,12},{8,0},{12,4},{16,24},{20,28},{24,16},{28,20},{32,40},... | collective-permute-start | bytes 614408 | tf_op jit(solution)/shard_map/ppermute | solution.py:310
  61.4 8.0 %collective-permute-start.2 = (bf16[80,1280]{1,0:T(8,128)(2,1)S(1)}, bf16[80,1280]{1,0:T(8,128)(2,1)S(1)}, u32[]{:S(2)}, u32[]{:S(2)}) collective-permute-start(bf16[80,1280]{1,0:T(8,128)(2,1)S(1)} %get-tuple-element.36), channel_id=1, source_target_pairs={{0,64},{4,68},{8,72},{12,76},{16,80},{20,84},{24,88},{28,92},{32,9... | collective-permute-start | bytes 614408 | tf_op jit(solution)/shard_map/ppermute | solution.py:310
  70.8 5.8 %collective-permute-start.3 = (bf16[40,1280]{1,0:T(8,128)(2,1)}, bf16[40,1280]{1,0:T(8,128)(2,1)S(1)}, u32[]{:S(2)}, u32[]{:S(2)}) collective-permute-start(bf16[40,1280]{1,0:T(8,128)(2,1)} %get-tuple-element.38), channel_id=1, source_target_pairs={{0,64},{4,68},{8,72},{12,76},{16,80},{20,84},{24,88},{28,92},{32,9... | collective-permute-start | bytes 307208 | tf_op jit(solution)/shard_map/ppermute | solution.py:310
  73.5 5.4 %collective-permute-start.4 = (bf16[40,1280]{1,0:T(8,128)(2,1)S(1)}, bf16[40,1280]{1,0:T(8,128)(2,1)S(1)}, u32[]{:S(2)}, u32[]{:S(2)}) collective-permute-start(bf16[40,1280]{1,0:T(8,128)(2,1)S(1)} %get-tuple-element.39), channel_id=1, source_target_pairs={{0,8},{4,12},{8,0},{12,4},{16,24},{20,28},{24,16},{28,20},{32,40},... | collective-permute-start | bytes 307208 | tf_op jit(solution)/shard_map/ppermute | solution.py:310
  78.9 26.2 %copy-start.1 = (s32[1,128]{1,0:T(1,128)S(1)}, s32[1,128]{1,0:T(1,128)}, u32[]{:S(2)}) copy-start(s32[1,128]{1,0:T(1,128)} %send_ref.3) | copy-start | bytes 1540

commit v6 on v5

--- a/solution.py
+++ b/solution.py
@@ -16,10 +16,10 @@
 QP = 384
 F32 = jnp.float32
 BF = jnp.bfloat16
-GAIN_AT = 64
-BIAS_AT = 74
-MEAN_AT = 84
-WG = 896
+PN = 5 * R
+PNE = PN + 32
+STEP = 2 * HD + 2
+WG = 1664
 HALF = (WG + 2 * QW) // 2
 
 MIB = 1024 * 1024
@@ -38,7 +38,7 @@
     scratch = list(scratch) + [pltpu.VMEM(args[i].shape, args[i].dtype) for i in hbm]
     scratch += [pltpu.VMEM(*outs[i]) for i in out_hbm]
     if hbm or out_hbm:
-        scratch.append(pltpu.SemaphoreType.DMA((8,)))
+        scratch.append(pltpu.SemaphoreType.DMA((10,)))
     return pl.pallas_call(
         body,
         out_shape=tuple(jax.ShapeDtypeStruct(s, d) for s, d in outs),
@@ -66,6 +66,11 @@
     return lax.broadcasted_iota(jnp.int32, shape, 0)
 
 
+def place_bits():
+    dp = lax.axis_index("dp")
+    return lax.rem(dp, 2), lax.rem(dp // 2, 2), lax.rem(dp // 16, 2)
+
+
 def one_hot(cond):
     return cond.astype(F32).astype(BF)
 
@@ -79,8 +84,10 @@
     return one_hot(hit & (odd == 0)), one_hot(hit & (odd == 1))
 
 
-def gather_body(send_ref, x_hbm, g_hbm, o_hbm, x_ref, g_ref, o_ref, sems):
+def gather_body(send_hbm, x_hbm, g_hbm, o_hbm, send_ref, x_ref, g_ref, o_ref, sems):
+    first = start(sems.at[7], send_hbm, send_ref)
     copies = [start(sems.at[0], x_hbm, x_ref), start(sems.at[1], g_hbm, g_ref)]
+    first.wait()
     even, odd = pair_picks(send_ref)
     for copy in copies:
         copy.wait()
@@ -116,8 +123,8 @@
 
 
 def block_body(
-    bits_ref, xg_ref, same_ref, gain_ref, bias_ref, wo_ref, wq_hbm,
-    pn_hbm, send_hbm, ng_ref, heads_ref, aux_ref,
+    xg_ref, same_ref, gain_ref, bias_ref, wo_ref, wq_hbm,
+    pn_hbm, send_hbm, ng_ref, heads_ref, stat_ref,
     wq_ref, pn_ref, send_ref, sems,
 ):
     copies = [start(sems.at[0], wq_hbm, wq_ref)]
@@ -132,20 +139,19 @@
     ng_ref[:R, :] = normed
     for i in range(4):
 
-        @pl.when(bits_ref[3] == i)
+        @pl.when(lax.axis_index("zero") == i)
         def _(i=i):
             cols = slice(i * QW, (i + 1) * QW)
-            tail = (R, QP - QW)
-            rows = [
-                x[:, cols], jnp.broadcast_to(mean, tail),
-                g32[:, cols], jnp.broadcast_to(inv, tail),
-                jnp.broadcast_to(gain_ref[:, cols], (R, QW)), jnp.zeros(tail, F32),
-            ]
-            aux_ref[...] = jnp.concatenate(rows, axis=1)
-
-    copies[0].wait()
+            pad = jnp.zeros((R, QP - QW), F32)
+            both = jnp.concatenate([x[:, cols], pad, g32[:, cols], pad], axis=1).astype(BF)
+            for t in range(6):
+                heads_ref[(5 + t) * R : (6 + t) * R] = both[:, t * R : (t + 1) * R]
+            stat_ref[R:, :QW] = jnp.broadcast_to(gain_ref[:, cols], (8, QW))
+
+    stat_ref[:R, :R] = jnp.where(lane((R, R)) < 64, mean, inv)
+    dh = dg(wo_ref[...], g, 1, 1).astype(BF)
+    copies.pop().wait()
     qkv = dg(wq_ref[...], normed, 1, 1).astype(BF)
-    dh = dg(wo_ref[...], g, 1, 1).astype(BF)
     same = same_ref[...] > 0.5
     rows = []
     for h in range(HG):
@@ -164,43 +170,45 @@
         rows.append(dg(q, sg, 1, 0).astype(BF))
         rows.append(dg(dhh, w16, 1, 0).astype(BF))
         rows.append(dg(v, w16, 1, 1).astype(BF))
-    heads_ref[...] = jnp.concatenate(rows, axis=0)
+    heads_ref[: 8 * HD] = jnp.concatenate(rows, axis=0)
     qg = jnp.concatenate(rows[0:3] + rows[4:7], axis=0)
     ho = jnp.concatenate([rows[3], rows[7]], axis=0)
-    other = (1 - bits_ref[0]) * 4 * HD
+    other = (1 - place_bits()[0]) * 4 * HD
     a = heads_ref[pl.ds(pl.multiple_of(other, 4 * HD), 3 * HD), :]
     b = heads_ref[pl.ds(pl.multiple_of(other + 3 * HD, HD), HD), :]
     send_ref[: 3 * HD, :] = dg(a, normed, 1, 0).astype(BF)
     send_ref[3 * HD :, :] = dg(b, g, 1, 0).astype(BF)
-    copies[0] = start(sems.at[1], send_ref, send_hbm)
+    copies.append(start(sems.at[9], send_ref, send_hbm))
     p = dg(ho, wo_ref[...], 0, 0)
+    for i in range(4):
+        for t in range(2):
+            pn_ref[i, t * R : (t + 1) * R] = p[:, i * QW + t * R : i * QW + (t + 1) * R].astype(BF)
+        rows = pl.ds(0, 2 * R)
+        copies.append(start(sems.at[1 + i], pn_ref.at[i, rows], pn_hbm.at[i, rows]))
     n = dg(qg, wq_ref[...], 0, 0)
     u = n * gain_ref[...]
     m1 = jnp.sum(u, axis=1, keepdims=True) * (1.0 / D)
     m2 = jnp.sum(u * xh, axis=1, keepdims=True) * (1.0 / D)
     gain_row = jnp.sum(n * xh, axis=0, keepdims=True)
     bias_row = jnp.sum(n, axis=0, keepdims=True)
-    first = lane((R, D)) - 10 * sub((R, D))
-    sel = (first >= 0) & (first < 10)
-    both = jnp.concatenate(
-        [jnp.where(sel, gain_row, 0.0).astype(BF), jnp.where(sel, bias_row, 0.0).astype(BF)], axis=0
-    )
-    f = sub((D, R)).astype(F32)
-    k = f - 10.0 * jnp.floor((f + 0.5) * 0.1)
-    both = dg(both, one_hot(k == (lane((D, R)) - GAIN_AT).astype(F32)), 1, 0)
-    extra = both[:R] + pltpu.roll(both[R:], BIAS_AT - GAIN_AT, 1)
-    ln = lane((R, R))
-    for j, m in enumerate((m1, m2)):
-        hi = m.astype(BF).astype(F32)
-        extra = jnp.where(ln == MEAN_AT + 2 * j, hi, extra)
-        extra = jnp.where(ln == MEAN_AT + 2 * j + 1, m - hi, extra)
-    pad = jnp.zeros((R, QP - QW), F32)
+    extra = [r[:, t * R : (t + 1) * R] for r in (gain_row, bias_row) for t in range(10)]
+    diagonal = sub((R, R)) == lane((R, R))
+    for m in (m1, m2):
+        row = jnp.sum(jnp.where(diagonal, m, 0.0), axis=0, keepdims=True)
+        high = row.astype(BF).astype(F32)
+        extra += [high, row - high]
+    extra.append(jnp.zeros((8, R), F32))
+    extra = jnp.concatenate(extra, axis=0).astype(BF)
     for i in range(4):
-        part = jnp.concatenate([p[:, i * QW : (i + 1) * QW], pad], axis=1)
-        pn_ref[i, :, :QP] = part.astype(BF)
-        part = jnp.concatenate([n[:, i * QW : (i + 1) * QW], extra[:, 64:]], axis=1)
-        pn_ref[i, :, QP:] = part.astype(BF)
-        copies.append(start(sems.at[2 + i], pn_ref.at[i], pn_hbm.at[i]))
+        at = i * QW
+        mixed = jnp.concatenate([p[:, at + 2 * R : at + QW], n[:, at : at + 64]], axis=1)
+        pn_ref[i, 2 * R : 3 * R] = mixed.astype(BF)
+        for t in range(2):
+            cols = slice(at + 64 + t * R, at + 64 + (t + 1) * R)
+            pn_ref[i, (3 + t) * R : (4 + t) * R] = n[:, cols].astype(BF)
+        pn_ref[i, PN:] = extra
+        rows = pl.ds(2 * R, PNE - 2 * R)
+        copies.append(start(sems.at[5 + i], pn_ref.at[i, rows], pn_hbm.at[i, rows]))
     for copy in copies:
         copy.wait()
 
@@ -219,50 +227,48 @@
     return ref[pl.ds(pl.multiple_of(j * HD, HD), HD), :].astype(F32)
 
 
-def pair_body(bits_ref, ng_ref, heads_ref, got_ref, sz_ref, sy_ref):
-    c, z, y = bits_ref[0], bits_ref[1], bits_ref[2]
+def pair_body(ng_ref, heads_ref, got_ref, sz_ref, sy_ref):
+    c, z, y = place_bits()
     a = own_rows(c, 1 - z, None, ng_ref, heads_ref)
     b = own_rows(c, 2, 1 - y, ng_ref, heads_ref)
     sz_ref[...] = (a + part_rows(got_ref, 1 - z)).astype(BF)
     sy_ref[...] = (b + part_rows(got_ref, 3 - y)).astype(BF)
 
 
-def second_body(
-    bits_ref, ng_ref, heads_ref, got_ref, gz_ref, gy_ref, keep_ref, sy_ref, sz_ref
+def post_body(
+    pn_ref, stat_ref, ng_ref, heads_ref, got_ref, gz_ref, gy_ref, o_ref, wz_ref, wy_ref
 ):
-    c, z, y = bits_ref[0], bits_ref[1], bits_ref[2]
+    c, z, y = place_bits()
+    pn = jnp.sum(pn_ref[:, :PN].astype(F32), axis=0)
+    extra = jnp.sum(pn_ref[:, PN:].astype(F32), axis=0)
+    gain_row = jnp.concatenate([extra[t : t + 1] for t in range(10)], axis=1)
+    bias_row = jnp.concatenate([extra[t : t + 1] for t in range(10, 20)], axis=1)
     wz = own_rows(c, z, None, ng_ref, heads_ref) + part_rows(got_ref, z)
     wz = wz + gz_ref[...].astype(F32)
+    wz = jnp.concatenate([wz, gain_row, bias_row, jnp.zeros((6, D), F32)], axis=0)
+    wz_ref[:, : HD + 8] = wz.T
     wy = own_rows(c, 2, y, ng_ref, heads_ref) + part_rows(got_ref, 2 + y)
-    wy = wy + gy_ref[...].astype(F32)
-    low, high = slice(0, HD // 2), slice(HD // 2, HD)
-    keep_ref[low] = jnp.where(y == 0, wz[low], wz[high])
-    keep_ref[high] = jnp.where(z == 0, wy[low], wy[high])
-    sy_ref[...] = jnp.where(y == 0, wz[high], wz[low]).astype(BF)
-    sz_ref[...] = jnp.where(z == 0, wy[high], wy[low]).astype(BF)
-
-
-def post_body(pn_ref, aux_ref, keep_ref, gy_ref, gz_ref, o_ref, w_ref):
-    got = jnp.concatenate([gy_ref[...].astype(F32), gz_ref[...].astype(F32)], axis=0)
-    w_ref[:, :HD] = (keep_ref[...] + got).T
-    slabs = [w_ref[pl.ds(i, R, stride=10), :][:, :HD] for i in range(10)]
-    slabs.append(jnp.zeros((R, WG - 64 - 10 * HD), F32))
-    pn = jnp.sum(pn_ref[...].astype(F32), axis=0)
-    ps = pn[:, :QW]
-    ns = pn[:, QP : QP + QW]
-    x = aux_ref[:, :QW]
-    mean = aux_ref[:, QW : QW + 1]
-    inv = aux_ref[:, QP + QW : QP + QW + 1]
+    wy_ref[:, :HD] = (wy + gy_ref[...].astype(F32)).T
+    slabs = []
+    for i in range(10):
+        rows = pl.ds(i, R, stride=10)
+        slabs += [wz_ref[rows, :][:, : HD + 2], wy_ref[rows, :][:, :HD]]
+    slabs.append(jnp.zeros((R, WG - 10 * STEP), F32))
+    tiles = [pn[t * R : (t + 1) * R] for t in range(5)]
+    both = jnp.concatenate(tiles, axis=1)
+    diagonal = sub((R, R)) == lane((R, R))
+    m1 = jnp.sum(jnp.where(diagonal, extra[20:21] + extra[21:22], 0.0), axis=1, keepdims=True)
+    m2 = jnp.sum(jnp.where(diagonal, extra[22:23] + extra[23:24], 0.0), axis=1, keepdims=True)
+    quarters = [heads_ref[(5 + t) * R : (6 + t) * R].astype(F32) for t in range(6)]
+    x = jnp.concatenate(quarters[:3], axis=1)[:, :QW]
+    g = jnp.concatenate(quarters[3:], axis=1)[:, :QW]
+    mean = stat_ref[:R, 0:1]
+    inv = stat_ref[:R, 64:65]
     xh = (x - mean) * inv
-    tile = pn[:, QP + 256 :]
-    ln = lane((R, R))
-    m1 = jnp.sum(jnp.where((ln == MEAN_AT) | (ln == MEAN_AT + 1), tile, 0.0), axis=1, keepdims=True)
-    m2 = jnp.sum(
-        jnp.where((ln == MEAN_AT + 2) | (ln == MEAN_AT + 3), tile, 0.0), axis=1, keepdims=True
-    )
-    enc = x + ps
-    grad = aux_ref[:, QP : QP + QW] + inv * (ns * aux_ref[:, 2 * QP : 2 * QP + QW] - m1 - xh * m2)
-    row = jnp.concatenate(slabs + [tile[:, 64:], enc, grad], axis=1).astype(BF)
+    enc = x + both[:, :QW]
+    grad = both[:, QW:] * stat_ref[R : R + 1, :QW] - m1 - xh * m2
+    grad = g + inv * grad
+    row = jnp.concatenate(slabs + [enc, grad], axis=1).astype(BF)
     at = sub((2 * R, R)) - 2 * lane((2 * R, R))
     both = dg(one_hot(at == 0), row[:, :HALF], 1, 0) + dg(one_hot(at == 1), row[:, HALF:], 1, 0)
     o_ref[...] = both.astype(BF).reshape(R, 2, HALF)
@@ -276,8 +282,11 @@
     i_ref[...] = rows[QW:]
     row = sub((16, 2 * R))
     src = lane((16, 2 * R)) // 2
-    bits = ((src // 2) % 2) * 4 + ((src // 16) % 2) * 2 + src % 2
-    mask = (row == bits) | (row == 8)
+    half = (row // 2) % 2
+    c_ok = src % 2 == row % 2
+    z_ok = (src // 2) % 2 == half
+    y_ok = (src // 16) % 2 == half
+    mask = ((row < 4) & c_ok & z_ok) | ((row >= 4) & (row < 8) & c_ok & y_ok) | (row == 8)
     first = lane((16, 2 * R)) % 2 == 0
     sums = jnp.concatenate(
         [
@@ -287,20 +296,16 @@
         axis=1,
     )
     for i in range(10):
-        a = sums[:, i * HD : i * HD + HD // 2]
-        b = sums[:, i * HD + HD // 2 : (i + 1) * HD]
-        a_ref[i, 0] = jnp.concatenate([a[0:2], a[2:4]], axis=1)
-        a_ref[i, 1] = jnp.concatenate([a[4:6], a[6:8]], axis=1)
-        a_ref[i, 2] = jnp.concatenate([b[0:2], b[4:6]], axis=1)
-        w_ref[i] = jnp.concatenate([b[2:4], b[6:8]], axis=1)
-    gain_ref[...] = sums[8:9, WG - 64 : WG - 54]
-    bias_ref[...] = sums[8:9, WG - 54 : WG - 44]
+        at = i * STEP
+        a_ref[i, 0] = sums[0:2, at : at + HD]
+        a_ref[i, 1] = sums[2:4, at : at + HD]
+        gain_ref[:, i : i + 1] = sums[8:9, at + HD : at + HD + 1]
+        bias_ref[:, i : i + 1] = sums[8:9, at + HD + 1 : at + HD + 2]
+        a_ref[i, 2] = sums[4:6, at + HD + 2 : at + STEP]
+        w_ref[i] = sums[6:8, at + HD + 2 : at + STEP]
 
 
 def local(patches, cotangent, send_order, recv_order, segment_ids, ln_gain, ln_bias, w_qkv, w_out):
-    zero = lax.axis_index("zero")
-    dp = lax.axis_index("dp")
-    bits = jnp.stack([dp & 1, (dp >> 1) & 1, (dp >> 4) & 1, zero])
     wq = w_qkv.transpose(1, 2, 3, 0).reshape(NQ, D)
     wo = w_out.reshape(NO, D)
     gain = ln_gain.reshape(1, D)
@@ -309,7 +314,7 @@
     def swap(a, bit):
         return lax.ppermute(a, "dp", [(i, i ^ bit) for i in range(128)])
 
-    (xg,) = call(gather_body, [((R, 2, D), BF)], send_order, patches, cotangent, hbm=(1, 2), out_hbm=(0,), mib=58)
+    (xg,) = call(gather_body, [((R, 2, D), BF)], send_order, patches, cotangent, hbm=(0, 1, 2), out_hbm=(0,), mib=58)
     same, gain, bias, wo = call(
         hold_body,
         [((R, R), F32), ((1, D), F32), ((1, D), F32), ((NO, D), BF)],
@@ -317,18 +322,17 @@
         mib=MIB_HOLD,
     )
     xg = lax.all_to_all(xg, "dp", 0, 0, tiled=True)
-    pn, send, ng, heads, aux = call(
+    pn, send, ng, heads, stat = call(
         block_body,
         [
-            ((4, R, 2 * QP), BF),
+            ((4, PNE, R), BF),
             ((4 * HD, D), BF),
             ((2 * R, D), BF),
-            ((8 * HD, R), BF),
-            ((R, 3 * QP), F32),
+            ((8 * HD + 6 * R, R), BF),
+            ((R + 8, QP), F32),
         ],
-        bits, xg, same, gain, bias, wo, wq,
-        smem=(0,),
-        hbm=(6,),
+        xg, same, gain, bias, wo, wq,
+        hbm=(5,),
         out_hbm=(0, 1),
         mib=MIB_BLOCK,
     )
@@ -337,24 +341,16 @@
     sz, sy = call(
         pair_body,
         [((HD, D), BF), ((HD, D), BF)],
-        bits, ng, heads, got,
-        smem=(0,),
+        ng, heads, got,
         mib=MIB_PAIR,
     )
     gz = swap(sz, 2)
     gy = swap(sy, 16)
-    keep, sy, sz = call(
-        second_body,
-        [((HD, D), F32), ((HD // 2, D), BF), ((HD // 2, D), BF)],
-        bits, ng, heads, got, gz, gy,
-        smem=(0,),
-        mib=MIB_PAIR,
-    )
     (back,) = call(
         post_body,
         [((R, 2, HALF), BF)],
-        pn, aux, keep, swap(sy, 16), swap(sz, 2),
-        scratch=[pltpu.VMEM((D, R), F32)],
+        pn, stat, ng, heads, got, gz, gy,
+        scratch=[pltpu.VMEM((D, R), F32)] * 2,
         mib=MIB_POST,
     )
     back = lax.all_to_all(back, "dp", 0, 0, tiled=True)

time: 107 us -> 98.5 us (0.921)
  starting transfers between devices: 36.8 us -> 31 us
  Pallas kernels: 13.6 us -> 10.4 us
  blocking collectives: 25.4 us -> 27 us
  waiting for transfers between devices: 29.5 us -> 28.1 us
    ppermute x5 -> x3, waiting for transfers between devices: 7.55 us -> 0.01 us  [swap(): return lax.ppermute(a, 'dp', [(i, i ^ bit) for i in range(128)])]
    all_to_all x1, waiting for transfers between devices: 0.01 us -> 6.02 us  [local(): pn = lax.all_to_all(pn, 'zero', 0, 0, tiled=True)]
    ppermute x5 -> x3, starting transfers between devices: 14.3 us -> 8.54 us  [swap(): return lax.ppermute(a, 'dp', [(i, i ^ bit) for i in range(128)])]
    pallas_call x7 -> x6, Pallas kernels: 13.6 us -> 10.4 us  [call(): pl.pallas_call(body, out_shape=tuple((jax.ShapeDtypeStruct(s, d) for s, d...]
    all_to_all x1, blocking collectives: 25.4 us -> 27 us  [local(): back = lax.all_to_all(back, 'dp', 0, 0, tiled=True)]
  transfers between devices with their start and end apart: 7 -> 5, of which waited for: 4 -> 2; matrix products, arithmetic and copies ran while one was open for 0% -> 0% of each run, Pallas kernels for 2% -> 1%
where the time goes in v6:
time: 98.5 us; the launch traced here: 97.3 us
  starting transfers between devices  31 us (31%)
  waiting for transfers between devices  28.1 us (29%)
  blocking collectives  27 us (27%)
  Pallas kernels  10.4 us (11%)
    all_to_all x1, blocking collectives, local(): back = lax.all_to_all(back, 'dp', 0, 0, tiled=True)  27 us
    all_to_all x1, waiting for transfers between devices, local(): xg = lax.all_to_all(xg, 'dp', 0, 0, tiled=True)  22 us
    all_to_all x1, starting transfers between devices, local(): xg = lax.all_to_all(xg, 'dp', 0, 0, tiled=True)  18.4 us
    pallas_call x6, Pallas kernels, call(): pl.pallas_call(body, out_shape=tuple((jax.ShapeDtypeStruct(s, d) for s, d...  10.4 us
    ppermute x3, starting transfers between devices, swap(): return lax.ppermute(a, 'dp', [(i, i ^ bit) for i in range(128)])  8.54 us
    all_to_all x1, waiting for transfers between devices, local(): pn = lax.all_to_all(pn, 'zero', 0, 0, tiled=True)  6.02 us
    all_to_all x1, starting transfers between devices, local(): pn = lax.all_to_all(pn, 'zero', 0, 0, tiled=True)  4.03 us
  transfers between devices with their start and end apart: 5, of which 2 were waited for; matrix products, arithmetic and copies ran while one was open for 0% of the time, Pallas kernels for 1%

profile of v6, /device:TPU:1, one launch (start us, length us, event | category | flops | bytes accessed | tf_op | source)
XLA Modules:
  0.0 97.3 jit_solution(16321024707320236031)
XLA Ops:
  0.6 0.0 copy-start.4
  0.6 0.0 copy-start.5
  0.7 0.0 copy-start
  0.7 0.0 copy-start.3
  0.7 0.0 copy-start.2
  0.7 2.5 %shard_map.136 = bf16[128,2,1280]{2,1,0:T(2,128)(2,1)} custom-call(s32[1,128]{1,0:T(1,128)} %send_ref.1, bf16[128,1280]{1,0:T(8,128)(2,1)} %x_hbm.1, bf16[128,1280]{1,0:T(8,128)(2,1)} %g_hbm.1), custom_call_target="tpu_custom_call" | custom-call | tf_op jit(solution)/shard_map/pallas_call | solution.py:42
  3.2 18.4 %all-to-all-start = ((bf16[128,2,1280]{2,1,0:T(2,128)(2,1)}), bf16[128,2,1280]{2,1,0:T(2,128)(2,1)S(1)}, u32[]{:S(2)}, u32[]{:S(2)}) async-start(bf16[128,2,1280]{2,1,0:T(2,128)(2,1)} %shard_map.136), calls=%async_computation | async-start | bytes 1310720 | tf_op jit(solution)/shard_map/all_to_all | solution.py:324
  21.6 0.0 copy-done.4
  21.6 0.0 copy-done.5
  21.7 0.0 copy-done
  21.7 0.0 copy-done.3
  21.7 0.0 copy-done.2
  21.7 0.2 shard_map.137
  21.9 22.0 %all-to-all-done.xg_ref = bf16[128,2,1280]{2,1,0:T(2,128)(2,1)S(1)} async-done(((bf16[128,2,1280]{2,1,0:T(2,128)(2,1)}), bf16[128,2,1280]{2,1,0:T(2,128)(2,1)S(1)}, u32[]{:S(2)}, u32[]{:S(2)}) %all-to-all-start) | async-done | bytes 655392 | tf_op jit(solution)/shard_map/all_to_all | solution.py:324
  44.0 4.9 %shard_map.138 = (bf16[4,672,128]{2,1,0:T(8,128)(2,1)}, bf16[320,1280]{1,0:T(8,128)(2,1)}, bf16[256,1280]{1,0:T(8,128)(2,1)S(1)}, bf16[1408,128]{1,0:T(8,128)(2,1)S(1)}, f32[136,384]{1,0:T(8,128)S(1)}) custom-call(bf16[128,2,1280]{2,1,0:T(2,128)(2,1)S(1)} %all-to-all-done.xg_ref, f32[128,128]{1,0:T(8,128)S(1)} %get-tuple-element.23.same_ref, ...), custom_call_target="tpu_custom_call" | custom-call | tf_op jit(solution)/shard_map/pallas_call | solution.py:42
  48.8 3.8 %collective-permute-start = (bf16[320,1280]{1,0:T(8,128)(2,1)}, bf16[320,1280]{1,0:T(8,128)(2,1)S(1)}, u32[]{:S(2)}, u32[]{:S(2)}) collective-permute-start(bf16[320,1280]{1,0:T(8,128)(2,1)} %get-tuple-element.31), channel_id=1, source_target_pairs={{0,4},{4,0},{8,12},{12,8},{16,20},{20,16},{24,28},{28,24},{32,36},... | collective-permute-start | bytes 2457608 | tf_op jit(solution)/shard_map/ppermute | solution.py:315
  52.6 4.0 %all-to-all-start.1 = ((bf16[4,672,128]{2,1,0:T(8,128)(2,1)}), bf16[4,672,128]{2,1,0:T(8,128)(2,1)S(1)}, u32[]{:S(2)}, u32[]{:S(2)}) async-start(bf16[4,672,128]{2,1,0:T(8,128)(2,1)} %get-tuple-element.27), calls=%async_computation.1 | async-start | bytes 1376256 | tf_op jit(solution)/shard_map/all_to_all | solution.py:340
  56.7 0.0 collective-permute-done.got_ref
  56.7 0.3 shard_map.139
  57.0 2.0 %collective-permute-start.1 = (bf16[80,1280]{1,0:T(8,128)(2,1)S(1)}, bf16[80,1280]{1,0:T(8,128)(2,1)S(1)}, u32[]{:S(2)}, u32[]{:S(2)}) collective-permute-start(bf16[80,1280]{1,0:T(8,128)(2,1)S(1)} %get-tuple-element.32), channel_id=1, source_target_pairs={{0,8},{4,12},{8,0},{12,4},{16,24},{20,28},{24,16},{28,20},{32,40},... | collective-permute-start | bytes 614408 | tf_op jit(solution)/shard_map/ppermute | solution.py:315
  59.0 2.7 %collective-permute-start.2 = (bf16[80,1280]{1,0:T(8,128)(2,1)S(1)}, bf16[80,1280]{1,0:T(8,128)(2,1)S(1)}, u32[]{:S(2)}, u32[]{:S(2)}) collective-permute-start(bf16[80,1280]{1,0:T(8,128)(2,1)S(1)} %get-tuple-element.33), channel_id=1, source_target_pairs={{0,64},{4,68},{8,72},{12,76},{16,80},{20,84},{24,88},{28,92},{32,9... | collective-permute-start | bytes 614408 | tf_op jit(solution)/shard_map/ppermute | solution.py:315
  61.7 6.0 %all-to-all-done.1.pn_ref = bf16[4,672,128]{2,1,0:T(8,128)(2,1)S(1)} async-done(((bf16[4,672,128]{2,1,0:T(8,128)(2,1)}), bf16[4,672,128]{2,1,0:T(8,128)(2,1)S(1)}, u32[]{:S(2)}, u32[]{:S(2)}) %all-to-all-start.1) | async-done | bytes 688160 | tf_op jit(solution)/shard_map/all_to_all | solution.py:340
  67.8 0.0 collective-permute-done.1.gz_ref
  67.8 0.0 collective-permute-done.2.gy_ref
  67.8 0.0 copy-start.1
  67.8 1.3 %shard_map.140 = bf16[128,2,1152]{2,1,0:T(2,128)(2,1)S(1)} custom-call(bf16[4,672,128]{2,1,0:T(8,128)(2,1)S(1)} %all-to-all-done.1.pn_ref, f32[136,384]{1,0:T(8,128)S(1)} %get-tuple-element.28.stat_ref, bf16[256,1280]{1,0:T(8,128)(2,1)S(1)} %get-tuple-element.29.ng_ref, bf16[1408,128]{1,0:T(8,128)(2,1)S(1)} %get-tuple-element.30.heads_ref, ...), custom_call_target="tpu_custom_call" | custom-call | tf_op jit(solution)/shard_map/pallas_call | solution.py:42
  69.1 27.0 %all_to_all.15.b_ref = bf16[128,2,1152]{2,1,0:T(2,128)(2,1)S(1)} all-to-all(bf16[128,2,1152]{2,1,0:T(2,128)(2,1)S(1)} %shard_map.140), channel_id=1, replica_groups=mesh['dp'=128,'zero'=4] {'dp'}, dimensions={0} | all-to-all | bytes 1179648 | tf_op jit(solution)/shard_map/all_to_all | solution.py:356
  96.1 0.0 copy-done.1
  96.1 1.2 %shard_map.141 = (bf16[320,128]{1,0:T(8,128)(2,1)}, bf16[320,128]{1,0:T(8,128)(2,1)}, f32[10,3,2,80]{3,2,1,0:T(2,128)}, f32[10,2,80]{2,1,0:T(2,128)}, f32[1,10]{1,0:T(1,128)}, /*index=5*/f32[1,10]{1,0:T(1,128)}) custom-call(s32[1,128]{1,0:T(1,128)S(1)} %copy-done.1, bf16[128,2,1152]{2,1,0:T(2,128)(2,1)S(1)} %all_to_all.15.b_ref), custom_call_target="tpu_custom_call" | custom-call | tf_op jit(solution)/shard_map/pallas_call | solution.py:42
  (2 shorter events, 0.0 us)
Async XLA Ops:
  0.6 21.0 %copy-start.4 = (f32[1280]{0:T(1024)S(1)}, f32[1280]{0:T(1024)}, u32[]{:S(2)}) copy-start(f32[1280]{0:T(1024)} %param.14) | copy-start | bytes 15364
  0.6 21.0 %copy-start.5 = (f32[1280]{0:T(1024)S(1)}, f32[1280]{0:T(1024)}, u32[]{:S(2)}) copy-start(f32[1280]{0:T(1024)} %param.15) | copy-start | bytes 15364
  0.7 21.0 %copy-start = (bf16[2,80,1280]{2,1,0:T(8,128)(2,1)S(1)}, bf16[2,80,1280]{2,1,0:T(8,128)(2,1)}, u32[]{:S(2)}) copy-start(bf16[2,80,1280]{2,1,0:T(8,128)(2,1)} %param.17) | copy-start | bytes 1228804
  0.7 21.0 %copy-start.3 = (s32[1,128]{1,0:T(1,128)S(1)}, s32[1,128]{1,0:T(1,128)}, u32[]{:S(2)}) copy-start(s32[1,128]{1,0:T(1,128)} %seg_ref.1) | copy-start | bytes 1540
  0.7 21.0 %copy-start.2 = (s32[1,128]{1,0:T(1,128)S(1)}, s32[1,128]{1,0:T(1,128)}, u32[]{:S(2)}) copy-start(s32[1,128]{1,0:T(1,128)} %recv_ref.1) | copy-start | bytes 1540
  3.2 40.8 %all-to-all-start = ((bf16[128,2,1280]{2,1,0:T(2,128)(2,1)}), bf16[128,2,1280]{2,1,0:T(2,128)(2,1)S(1)}, u32[]{:S(2)}, u32[]{:S(2)}) async-start(bf16[128,2,1280]{2,1,0:T(2,128)(2,1)} %shard_map.136), calls=%async_computation | async-start | bytes 1310720 | tf_op jit(solution)/shard_map/all_to_all | solution.py:324
  48.8 7.8 %collective-permute-start = (bf16[320,1280]{1,0:T(8,128)(2,1)}, bf16[320,1280]{1,0:T(8,128)(2,1)S(1)}, u32[]{:S(2)}, u32[]{:S(2)}) collective-permute-start(bf16[320,1280]{1,0:T(8,128)(2,1)} %get-tuple-element.31), channel_id=1, source_target_pairs={{0,4},{4,0},{8,12},{12,8},{16,20},{20,16},{24,28},{28,24},{32,36},... | collective-permute-start | bytes 2457608 | tf_op jit(solution)/shard_map/ppermute | solution.py:315
  52.6 15.1 %all-to-all-start.1 = ((bf16[4,672,128]{2,1,0:T(8,128)(2,1)}), bf16[4,672,128]{2,1,0:T(8,128)(2,1)S(1)}, u32[]{:S(2)}, u32[]{:S(2)}) async-start(bf16[4,672,128]{2,1,0:T(8,128)(2,1)} %get-tuple-element.27), calls=%async_computation.1 | async-start | bytes 1376256 | tf_op jit(solution)/shard_map/all_to_all | solution.py:340
  57.0 10.8 %collective-permute-start.1 = (bf16[80,1280]{1,0:T(8,128)(2,1)S(1)}, bf16[80,1280]{1,0:T(8,128)(2,1)S(1)}, u32[]{:S(2)}, u32[]{:S(2)}) collective-permute-start(bf16[80,1280]{1,0:T(8,128)(2,1)S(1)} %get-tuple-element.32), channel_id=1, source_target_pairs={{0,8},{4,12},{8,0},{12,4},{16,24},{20,28},{24,16},{28,20},{32,40},... | collective-permute-start | bytes 614408 | tf_op jit(solution)/shard_map/ppermute | solution.py:315
  59.0 8.7 %collective-permute-start.2 = (bf16[80,1280]{1,0:T(8,128)(2,1)S(1)}, bf16[80,1280]{1,0:T(8,128)(2,1)S(1)}, u32[]{:S(2)}, u32[]{:S(2)}) collective-permute-start(bf16[80,1280]{1,0:T(8,128)(2,1)S(1)} %get-tuple-element.33), channel_id=1, source_target_pairs={{0,64},{4,68},{8,72},{12,76},{16,80},{20,84},{24,88},{28,92},{32,9... | collective-permute-start | bytes 614408 | tf_op jit(solution)/shard_map/ppermute | solution.py:315
  67.8 28.4 %copy-start.1 = (s32[1,128]{1,0:T(1,128)S(1)}, s32[1,128]{1,0:T(1,128)}, u32[]{:S(2)}) copy-start(s32[1,128]{1,0:T(1,128)} %send_ref.1) | copy-start | bytes 1540

commit v7 on v6

--- a/solution.py
+++ b/solution.py
@@ -22,40 +22,21 @@
 WG = 1664
 HALF = (WG + 2 * QW) // 2
 
-MIB = 1024 * 1024
-GATHER_PARTS = 2
-MIB_HOLD, MIB_BLOCK, MIB_PAIR, MIB_POST = 16, 50, 50, 50
-
 
 def dg(a, b, ca, cb):
     return lax.dot_general(a, b, (((ca,), (cb,)), ((), ())), preferred_element_type=F32)
 
 
-def call(body, outs, *args, smem=(), hbm=(), out_hbm=(), scratch=(), mib=50):
-    def space(i):
-        return pltpu.SMEM if i in smem else pltpu.HBM if i in hbm else pltpu.VMEM
-
-    scratch = list(scratch) + [pltpu.VMEM(args[i].shape, args[i].dtype) for i in hbm]
-    scratch += [pltpu.VMEM(*outs[i]) for i in out_hbm]
-    if hbm or out_hbm:
-        scratch.append(pltpu.SemaphoreType.DMA((10,)))
+def call(body, outs, *args, scratch=()):
+    vmem = pl.BlockSpec(memory_space=pltpu.VMEM)
     return pl.pallas_call(
         body,
         out_shape=tuple(jax.ShapeDtypeStruct(s, d) for s, d in outs),
-        in_specs=[pl.BlockSpec(memory_space=space(i)) for i in range(len(args))],
-        out_specs=tuple(
-            pl.BlockSpec(memory_space=pltpu.HBM if i in out_hbm else pltpu.VMEM)
-            for i in range(len(outs))
-        ),
+        in_specs=[vmem] * len(args),
+        out_specs=(vmem,) * len(outs),
         scratch_shapes=scratch,
-        compiler_params=pltpu.CompilerParams(vmem_limit_bytes=mib * MIB),
+        compiler_params=pltpu.CompilerParams(vmem_limit_bytes=16 * 1024 * 1024),
     )(*args)
-
-
-def start(sem, a, b):
-    copy = pltpu.make_async_copy(a, b, sem)
-    copy.start()
-    return copy
 
 
 def lane(shape):
@@ -84,23 +65,20 @@
     return one_hot(hit & (odd == 0)), one_hot(hit & (odd == 1))
 
 
-def gather_body(send_hbm, x_hbm, g_hbm, o_hbm, send_ref, x_ref, g_ref, o_ref, sems):
-    first = start(sems.at[7], send_hbm, send_ref)
-    copies = [start(sems.at[0], x_hbm, x_ref), start(sems.at[1], g_hbm, g_ref)]
-    first.wait()
+def gather_body(
+    send_ref, xg_ref, recv_ref, seg_ref, gain_ref, bias_ref, wo_ref,
+    o_ref, same_ref, gain_out, bias_out, wo_out,
+):
     even, odd = pair_picks(send_ref)
-    for copy in copies:
-        copy.wait()
-    copies = []
-    step = R // GATHER_PARTS
-    for i in range(GATHER_PARTS):
-        rows = slice(2 * step * i, 2 * step * (i + 1))
-        part = dg(even[:, rows], x_ref[...], 0, 0) + dg(odd[:, rows], g_ref[...], 0, 0)
-        at = pl.ds(step * i, step)
-        o_ref[at] = part.astype(BF).reshape(step, 2, D)
-        copies.append(start(sems.at[2 + i], o_ref.at[at], o_hbm.at[at]))
-    for copy in copies:
-        copy.wait()
+    pick = jnp.concatenate([even, odd], axis=0)
+    o_ref[...] = dg(pick, xg_ref[...], 0, 0).astype(BF).reshape(R, 2, D)
+    hit = sub((R, R)) == recv_ref[...]
+    seg = jnp.sum(jnp.where(hit, seg_ref[...], 0), axis=1, keepdims=True)
+    group = one_hot(seg == lane((R, R)))
+    same_ref[...] = dg(group, group, 1, 1)
+    gain_out[...] = gain_ref[...].reshape(1, D)
+    bias_out[...] = bias_ref[...].reshape(1, D)
+    wo_out[...] = wo_ref[...]
 
 
 def norm_stats(x):
@@ -110,24 +88,10 @@
     return mean, inv, centred * inv
 
 
-def hold_body(
-    recv_ref, seg_ref, gain_ref, bias_ref, wo_ref, same_ref, gain_out, bias_out, wo_out
+def block_body(
+    xg_ref, same_ref, gain_ref, bias_ref, wo_ref, wq_ref,
+    pn_ref, ng_ref, heads_ref, stat_ref,
 ):
-    hit = sub((R, R)) == recv_ref[...]
-    seg = jnp.sum(jnp.where(hit, seg_ref[...], 0), axis=1, keepdims=True)
-    group = one_hot(seg == lane((R, R)))
-    same_ref[...] = dg(group, group, 1, 1)
-    gain_out[...] = gain_ref[...]
-    bias_out[...] = bias_ref[...]
-    wo_out[...] = wo_ref[...]
-
-
-def block_body(
-    xg_ref, same_ref, gain_ref, bias_ref, wo_ref, wq_hbm,
-    pn_hbm, send_hbm, ng_ref, heads_ref, stat_ref,
-    wq_ref, pn_ref, send_ref, sems,
-):
-    copies = [start(sems.at[0], wq_hbm, wq_ref)]
     xg = xg_ref[...].reshape(2 * R, D)
     at = lane((R, 2 * R)) - 2 * sub((R, 2 * R))
     x = dg(one_hot(at == 0), xg, 1, 0)
@@ -150,7 +114,6 @@
 
     stat_ref[:R, :R] = jnp.where(lane((R, R)) < 64, mean, inv)
     dh = dg(wo_ref[...], g, 1, 1).astype(BF)
-    copies.pop().wait()
     qkv = dg(wq_ref[...], normed, 1, 1).astype(BF)
     same = same_ref[...] > 0.5
     rows = []
@@ -173,18 +136,10 @@
     heads_ref[: 8 * HD] = jnp.concatenate(rows, axis=0)
     qg = jnp.concatenate(rows[0:3] + rows[4:7], axis=0)
     ho = jnp.concatenate([rows[3], rows[7]], axis=0)
-    other = (1 - place_bits()[0]) * 4 * HD
-    a = heads_ref[pl.ds(pl.multiple_of(other, 4 * HD), 3 * HD), :]
-    b = heads_ref[pl.ds(pl.multiple_of(other + 3 * HD, HD), HD), :]
-    send_ref[: 3 * HD, :] = dg(a, normed, 1, 0).astype(BF)
-    send_ref[3 * HD :, :] = dg(b, g, 1, 0).astype(BF)
-    copies.append(start(sems.at[9], send_ref, send_hbm))
     p = dg(ho, wo_ref[...], 0, 0)
     for i in range(4):
         for t in range(2):
             pn_ref[i, t * R : (t + 1) * R] = p[:, i * QW + t * R : i * QW + (t + 1) * R].astype(BF)
-        rows = pl.ds(0, 2 * R)
-        copies.append(start(sems.at[1 + i], pn_ref.at[i, rows], pn_hbm.at[i, rows]))
     n = dg(qg, wq_ref[...], 0, 0)
     u = n * gain_ref[...]
     m1 = jnp.sum(u, axis=1, keepdims=True) * (1.0 / D)
@@ -207,10 +162,14 @@
             cols = slice(at + 64 + t * R, at + 64 + (t + 1) * R)
             pn_ref[i, (3 + t) * R : (4 + t) * R] = n[:, cols].astype(BF)
         pn_ref[i, PN:] = extra
-        rows = pl.ds(2 * R, PNE - 2 * R)
-        copies.append(start(sems.at[5 + i], pn_ref.at[i, rows], pn_hbm.at[i, rows]))
-    for copy in copies:
-        copy.wait()
+
+
+def other_body(ng_ref, heads_ref, send_ref):
+    other = (1 - place_bits()[0]) * 4 * HD
+    a = heads_ref[pl.ds(pl.multiple_of(other, 4 * HD), 3 * HD), :]
+    b = heads_ref[pl.ds(pl.multiple_of(other + 3 * HD, HD), HD), :]
+    send_ref[: 3 * HD, :] = dg(a, ng_ref[:R, :], 1, 0).astype(BF)
+    send_ref[3 * HD :, :] = dg(b, ng_ref[R:, :], 1, 0).astype(BF)
 
 
 def own_rows(c, first, choose_out, ng_ref, heads_ref):
@@ -308,41 +267,34 @@
 def local(patches, cotangent, send_order, recv_order, segment_ids, ln_gain, ln_bias, w_qkv, w_out):
     wq = w_qkv.transpose(1, 2, 3, 0).reshape(NQ, D)
     wo = w_out.reshape(NO, D)
-    gain = ln_gain.reshape(1, D)
-    bias = ln_bias.reshape(1, D)
 
     def swap(a, bit):
         return lax.ppermute(a, "dp", [(i, i ^ bit) for i in range(128)])
 
-    (xg,) = call(gather_body, [((R, 2, D), BF)], send_order, patches, cotangent, hbm=(0, 1, 2), out_hbm=(0,), mib=58)
-    same, gain, bias, wo = call(
-        hold_body,
-        [((R, R), F32), ((1, D), F32), ((1, D), F32), ((NO, D), BF)],
-        recv_order, segment_ids, gain, bias, wo,
-        mib=MIB_HOLD,
+    xg = jnp.concatenate([patches, cotangent], axis=0)
+    xg, same, gain, bias, wo = call(
+        gather_body,
+        [((R, 2, D), BF), ((R, R), F32), ((1, D), F32), ((1, D), F32), ((NO, D), BF)],
+        send_order, xg, recv_order, segment_ids, ln_gain, ln_bias, wo,
     )
     xg = lax.all_to_all(xg, "dp", 0, 0, tiled=True)
-    pn, send, ng, heads, stat = call(
+    pn, ng, heads, stat = call(
         block_body,
         [
             ((4, PNE, R), BF),
-            ((4 * HD, D), BF),
             ((2 * R, D), BF),
             ((8 * HD + 6 * R, R), BF),
             ((R + 8, QP), F32),
         ],
         xg, same, gain, bias, wo, wq,
-        hbm=(5,),
-        out_hbm=(0, 1),
-        mib=MIB_BLOCK,
-    )
+    )
+    (send,) = call(other_body, [((4 * HD, D), BF)], ng, heads)
     got = swap(send, 1)
     pn = lax.all_to_all(pn, "zero", 0, 0, tiled=True)
     sz, sy = call(
         pair_body,
         [((HD, D), BF), ((HD, D), BF)],
         ng, heads, got,
-        mib=MIB_PAIR,
     )
     gz = swap(sz, 2)
     gy = swap(sy, 16)
@@ -351,7 +303,6 @@
         [((R, 2, HALF), BF)],
         pn, stat, ng, heads, got, gz, gy,
         scratch=[pltpu.VMEM((D, R), F32)] * 2,
-        mib=MIB_POST,
     )
     back = lax.all_to_all(back, "dp", 0, 0, tiled=True)
     enc, grad, qkv_share, out_share, gain_grad, bias_grad = call(

time: 98.5 us -> 96 us (0.975)
  blocking collectives: 27 us -> 67.6 us
  waiting for transfers between devices: 28.1 us -> 6.03 us
  starting transfers between devices: 31 us -> 12.5 us
  Pallas kernels: 10.4 us -> 6.76 us
  other arithmetic: 0 us -> 1.16 us
    all_to_all x0 -> x1, blocking collectives: none -> 40.5 us  [local(): xg = lax.all_to_all(xg, 'dp', 0, 0, tiled=True)]
    all_to_all x1 -> x0, waiting for transfers between devices: 22 us -> none  [local(): xg = lax.all_to_all(xg, 'dp', 0, 0, tiled=True)]
    all_to_all x1 -> x0, starting transfers between devices: 18.4 us -> none  [local(): xg = lax.all_to_all(xg, 'dp', 0, 0, tiled=True)]
    pallas_call x6, Pallas kernels: 10.4 us -> 6.76 us  [call(): pl.pallas_call(body, out_shape=tuple((jax.ShapeDtypeStruct(s, d) for s, d...]
    concatenate x0 -> x1, other arithmetic: none -> 1.16 us  [local(): xg = jnp.concatenate([patches, cotangent], axis=0)]
  transfers between devices with their start and end apart: 5 -> 4, of which waited for: 2 -> 1; matrix products, arithmetic and copies ran while one was open for 0% -> 0% of each run, Pallas kernels for 1% -> 0%
where the time goes in v7:
time: 96 us; the launch traced here: 94.9 us
  blocking collectives  67.6 us (70%)
  starting transfers between devices  12.5 us (13%)
  Pallas kernels  6.76 us (7%)
  waiting for transfers between devices  6.03 us (6%)
  other arithmetic  1.16 us (1%)
    all_to_all x1, blocking collectives, local(): xg = lax.all_to_all(xg, 'dp', 0, 0, tiled=True)  40.5 us
    all_to_all x1, blocking collectives, local(): back = lax.all_to_all(back, 'dp', 0, 0, tiled=True)  27 us
    ppermute x3, starting transfers between devices, swap(): return lax.ppermute(a, 'dp', [(i, i ^ bit) for i in range(128)])  8.52 us
    pallas_call x6, Pallas kernels, call(): pl.pallas_call(body, out_shape=tuple((jax.ShapeDtypeStruct(s, d) for s, d...  6.76 us
    all_to_all x1, waiting for transfers between devices, local(): pn = lax.all_to_all(pn, 'zero', 0, 0, tiled=True)  6.02 us
    all_to_all x1, starting transfers between devices, local(): pn = lax.all_to_all(pn, 'zero', 0, 0, tiled=True)  4.02 us
  transfers between devices with their start and end apart: 4, of which 1 were waited for; matrix products, arithmetic and copies ran while one was open for 0% of the time, Pallas kernels for 0%

profile of v7, /device:TPU:1, one launch (start us, length us, event | category | flops | bytes accessed | tf_op | source)
XLA Modules:
  0.0 94.9 jit_solution(17918602927027769437)
XLA Ops:
  0.6 0.0 copy-start.5
  0.6 0.0 copy-start.2
  0.7 0.0 copy-start.4
  0.7 0.0 copy-start.3
  0.7 0.0 copy-start.7
  0.7 0.0 copy-start.6
  0.7 1.2 %pad_maximum_fusion.xg_ref = bf16[256,1280]{1,0:T(8,128)(2,1)S(1)} fusion(bf16[128,1280]{1,0:T(8,128)(2,1)} %param.10, bf16[128,1280]{1,0:T(8,128)(2,1)} %param.9), kind=kLoop, calls=%fused_computation | loop fusion | flops 1310720 | bytes 1310720 | tf_op jit(solution)/shard_map/concatenate | solution.py:274
  1.9 0.0 copy-start
  1.9 0.0 copy-done.5
  1.9 0.0 copy-done.2
  1.9 0.0 copy-done.4
  1.9 0.0 copy-done.3
  1.9 0.0 copy-done.7
  1.9 0.0 copy-done.6
  1.9 0.6 shard_map.136
  2.5 40.5 %all_to_all.15.xg_ref = bf16[128,2,1280]{2,1,0:T(2,128)(2,1)S(1)} all-to-all(bf16[128,2,1280]{2,1,0:T(2,128)(2,1)S(1)} %get-tuple-element.23), channel_id=1, replica_groups=mesh['dp'=128,'zero'=4] {'dp'}, dimensions={0} | all-to-all | bytes 1310720 | tf_op jit(solution)/shard_map/all_to_all | solution.py:280
  43.0 0.0 copy-done
  43.0 3.1 %shard_map.137 = (bf16[4,672,128]{2,1,0:T(8,128)(2,1)S(1)}, bf16[256,1280]{1,0:T(8,128)(2,1)S(1)}, bf16[1408,128]{1,0:T(8,128)(2,1)S(1)}, f32[136,384]{1,0:T(8,128)S(1)}) custom-call(bf16[128,2,1280]{2,1,0:T(2,128)(2,1)S(1)} %all_to_all.15.xg_ref, f32[128,128]{1,0:T(8,128)S(1)} %get-tuple-element.24.same_ref, f32[1,1280]{1,0:T(1,128)S(1)} %get-tuple-element.25.gain_ref, ...), custom_call_target="tpu_custom_call" | custom-call | tf_op jit(solution)/shard_map/pallas_call | solution.py:32
  46.1 0.0 copy-start.1
  46.1 0.4 shard_map.138
  46.5 3.8 %collective-permute-start = (bf16[320,1280]{1,0:T(8,128)(2,1)S(1)}, bf16[320,1280]{1,0:T(8,128)(2,1)S(1)}, u32[]{:S(2)}, u32[]{:S(2)}) collective-permute-start(bf16[320,1280]{1,0:T(8,128)(2,1)S(1)} %shard_map.138), channel_id=1, source_target_pairs={{0,4},{4,0},{8,12},{12,8},{16,20},{20,16},{24,28},{28,24},{32,36},... | collective-permute-start | bytes 2457608 | tf_op jit(solution)/shard_map/ppermute | solution.py:272
  50.3 0.0 copy-done.1
  50.3 4.0 %all-to-all-start.1 = ((bf16[4,672,128]{2,1,0:T(8,128)(2,1)}), bf16[4,672,128]{2,1,0:T(8,128)(2,1)S(1)}, u32[]{:S(2)}, u32[]{:S(2)}) async-start(bf16[4,672,128]{2,1,0:T(8,128)(2,1)} %copy-done.1), calls=%async_computation.1 | async-start | bytes 1376256 | tf_op jit(solution)/shard_map/all_to_all | solution.py:293
  54.3 0.0 collective-permute-done.got_ref
  54.3 0.3 shard_map.139
  54.6 2.0 %collective-permute-start.1 = (bf16[80,1280]{1,0:T(8,128)(2,1)S(1)}, bf16[80,1280]{1,0:T(8,128)(2,1)S(1)}, u32[]{:S(2)}, u32[]{:S(2)}) collective-permute-start(bf16[80,1280]{1,0:T(8,128)(2,1)S(1)} %get-tuple-element.32), channel_id=1, source_target_pairs={{0,8},{4,12},{8,0},{12,4},{16,24},{20,28},{24,16},{28,20},{32,40},... | collective-permute-start | bytes 614408 | tf_op jit(solution)/shard_map/ppermute | solution.py:272
  56.7 2.7 %collective-permute-start.2 = (bf16[80,1280]{1,0:T(8,128)(2,1)S(1)}, bf16[80,1280]{1,0:T(8,128)(2,1)S(1)}, u32[]{:S(2)}, u32[]{:S(2)}) collective-permute-start(bf16[80,1280]{1,0:T(8,128)(2,1)S(1)} %get-tuple-element.33), channel_id=1, source_target_pairs={{0,64},{4,68},{8,72},{12,76},{16,80},{20,84},{24,88},{28,92},{32,9... | collective-permute-start | bytes 614408 | tf_op jit(solution)/shard_map/ppermute | solution.py:272
  59.4 6.0 %all-to-all-done.1.pn_ref = bf16[4,672,128]{2,1,0:T(8,128)(2,1)S(1)} async-done(((bf16[4,672,128]{2,1,0:T(8,128)(2,1)}), bf16[4,672,128]{2,1,0:T(8,128)(2,1)S(1)}, u32[]{:S(2)}, u32[]{:S(2)}) %all-to-all-start.1) | async-done | bytes 688160 | tf_op jit(solution)/shard_map/all_to_all | solution.py:293
  65.4 0.0 collective-permute-done.1.gz_ref
  65.4 0.0 collective-permute-done.2.gy_ref
  65.4 1.3 %shard_map.140 = bf16[128,2,1152]{2,1,0:T(2,128)(2,1)S(1)} custom-call(bf16[4,672,128]{2,1,0:T(8,128)(2,1)S(1)} %all-to-all-done.1.pn_ref, f32[136,384]{1,0:T(8,128)S(1)} %get-tuple-element.29.stat_ref, bf16[256,1280]{1,0:T(8,128)(2,1)S(1)} %get-tuple-element.30.ng_ref, bf16[1408,128]{1,0:T(8,128)(2,1)S(1)} %get-tuple-element.31.heads_ref, ...), custom_call_target="tpu_custom_call" | custom-call | tf_op jit(solution)/shard_map/pallas_call | solution.py:32
  66.7 27.0 %all_to_all.16.b_ref = bf16[128,2,1152]{2,1,0:T(2,128)(2,1)S(1)} all-to-all(bf16[128,2,1152]{2,1,0:T(2,128)(2,1)S(1)} %shard_map.140), channel_id=1, replica_groups=mesh['dp'=128,'zero'=4] {'dp'}, dimensions={0} | all-to-all | bytes 1179648 | tf_op jit(solution)/shard_map/all_to_all | solution.py:307
  93.8 1.2 %shard_map.141 = (bf16[320,128]{1,0:T(8,128)(2,1)}, bf16[320,128]{1,0:T(8,128)(2,1)}, f32[10,3,2,80]{3,2,1,0:T(2,128)}, f32[10,2,80]{2,1,0:T(2,128)}, f32[1,10]{1,0:T(1,128)}, /*index=5*/f32[1,10]{1,0:T(1,128)}) custom-call(s32[1,128]{1,0:T(1,128)S(1)} %copy-done.5, bf16[128,2,1152]{2,1,0:T(2,128)(2,1)S(1)} %all_to_all.16.b_ref), custom_call_target="tpu_custom_call" | custom-call | tf_op jit(solution)/shard_map/pallas_call | solution.py:32
Async XLA Ops:
  0.6 1.2 %copy-start.5 = (s32[1,128]{1,0:T(1,128)S(1)}, s32[1,128]{1,0:T(1,128)}, u32[]{:S(2)}) copy-start(s32[1,128]{1,0:T(1,128)} %send_ref.3) | copy-start | bytes 1540
  0.6 1.2 %copy-start.2 = (bf16[2,80,1280]{2,1,0:T(8,128)(2,1)S(1)}, bf16[2,80,1280]{2,1,0:T(8,128)(2,1)}, u32[]{:S(2)}) copy-start(bf16[2,80,1280]{2,1,0:T(8,128)(2,1)} %param.17) | copy-start | bytes 1228804
  0.7 1.2 %copy-start.4 = (f32[1280]{0:T(1024)S(1)}, f32[1280]{0:T(1024)}, u32[]{:S(2)}) copy-start(f32[1280]{0:T(1024)} %bias_ref.1) | copy-start | bytes 15364
  0.7 1.2 %copy-start.3 = (f32[1280]{0:T(1024)S(1)}, f32[1280]{0:T(1024)}, u32[]{:S(2)}) copy-start(f32[1280]{0:T(1024)} %gain_ref.1) | copy-start | bytes 15364
  0.7 1.2 %copy-start.7 = (s32[1,128]{1,0:T(1,128)S(1)}, s32[1,128]{1,0:T(1,128)}, u32[]{:S(2)}) copy-start(s32[1,128]{1,0:T(1,128)} %seg_ref.1) | copy-start | bytes 1540
  0.7 1.2 %copy-start.6 = (s32[1,128]{1,0:T(1,128)S(1)}, s32[1,128]{1,0:T(1,128)}, u32[]{:S(2)}) copy-start(s32[1,128]{1,0:T(1,128)} %recv_ref.1) | copy-start | bytes 1540
  1.9 41.2 %copy-start = (bf16[1280,2,3,80]{0,3,2,1:T(8,128)(2,1)S(1)}, bf16[1280,2,3,80]{0,3,2,1:T(8,128)(2,1)}, u32[]{:S(2)}) copy-start(bf16[1280,2,3,80]{0,3,2,1:T(8,128)(2,1)} %param.16) | copy-start | bytes 3686404
  46.1 4.2 %copy-start.1 = (bf16[4,672,128]{2,1,0:T(8,128)(2,1)}, bf16[4,672,128]{2,1,0:T(8,128)(2,1)S(1)}, u32[]{:S(2)}) copy-start(bf16[4,672,128]{2,1,0:T(8,128)(2,1)S(1)} %get-tuple-element.28) | copy-start | bytes 2064388
  46.5 7.8 %collective-permute-start = (bf16[320,1280]{1,0:T(8,128)(2,1)S(1)}, bf16[320,1280]{1,0:T(8,128)(2,1)S(1)}, u32[]{:S(2)}, u32[]{:S(2)}) collective-permute-start(bf16[320,1280]{1,0:T(8,128)(2,1)S(1)} %shard_map.138), channel_id=1, source_target_pairs={{0,4},{4,0},{8,12},{12,8},{16,20},{20,16},{24,28},{28,24},{32,36},... | collective-permute-start | bytes 2457608 | tf_op jit(solution)/shard_map/ppermute | solution.py:272
  50.3 15.1 %all-to-all-start.1 = ((bf16[4,672,128]{2,1,0:T(8,128)(2,1)}), bf16[4,672,128]{2,1,0:T(8,128)(2,1)S(1)}, u32[]{:S(2)}, u32[]{:S(2)}) async-start(bf16[4,672,128]{2,1,0:T(8,128)(2,1)} %copy-done.1), calls=%async_computation.1 | async-start | bytes 1376256 | tf_op jit(solution)/shard_map/all_to_all | solution.py:293
  54.6 10.8 %collective-permute-start.1 = (bf16[80,1280]{1,0:T(8,128)(2,1)S(1)}, bf16[80,1280]{1,0:T(8,128)(2,1)S(1)}, u32[]{:S(2)}, u32[]{:S(2)}) collective-permute-start(bf16[80,1280]{1,0:T(8,128)(2,1)S(1)} %get-tuple-element.32), channel_id=1, source_target_pairs={{0,8},{4,12},{8,0},{12,4},{16,24},{20,28},{24,16},{28,20},{32,40},... | collective-permute-start | bytes 614408 | tf_op jit(solution)/shard_map/ppermute | solution.py:272
  56.7 8.7 %collective-permute-start.2 = (bf16[80,1280]{1,0:T(8,128)(2,1)S(1)}, bf16[80,1280]{1,0:T(8,128)(2,1)S(1)}, u32[]{:S(2)}, u32[]{:S(2)}) collective-permute-start(bf16[80,1280]{1,0:T(8,128)(2,1)S(1)} %get-tuple-element.33), channel_id=1, source_target_pairs={{0,64},{4,68},{8,72},{12,76},{16,80},{20,84},{24,88},{28,92},{32,9... | collective-permute-start | bytes 614408 | tf_op jit(solution)/shard_map/ppermute | solution.py:272

commit v8 on v7

--- a/solution.py
+++ b/solution.py
@@ -49,7 +49,12 @@
 
 def place_bits():
     dp = lax.axis_index("dp")
-    return lax.rem(dp, 2), lax.rem(dp // 2, 2), lax.rem(dp // 16, 2)
+    core = lax.rem(dp, 2)
+    return core, jnp.where(core == 0, lax.rem(dp // 2, 2), lax.rem(dp // 16, 2))
+
+
+def partner(i):
+    return i ^ (2 if i % 2 == 0 else 16)
 
 
 def one_hot(cond):
@@ -172,42 +177,32 @@
     send_ref[3 * HD :, :] = dg(b, ng_ref[R:, :], 1, 0).astype(BF)
 
 
-def own_rows(c, first, choose_out, ng_ref, heads_ref):
-    a = heads_ref[pl.ds(pl.multiple_of((c * 4 + first) * HD, HD), HD), :]
-    if choose_out is None:
-        return dg(a, ng_ref[:R, :], 1, 0)
-    b = heads_ref[pl.ds(pl.multiple_of((c * 4 + 3) * HD, HD), HD), :]
-    pick = choose_out.astype(F32)
-    left = jnp.concatenate([a.astype(F32) * (1.0 - pick), b.astype(F32) * pick], axis=1).astype(BF)
-    return dg(left, ng_ref[...], 1, 0)
-
-
-def part_rows(ref, j):
-    return ref[pl.ds(pl.multiple_of(j * HD, HD), HD), :].astype(F32)
-
-
-def pair_body(ng_ref, heads_ref, got_ref, sz_ref, sy_ref):
-    c, z, y = place_bits()
-    a = own_rows(c, 1 - z, None, ng_ref, heads_ref)
-    b = own_rows(c, 2, 1 - y, ng_ref, heads_ref)
-    sz_ref[...] = (a + part_rows(got_ref, 1 - z)).astype(BF)
-    sy_ref[...] = (b + part_rows(got_ref, 3 - y)).astype(BF)
+def half_rows(c, half, ng_ref, heads_ref, got_ref):
+    rows = heads_ref[pl.ds(pl.multiple_of((c * 2 + half) * 2 * HD, 2 * HD), 2 * HD), :]
+    out = half.astype(F32) * (sub((2 * HD, R)) >= HD).astype(F32)
+    rows = rows.astype(F32)
+    left = jnp.concatenate([rows * (1.0 - out), rows * out], axis=1).astype(BF)
+    got = got_ref[pl.ds(pl.multiple_of(half * 2 * HD, 2 * HD), 2 * HD), :]
+    return dg(left, ng_ref[...], 1, 0) + got.astype(F32)
+
+
+def pair_body(ng_ref, heads_ref, got_ref, send_ref):
+    c, half = place_bits()
+    send_ref[...] = half_rows(c, 1 - half, ng_ref, heads_ref, got_ref).astype(BF)
 
 
 def post_body(
-    pn_ref, stat_ref, ng_ref, heads_ref, got_ref, gz_ref, gy_ref, o_ref, wz_ref, wy_ref
+    pn_ref, stat_ref, ng_ref, heads_ref, got_ref, pair_ref, o_ref, wz_ref, wy_ref
 ):
-    c, z, y = place_bits()
+    c, half = place_bits()
     pn = jnp.sum(pn_ref[:, :PN].astype(F32), axis=0)
     extra = jnp.sum(pn_ref[:, PN:].astype(F32), axis=0)
     gain_row = jnp.concatenate([extra[t : t + 1] for t in range(10)], axis=1)
     bias_row = jnp.concatenate([extra[t : t + 1] for t in range(10, 20)], axis=1)
-    wz = own_rows(c, z, None, ng_ref, heads_ref) + part_rows(got_ref, z)
-    wz = wz + gz_ref[...].astype(F32)
-    wz = jnp.concatenate([wz, gain_row, bias_row, jnp.zeros((6, D), F32)], axis=0)
+    wg = half_rows(c, half, ng_ref, heads_ref, got_ref) + pair_ref[...].astype(F32)
+    wz = jnp.concatenate([wg[:HD], gain_row, bias_row, jnp.zeros((6, D), F32)], axis=0)
     wz_ref[:, : HD + 8] = wz.T
-    wy = own_rows(c, 2, y, ng_ref, heads_ref) + part_rows(got_ref, 2 + y)
-    wy_ref[:, :HD] = (wy + gy_ref[...].astype(F32)).T
+    wy_ref[:, :HD] = wg[HD:].T
     slabs = []
     for i in range(10):
         rows = pl.ds(i, R, stride=10)
@@ -241,11 +236,8 @@
     i_ref[...] = rows[QW:]
     row = sub((16, 2 * R))
     src = lane((16, 2 * R)) // 2
-    half = (row // 2) % 2
-    c_ok = src % 2 == row % 2
-    z_ok = (src // 2) % 2 == half
-    y_ok = (src // 16) % 2 == half
-    mask = ((row < 4) & c_ok & z_ok) | ((row >= 4) & (row < 8) & c_ok & y_ok) | (row == 8)
+    half = jnp.where(src % 2 == 0, (src // 2) % 2, (src // 16) % 2)
+    mask = (row == 2 * half + src % 2) | (row == 8)
     first = lane((16, 2 * R)) % 2 == 0
     sums = jnp.concatenate(
         [
@@ -257,19 +249,19 @@
     for i in range(10):
         at = i * STEP
         a_ref[i, 0] = sums[0:2, at : at + HD]
-        a_ref[i, 1] = sums[2:4, at : at + HD]
+        a_ref[i, 1] = sums[0:2, at + HD + 2 : at + STEP]
+        a_ref[i, 2] = sums[2:4, at : at + HD]
+        w_ref[i] = sums[2:4, at + HD + 2 : at + STEP]
         gain_ref[:, i : i + 1] = sums[8:9, at + HD : at + HD + 1]
         bias_ref[:, i : i + 1] = sums[8:9, at + HD + 1 : at + HD + 2]
-        a_ref[i, 2] = sums[4:6, at + HD + 2 : at + STEP]
-        w_ref[i] = sums[6:8, at + HD + 2 : at + STEP]
 
 
 def local(patches, cotangent, send_order, recv_order, segment_ids, ln_gain, ln_bias, w_qkv, w_out):
     wq = w_qkv.transpose(1, 2, 3, 0).reshape(NQ, D)
     wo = w_out.reshape(NO, D)
 
-    def swap(a, bit):
-        return lax.ppermute(a, "dp", [(i, i ^ bit) for i in range(128)])
+    def swap(a, other):
+        return lax.ppermute(a, "dp", [(i, other(i)) for i in range(128)])
 
     xg = jnp.concatenate([patches, cotangent], axis=0)
     xg, same, gain, bias, wo = call(
@@ -289,19 +281,14 @@
         xg, same, gain, bias, wo, wq,
     )
     (send,) = call(other_body, [((4 * HD, D), BF)], ng, heads)
-    got = swap(send, 1)
+    got = swap(send, lambda i: i ^ 1)
     pn = lax.all_to_all(pn, "zero", 0, 0, tiled=True)
-    sz, sy = call(
-        pair_body,
-        [((HD, D), BF), ((HD, D), BF)],
-        ng, heads, got,
-    )
-    gz = swap(sz, 2)
-    gy = swap(sy, 16)
+    (pair,) = call(pair_body, [((2 * HD, D), BF)], ng, heads, got)
+    pair = swap(pair, partner)
     (back,) = call(
         post_body,
         [((R, 2, HALF), BF)],
-        pn, stat, ng, heads, got, gz, gy,
+        pn, stat, ng, heads, got, pair,
         scratch=[pltpu.VMEM((D, R), F32)] * 2,
     )
     back = lax.all_to_all(back, "dp", 0, 0, tiled=True)

time: 96 us -> 94.9 us (0.989)
  waiting for transfers between devices: 6.03 us -> 8.24 us
  starting transfers between devices: 12.5 us -> 10.4 us
    all_to_all x1, waiting for transfers between devices: 6.02 us -> 8.24 us  [local(): pn = lax.all_to_all(pn, 'zero', 0, 0, tiled=True)]
    ppermute x3 -> x2, starting transfers between devices: 8.52 us -> 6.33 us  [swap(): return lax.ppermute(a, 'dp', [(i, other(i)) for i in range(128)])]
  transfers between devices with their start and end apart: 4 -> 3, of which waited for: 1 -> 1; matrix products, arithmetic and copies ran while one was open for 0% -> 0% of each run, Pallas kernels for 0% -> 0%
where the time goes in v8:
time: 94.9 us; the launch traced here: 94.6 us
  blocking collectives  67.2 us (71%)
  starting transfers between devices  10.4 us (11%)
  waiting for transfers between devices  8.24 us (9%)
  Pallas kernels  6.76 us (7%)
  other arithmetic  1.16 us (1%)
    all_to_all x1, blocking collectives, local(): xg = lax.all_to_all(xg, 'dp', 0, 0, tiled=True)  40.5 us
    all_to_all x1, blocking collectives, local(): back = lax.all_to_all(back, 'dp', 0, 0, tiled=True)  26.6 us
    all_to_all x1, waiting for transfers between devices, local(): pn = lax.all_to_all(pn, 'zero', 0, 0, tiled=True)  8.24 us
    pallas_call x6, Pallas kernels, call(): pl.pallas_call(body, out_shape=tuple((jax.ShapeDtypeStruct(s, d) for s, d...  6.76 us
    ppermute x2, starting transfers between devices, swap(): return lax.ppermute(a, 'dp', [(i, other(i)) for i in range(128)])  6.33 us
    all_to_all x1, starting transfers between devices, local(): pn = lax.all_to_all(pn, 'zero', 0, 0, tiled=True)  4.02 us
  transfers between devices with their start and end apart: 3, of which 1 were waited for; matrix products, arithmetic and copies ran while one was open for 0% of the time, Pallas kernels for 0%

profile of v8, /device:TPU:1, one launch (start us, length us, event | category | flops | bytes accessed | tf_op | source)
XLA Modules:
  0.0 94.6 jit_solution(8439169339963689636)
XLA Ops:
  0.6 0.0 copy-start.5
  0.6 0.0 copy-start.2
  0.7 0.0 copy-start.4
  0.7 0.0 copy-start.3
  0.7 0.0 copy-start.7
  0.7 0.0 copy-start.6
  0.7 1.2 %pad_maximum_fusion.xg_ref = bf16[256,1280]{1,0:T(8,128)(2,1)S(1)} fusion(bf16[128,1280]{1,0:T(8,128)(2,1)} %param.10, bf16[128,1280]{1,0:T(8,128)(2,1)} %param.9), kind=kLoop, calls=%fused_computation | loop fusion | flops 1310720 | bytes 1310720 | tf_op jit(solution)/shard_map/concatenate | solution.py:266
  1.9 0.0 copy-start
  1.9 0.0 copy-done.5
  1.9 0.0 copy-done.2
  1.9 0.0 copy-done.4
  1.9 0.0 copy-done.3
  1.9 0.0 copy-done.7
  1.9 0.0 copy-done.6
  1.9 0.6 shard_map.136
  2.5 40.5 %all_to_all.15.xg_ref = bf16[128,2,1280]{2,1,0:T(2,128)(2,1)S(1)} all-to-all(bf16[128,2,1280]{2,1,0:T(2,128)(2,1)S(1)} %get-tuple-element.21), channel_id=1, replica_groups=mesh['dp'=128,'zero'=4] {'dp'}, dimensions={0} | all-to-all | bytes 1310720 | tf_op jit(solution)/shard_map/all_to_all | solution.py:272
  43.0 0.0 copy-done
  43.0 3.1 %shard_map.137 = (bf16[4,672,128]{2,1,0:T(8,128)(2,1)S(1)}, bf16[256,1280]{1,0:T(8,128)(2,1)S(1)}, bf16[1408,128]{1,0:T(8,128)(2,1)S(1)}, f32[136,384]{1,0:T(8,128)S(1)}) custom-call(bf16[128,2,1280]{2,1,0:T(2,128)(2,1)S(1)} %all_to_all.15.xg_ref, f32[128,128]{1,0:T(8,128)S(1)} %get-tuple-element.22.same_ref, f32[1,1280]{1,0:T(1,128)S(1)} %get-tuple-element.23.gain_ref, ...), custom_call_target="tpu_custom_call" | custom-call | tf_op jit(solution)/shard_map/pallas_call | solution.py:32
  46.1 0.0 copy-start.1
  46.1 0.4 shard_map.138
  46.5 3.8 %collective-permute-start = (bf16[320,1280]{1,0:T(8,128)(2,1)S(1)}, bf16[320,1280]{1,0:T(8,128)(2,1)S(1)}, u32[]{:S(2)}, u32[]{:S(2)}) collective-permute-start(bf16[320,1280]{1,0:T(8,128)(2,1)S(1)} %shard_map.138), channel_id=1, source_target_pairs={{0,4},{4,0},{8,12},{12,8},{16,20},{20,16},{24,28},{28,24},{32,36},... | collective-permute-start | bytes 2457608 | tf_op jit(solution)/shard_map/ppermute | solution.py:264
  50.3 0.0 copy-done.1
  50.3 4.0 %all-to-all-start.1 = ((bf16[4,672,128]{2,1,0:T(8,128)(2,1)}), bf16[4,672,128]{2,1,0:T(8,128)(2,1)S(1)}, u32[]{:S(2)}, u32[]{:S(2)}) async-start(bf16[4,672,128]{2,1,0:T(8,128)(2,1)} %copy-done.1), calls=%async_computation.1 | async-start | bytes 1376256 | tf_op jit(solution)/shard_map/all_to_all | solution.py:285
  54.3 0.0 collective-permute-done.got_ref
  54.3 0.3 shard_map.139
  54.6 2.5 %collective-permute-start.1 = (bf16[160,1280]{1,0:T(8,128)(2,1)S(1)}, bf16[160,1280]{1,0:T(8,128)(2,1)S(1)}, u32[]{:S(2)}, u32[]{:S(2)}) collective-permute-start(bf16[160,1280]{1,0:T(8,128)(2,1)S(1)} %shard_map.139), channel_id=1, source_target_pairs={{0,8},{4,68},{8,0},{12,76},{16,24},{20,84},{24,16},{28,92},{32,40}... | collective-permute-start | bytes 1228808 | tf_op jit(solution)/shard_map/ppermute | solution.py:264
  57.2 8.2 %all-to-all-done.1.pn_ref = bf16[4,672,128]{2,1,0:T(8,128)(2,1)S(1)} async-done(((bf16[4,672,128]{2,1,0:T(8,128)(2,1)}), bf16[4,672,128]{2,1,0:T(8,128)(2,1)S(1)}, u32[]{:S(2)}, u32[]{:S(2)}) %all-to-all-start.1) | async-done | bytes 688160 | tf_op jit(solution)/shard_map/all_to_all | solution.py:285
  65.4 0.0 collective-permute-done.1.pair_ref
  65.4 1.3 %shard_map.140 = bf16[128,2,1152]{2,1,0:T(2,128)(2,1)S(1)} custom-call(bf16[4,672,128]{2,1,0:T(8,128)(2,1)S(1)} %all-to-all-done.1.pn_ref, f32[136,384]{1,0:T(8,128)S(1)} %get-tuple-element.27.stat_ref, bf16[256,1280]{1,0:T(8,128)(2,1)S(1)} %get-tuple-element.28.ng_ref, bf16[1408,128]{1,0:T(8,128)(2,1)S(1)} %get-tuple-element.29.heads_ref, ...), custom_call_target="tpu_custom_call" | custom-call | tf_op jit(solution)/shard_map/pallas_call | solution.py:32
  66.8 26.6 %all_to_all.16.b_ref = bf16[128,2,1152]{2,1,0:T(2,128)(2,1)S(1)} all-to-all(bf16[128,2,1152]{2,1,0:T(2,128)(2,1)S(1)} %shard_map.140), channel_id=1, replica_groups=mesh['dp'=128,'zero'=4] {'dp'}, dimensions={0} | all-to-all | bytes 1179648 | tf_op jit(solution)/shard_map/all_to_all | solution.py:294
  93.4 1.2 %shard_map.141 = (bf16[320,128]{1,0:T(8,128)(2,1)}, bf16[320,128]{1,0:T(8,128)(2,1)}, f32[10,3,2,80]{3,2,1,0:T(2,128)}, f32[10,2,80]{2,1,0:T(2,128)}, f32[1,10]{1,0:T(1,128)}, /*index=5*/f32[1,10]{1,0:T(1,128)}) custom-call(s32[1,128]{1,0:T(1,128)S(1)} %copy-done.5, bf16[128,2,1152]{2,1,0:T(2,128)(2,1)S(1)} %all_to_all.16.b_ref), custom_call_target="tpu_custom_call" | custom-call | tf_op jit(solution)/shard_map/pallas_call | solution.py:32
Async XLA Ops:
  0.6 1.2 %copy-start.5 = (s32[1,128]{1,0:T(1,128)S(1)}, s32[1,128]{1,0:T(1,128)}, u32[]{:S(2)}) copy-start(s32[1,128]{1,0:T(1,128)} %send_ref.3) | copy-start | bytes 1540
  0.6 1.2 %copy-start.2 = (bf16[2,80,1280]{2,1,0:T(8,128)(2,1)S(1)}, bf16[2,80,1280]{2,1,0:T(8,128)(2,1)}, u32[]{:S(2)}) copy-start(bf16[2,80,1280]{2,1,0:T(8,128)(2,1)} %param.17) | copy-start | bytes 1228804
  0.7 1.2 %copy-start.4 = (f32[1280]{0:T(1024)S(1)}, f32[1280]{0:T(1024)}, u32[]{:S(2)}) copy-start(f32[1280]{0:T(1024)} %bias_ref.1) | copy-start | bytes 15364
  0.7 1.2 %copy-start.3 = (f32[1280]{0:T(1024)S(1)}, f32[1280]{0:T(1024)}, u32[]{:S(2)}) copy-start(f32[1280]{0:T(1024)} %gain_ref.1) | copy-start | bytes 15364
  0.7 1.2 %copy-start.7 = (s32[1,128]{1,0:T(1,128)S(1)}, s32[1,128]{1,0:T(1,128)}, u32[]{:S(2)}) copy-start(s32[1,128]{1,0:T(1,128)} %seg_ref.1) | copy-start | bytes 1540
  0.7 1.2 %copy-start.6 = (s32[1,128]{1,0:T(1,128)S(1)}, s32[1,128]{1,0:T(1,128)}, u32[]{:S(2)}) copy-start(s32[1,128]{1,0:T(1,128)} %recv_ref.1) | copy-start | bytes 1540
  1.9 41.2 %copy-start = (bf16[1280,2,3,80]{0,3,2,1:T(8,128)(2,1)S(1)}, bf16[1280,2,3,80]{0,3,2,1:T(8,128)(2,1)}, u32[]{:S(2)}) copy-start(bf16[1280,2,3,80]{0,3,2,1:T(8,128)(2,1)} %param.16) | copy-start | bytes 3686404
  46.1 4.2 %copy-start.1 = (bf16[4,672,128]{2,1,0:T(8,128)(2,1)}, bf16[4,672,128]{2,1,0:T(8,128)(2,1)S(1)}, u32[]{:S(2)}) copy-start(bf16[4,672,128]{2,1,0:T(8,128)(2,1)S(1)} %get-tuple-element.26) | copy-start | bytes 2064388
  46.5 7.8 %collective-permute-start = (bf16[320,1280]{1,0:T(8,128)(2,1)S(1)}, bf16[320,1280]{1,0:T(8,128)(2,1)S(1)}, u32[]{:S(2)}, u32[]{:S(2)}) collective-permute-start(bf16[320,1280]{1,0:T(8,128)(2,1)S(1)} %shard_map.138), channel_id=1, source_target_pairs={{0,4},{4,0},{8,12},{12,8},{16,20},{20,16},{24,28},{28,24},{32,36},... | collective-permute-start | bytes 2457608 | tf_op jit(solution)/shard_map/ppermute | solution.py:264
  50.3 15.1 %all-to-all-start.1 = ((bf16[4,672,128]{2,1,0:T(8,128)(2,1)}), bf16[4,672,128]{2,1,0:T(8,128)(2,1)S(1)}, u32[]{:S(2)}, u32[]{:S(2)}) async-start(bf16[4,672,128]{2,1,0:T(8,128)(2,1)} %copy-done.1), calls=%async_computation.1 | async-start | bytes 1376256 | tf_op jit(solution)/shard_map/all_to_all | solution.py:285
  54.6 10.8 %collective-permute-start.1 = (bf16[160,1280]{1,0:T(8,128)(2,1)S(1)}, bf16[160,1280]{1,0:T(8,128)(2,1)S(1)}, u32[]{:S(2)}, u32[]{:S(2)}) collective-permute-start(bf16[160,1280]{1,0:T(8,128)(2,1)S(1)} %shard_map.139), channel_id=1, source_target_pairs={{0,8},{4,68},{8,0},{12,76},{16,24},{20,84},{24,16},{28,92},{32,40}... | collective-permute-start | bytes 1228808 | tf_op jit(solution)/shard_map/ppermute | solution.py:264

commit v9 on v8

--- a/solution.py
+++ b/solution.py
@@ -17,9 +17,9 @@
 F32 = jnp.float32
 BF = jnp.bfloat16
 PN = 5 * R
-PNE = PN + 32
-STEP = 2 * HD + 2
-WG = 1664
+PNE = PN + 48
+SUMS = 20 * HD
+WG = SUMS + 64
 HALF = (WG + 2 * QW) // 2
 
 
@@ -70,11 +70,17 @@
     return one_hot(hit & (odd == 0)), one_hot(hit & (odd == 1))
 
 
+def high_low(value):
+    high = value.astype(BF).astype(F32)
+    return [high, value - high]
+
+
 def gather_body(
     send_ref, xg_ref, recv_ref, seg_ref, gain_ref, bias_ref, wo_ref,
-    o_ref, same_ref, gain_out, bias_out, wo_out,
+    o_ref, odd_ref, same_ref, gain_out, bias_out, wo_out,
 ):
     even, odd = pair_picks(send_ref)
+    odd_ref[...] = odd
     pick = jnp.concatenate([even, odd], axis=0)
     o_ref[...] = dg(pick, xg_ref[...], 0, 0).astype(BF).reshape(R, 2, D)
     hit = sub((R, R)) == recv_ref[...]
@@ -115,9 +121,11 @@
             both = jnp.concatenate([x[:, cols], pad, g32[:, cols], pad], axis=1).astype(BF)
             for t in range(6):
                 heads_ref[(5 + t) * R : (6 + t) * R] = both[:, t * R : (t + 1) * R]
-            stat_ref[R:, :QW] = jnp.broadcast_to(gain_ref[:, cols], (8, QW))
-
-    stat_ref[:R, :R] = jnp.where(lane((R, R)) < 64, mean, inv)
+            line = jnp.concatenate([gain_ref[:, cols], jnp.zeros((1, QP - QW), F32)], axis=1)
+            for t in range(3):
+                stat_ref[R + t : R + t + 1] = line[:, t * R : (t + 1) * R]
+
+    stat_ref[:R] = jnp.where(lane((R, R)) < 64, mean, inv)
     dh = dg(wo_ref[...], g, 1, 1).astype(BF)
     qkv = dg(wq_ref[...], normed, 1, 1).astype(BF)
     same = same_ref[...] > 0.5
@@ -151,13 +159,13 @@
     m2 = jnp.sum(u * xh, axis=1, keepdims=True) * (1.0 / D)
     gain_row = jnp.sum(n * xh, axis=0, keepdims=True)
     bias_row = jnp.sum(n, axis=0, keepdims=True)
-    extra = [r[:, t * R : (t + 1) * R] for r in (gain_row, bias_row) for t in range(10)]
+    extra = []
+    for row in high_low(gain_row) + high_low(bias_row):
+        extra += [row[:, t * R : (t + 1) * R] for t in range(10)]
     diagonal = sub((R, R)) == lane((R, R))
     for m in (m1, m2):
-        row = jnp.sum(jnp.where(diagonal, m, 0.0), axis=0, keepdims=True)
-        high = row.astype(BF).astype(F32)
-        extra += [high, row - high]
-    extra.append(jnp.zeros((8, R), F32))
+        extra += high_low(jnp.sum(jnp.where(diagonal, m, 0.0), axis=0, keepdims=True))
+    extra.append(jnp.zeros((PNE - PN - 44, R), F32))
     extra = jnp.concatenate(extra, axis=0).astype(BF)
     for i in range(4):
         at = i * QW
@@ -191,28 +199,35 @@
     send_ref[...] = half_rows(c, 1 - half, ng_ref, heads_ref, got_ref).astype(BF)
 
 
-def post_body(
-    pn_ref, stat_ref, ng_ref, heads_ref, got_ref, pair_ref, o_ref, wz_ref, wy_ref
-):
+def weights_body(ng_ref, heads_ref, got_ref, pair_ref, o_ref, first_ref, second_ref):
     c, half = place_bits()
-    pn = jnp.sum(pn_ref[:, :PN].astype(F32), axis=0)
-    extra = jnp.sum(pn_ref[:, PN:].astype(F32), axis=0)
-    gain_row = jnp.concatenate([extra[t : t + 1] for t in range(10)], axis=1)
-    bias_row = jnp.concatenate([extra[t : t + 1] for t in range(10, 20)], axis=1)
     wg = half_rows(c, half, ng_ref, heads_ref, got_ref) + pair_ref[...].astype(F32)
-    wz = jnp.concatenate([wg[:HD], gain_row, bias_row, jnp.zeros((6, D), F32)], axis=0)
-    wz_ref[:, : HD + 8] = wz.T
-    wy_ref[:, :HD] = wg[HD:].T
+    first_ref[:, :HD] = wg[:HD].T
+    second_ref[:, :HD] = wg[HD:].T
     slabs = []
     for i in range(10):
         rows = pl.ds(i, R, stride=10)
-        slabs += [wz_ref[rows, :][:, : HD + 2], wy_ref[rows, :][:, :HD]]
-    slabs.append(jnp.zeros((R, WG - 10 * STEP), F32))
+        slabs += [first_ref[rows, :][:, :HD], second_ref[rows, :][:, :HD]]
+    slabs.append(jnp.zeros((R, 2 * HALF - SUMS), F32))
+    row = jnp.concatenate(slabs, axis=1).astype(BF)
+    both = jnp.concatenate([row[:, :HALF], row[:, HALF:]], axis=0)
+    out = sub((2 * R, 2 * R))
+    both = dg(one_hot(lane((2 * R, 2 * R)) == out // 2 + R * (out % 2)), both, 1, 0)
+    o_ref[...] = both.astype(BF)
+
+
+def post_body(pn_ref, stat_ref, heads_ref, wg_ref, o_ref, sum_ref):
+    pn = jnp.sum(pn_ref[:, :PN].astype(F32), axis=0)
+    extra = jnp.sum(pn_ref[:, PN:].astype(F32), axis=0)
+    sums = [jnp.concatenate([extra[t : t + 1] for t in range(k, k + 10)], axis=1) for k in (0, 10, 20, 30)]
+    rows = high_low(sums[0] + sums[1]) + high_low(sums[2] + sums[3])
+    sum_ref[:, :8] = jnp.concatenate(rows + [jnp.zeros((4, D), F32)], axis=0).T
+    sums = [sum_ref[pl.ds(i, R, stride=10), :][:, :4] for i in range(10)]
     tiles = [pn[t * R : (t + 1) * R] for t in range(5)]
     both = jnp.concatenate(tiles, axis=1)
     diagonal = sub((R, R)) == lane((R, R))
-    m1 = jnp.sum(jnp.where(diagonal, extra[20:21] + extra[21:22], 0.0), axis=1, keepdims=True)
-    m2 = jnp.sum(jnp.where(diagonal, extra[22:23] + extra[23:24], 0.0), axis=1, keepdims=True)
+    m1 = jnp.sum(jnp.where(diagonal, extra[40:41] + extra[41:42], 0.0), axis=1, keepdims=True)
+    m2 = jnp.sum(jnp.where(diagonal, extra[42:43] + extra[43:44], 0.0), axis=1, keepdims=True)
     quarters = [heads_ref[(5 + t) * R : (6 + t) * R].astype(F32) for t in range(6)]
     x = jnp.concatenate(quarters[:3], axis=1)[:, :QW]
     g = jnp.concatenate(quarters[3:], axis=1)[:, :QW]
@@ -220,18 +235,20 @@
     inv = stat_ref[:R, 64:65]
     xh = (x - mean) * inv
     enc = x + both[:, :QW]
-    grad = both[:, QW:] * stat_ref[R : R + 1, :QW] - m1 - xh * m2
+    gain = jnp.concatenate([stat_ref[R + t : R + t + 1] for t in range(3)], axis=1)[:, :QW]
+    grad = both[:, QW:] * gain - m1 - xh * m2
     grad = g + inv * grad
-    row = jnp.concatenate(slabs + [enc, grad], axis=1).astype(BF)
-    at = sub((2 * R, R)) - 2 * lane((2 * R, R))
-    both = dg(one_hot(at == 0), row[:, :HALF], 1, 0) + dg(one_hot(at == 1), row[:, HALF:], 1, 0)
-    o_ref[...] = both.astype(BF).reshape(R, 2, HALF)
-
-
-def final_body(send_ref, b_ref, e_ref, i_ref, a_ref, w_ref, gain_ref, bias_ref):
-    _, odd = pair_picks(send_ref)
+    at = SUMS - HALF - 64
+    gap = jnp.zeros((R, 64), F32)
+    row = jnp.concatenate([gap] + sums + [gap[:, :24], enc, grad], axis=1).astype(BF)
+    odd = one_hot(sub((2 * R, R)) == 2 * lane((2 * R, R)) + 1)
+    tail = dg(odd, row, 1, 0) + wg_ref[:, at:].astype(F32)
+    o_ref[...] = jnp.concatenate([wg_ref[:, :at], tail.astype(BF)], axis=1).reshape(R, 2, HALF)
+
+
+def final_body(odd_ref, b_ref, e_ref, i_ref, a_ref, w_ref, gain_ref, bias_ref):
     back = b_ref[...].reshape(2 * R, HALF)
-    rows = dg(back[:, WG - HALF :], odd, 0, 1).astype(BF)
+    rows = dg(back[:, WG - HALF :], odd_ref[...], 0, 1).astype(BF)
     e_ref[...] = rows[:QW]
     i_ref[...] = rows[QW:]
     row = sub((16, 2 * R))
@@ -247,13 +264,14 @@
         axis=1,
     )
     for i in range(10):
-        at = i * STEP
+        at = i * 2 * HD
         a_ref[i, 0] = sums[0:2, at : at + HD]
-        a_ref[i, 1] = sums[0:2, at + HD + 2 : at + STEP]
+        a_ref[i, 1] = sums[0:2, at + HD : at + 2 * HD]
         a_ref[i, 2] = sums[2:4, at : at + HD]
-        w_ref[i] = sums[2:4, at + HD + 2 : at + STEP]
-        gain_ref[:, i : i + 1] = sums[8:9, at + HD : at + HD + 1]
-        bias_ref[:, i : i + 1] = sums[8:9, at + HD + 1 : at + HD + 2]
+        w_ref[i] = sums[2:4, at + HD : at + 2 * HD]
+        at = SUMS + 4 * i
+        gain_ref[:, i : i + 1] = sums[8:9, at : at + 1] + sums[8:9, at + 1 : at + 2]
+        bias_ref[:, i : i + 1] = sums[8:9, at + 2 : at + 3] + sums[8:9, at + 3 : at + 4]
 
 
 def local(patches, cotangent, send_order, recv_order, segment_ids, ln_gain, ln_bias, w_qkv, w_out):
@@ -264,9 +282,9 @@
         return lax.ppermute(a, "dp", [(i, other(i)) for i in range(128)])
 
     xg = jnp.concatenate([patches, cotangent], axis=0)
-    xg, same, gain, bias, wo = call(
+    xg, odd, same, gain, bias, wo = call(
         gather_body,
-        [((R, 2, D), BF), ((R, R), F32), ((1, D), F32), ((1, D), F32), ((NO, D), BF)],
+        [((R, 2, D), BF), ((R, 2 * R), BF), ((R, R), F32), ((1, D), F32), ((1, D), F32), ((NO, D), BF)],
         send_order, xg, recv_order, segment_ids, ln_gain, ln_bias, wo,
     )
     xg = lax.all_to_all(xg, "dp", 0, 0, tiled=True)
@@ -276,7 +294,7 @@
             ((4, PNE, R), BF),
             ((2 * R, D), BF),
             ((8 * HD + 6 * R, R), BF),
-            ((R + 8, QP), F32),
+            ((R + 8, R), F32),
         ],
         xg, same, gain, bias, wo, wq,
     )
@@ -285,11 +303,12 @@
     pn = lax.all_to_all(pn, "zero", 0, 0, tiled=True)
     (pair,) = call(pair_body, [((2 * HD, D), BF)], ng, heads, got)
     pair = swap(pair, partner)
+    scratch = pltpu.VMEM((D, R), F32)
+    (wg,) = call(
+        weights_body, [((2 * R, HALF), BF)], ng, heads, got, pair, scratch=[scratch] * 2
+    )
     (back,) = call(
-        post_body,
-        [((R, 2, HALF), BF)],
-        pn, stat, ng, heads, got, pair,
-        scratch=[pltpu.VMEM((D, R), F32)] * 2,
+        post_body, [((R, 2, HALF), BF)], pn, stat, heads, wg, scratch=[scratch]
     )
     back = lax.all_to_all(back, "dp", 0, 0, tiled=True)
     enc, grad, qkv_share, out_share, gain_grad, bias_grad = call(
@@ -302,7 +321,7 @@
             ((1, 10), F32),
             ((1, 10), F32),
         ],
-        send_order, back,
+        odd, back,
     )
     return (
         enc.T,

time: 94.9 us -> 94.6 us (level)
    all_to_all x1, waiting for transfers between devices: 8.24 us -> 0.94 us  [local(): pn = lax.all_to_all(pn, 'zero', 0, 0, tiled=True)]
    ppermute x2, waiting for transfers between devices: 0.01 us -> 6.44 us  [swap(): return lax.ppermute(a, 'dp', [(i, other(i)) for i in range(128)])]
    pallas_call x6 -> x7, Pallas kernels: 6.76 us -> 7.36 us  [call(): pl.pallas_call(body, out_shape=tuple((jax.ShapeDtypeStruct(s, d) for s, d...]
  transfers between devices with their start and end apart: 3 -> 3, of which waited for: 1 -> 2; matrix products, arithmetic and copies ran while one was open for 0% -> 0% of each run, Pallas kernels for 0% -> 1%
where the time goes in v9:
time: 94.6 us; the launch traced here: 94.3 us
  blocking collectives  67.2 us (71%)
  starting transfers between devices  10.3 us (11%)
  waiting for transfers between devices  7.39 us (8%)
  Pallas kernels  7.36 us (8%)
  other arithmetic  1.16 us (1%)
    all_to_all x1, blocking collectives, local(): xg = lax.all_to_all(xg, 'dp', 0, 0, tiled=True)  40.6 us
    all_to_all x1, blocking collectives, local(): back = lax.all_to_all(back, 'dp', 0, 0, tiled=True)  26.6 us
    pallas_call x7, Pallas kernels, call(): pl.pallas_call(body, out_shape=tuple((jax.ShapeDtypeStruct(s, d) for s, d...  7.36 us
    ppermute x2, waiting for transfers between devices, swap(): return lax.ppermute(a, 'dp', [(i, other(i)) for i in range(128)])  6.44 us
    ppermute x2, starting transfers between devices, swap(): return lax.ppermute(a, 'dp', [(i, other(i)) for i in range(128)])  6.34 us
    all_to_all x1, starting transfers between devices, local(): pn = lax.all_to_all(pn, 'zero', 0, 0, tiled=True)  4.01 us
  transfers between devices with their start and end apart: 3, of which 2 were waited for; matrix products, arithmetic and copies ran while one was open for 0% of the time, Pallas kernels for 1%

profile of v9, /device:TPU:1, one launch (start us, length us, event | category | flops | bytes accessed | tf_op | source)
XLA Modules:
  0.0 94.3 jit_solution(17299962537003463123)
XLA Ops:
  0.6 0.0 copy-start.2
  0.6 0.0 copy-start.4
  0.7 0.0 copy-start.3
  0.7 0.0 copy-start.7
  0.7 0.0 copy-start.6
  0.7 0.0 copy-start.5
  0.7 1.2 %pad_maximum_fusion.xg_ref = bf16[256,1280]{1,0:T(8,128)(2,1)S(1)} fusion(bf16[128,1280]{1,0:T(8,128)(2,1)} %param.10, bf16[128,1280]{1,0:T(8,128)(2,1)} %param.9), kind=kLoop, calls=%fused_computation | loop fusion | flops 1310720 | bytes 1310720 | tf_op jit(solution)/shard_map/concatenate | solution.py:284
  1.9 0.0 copy-start
  1.9 0.0 copy-done.2
  1.9 0.0 copy-done.4
  1.9 0.0 copy-done.3
  1.9 0.0 copy-done.7
  1.9 0.0 copy-done.6
  1.9 0.0 copy-done.5
  1.9 0.6 shard_map.136
  2.5 40.6 %all_to_all.15.xg_ref = bf16[128,2,1280]{2,1,0:T(2,128)(2,1)S(1)} all-to-all(bf16[128,2,1280]{2,1,0:T(2,128)(2,1)S(1)} %get-tuple-element.23), channel_id=1, replica_groups=mesh['dp'=128,'zero'=4] {'dp'}, dimensions={0} | all-to-all | bytes 1310720 | tf_op jit(solution)/shard_map/all_to_all | solution.py:290
  43.0 0.0 copy-done
  43.0 3.1 %shard_map.137 = (bf16[4,688,128]{2,1,0:T(8,128)(2,1)S(1)}, bf16[256,1280]{1,0:T(8,128)(2,1)S(1)}, bf16[1408,128]{1,0:T(8,128)(2,1)S(1)}, f32[136,128]{1,0:T(8,128)S(1)}) custom-call(bf16[128,2,1280]{2,1,0:T(2,128)(2,1)S(1)} %all_to_all.15.xg_ref, f32[128,128]{1,0:T(8,128)S(1)} %get-tuple-element.24.same_ref, f32[1,1280]{1,0:T(1,128)S(1)} %get-tuple-element.25.gain_ref, ...), custom_call_target="tpu_custom_call" | custom-call | tf_op jit(solution)/shard_map/pallas_call | solution.py:32
  46.1 0.0 copy-start.1
  46.1 0.4 shard_map.138
  46.5 3.8 %collective-permute-start = (bf16[320,1280]{1,0:T(8,128)(2,1)S(1)}, bf16[320,1280]{1,0:T(8,128)(2,1)S(1)}, u32[]{:S(2)}, u32[]{:S(2)}) collective-permute-start(bf16[320,1280]{1,0:T(8,128)(2,1)S(1)} %shard_map.138), channel_id=1, source_target_pairs={{0,4},{4,0},{8,12},{12,8},{16,20},{20,16},{24,28},{28,24},{32,36},... | collective-permute-start | bytes 2457608 | tf_op jit(solution)/shard_map/ppermute | solution.py:282
  50.3 0.0 copy-done.1
  50.3 4.0 %all-to-all-start.1 = ((bf16[4,688,128]{2,1,0:T(8,128)(2,1)}), bf16[4,688,128]{2,1,0:T(8,128)(2,1)S(1)}, u32[]{:S(2)}, u32[]{:S(2)}) async-start(bf16[4,688,128]{2,1,0:T(8,128)(2,1)} %copy-done.1), calls=%async_computation.1 | async-start | bytes 1409024 | tf_op jit(solution)/shard_map/all_to_all | solution.py:303
  54.3 0.0 collective-permute-done.got_ref
  54.3 0.3 shard_map.139
  54.6 2.5 %collective-permute-start.1 = (bf16[160,1280]{1,0:T(8,128)(2,1)S(1)}, bf16[160,1280]{1,0:T(8,128)(2,1)S(1)}, u32[]{:S(2)}, u32[]{:S(2)}) collective-permute-start(bf16[160,1280]{1,0:T(8,128)(2,1)S(1)} %shard_map.139), channel_id=1, source_target_pairs={{0,8},{4,68},{8,0},{12,76},{16,24},{20,84},{24,16},{28,92},{32,40}... | collective-permute-start | bytes 1228808 | tf_op jit(solution)/shard_map/ppermute | solution.py:282
  57.2 6.4 %collective-permute-done.1.pair_ref = bf16[160,1280]{1,0:T(8,128)(2,1)S(1)} collective-permute-done((bf16[160,1280]{1,0:T(8,128)(2,1)S(1)}, bf16[160,1280]{1,0:T(8,128)(2,1)S(1)}, u32[]{:S(2)}, u32[]{:S(2)}) %collective-permute-start.1) | collective-permute-done | bytes 409632 | tf_op jit(solution)/shard_map/ppermute | solution.py:282
  63.6 1.0 %shard_map.140.wg_ref = bf16[256,1152]{1,0:T(8,128)(2,1)S(1)} custom-call(bf16[256,1280]{1,0:T(8,128)(2,1)S(1)} %get-tuple-element.31.ng_ref, bf16[1408,128]{1,0:T(8,128)(2,1)S(1)} %get-tuple-element.30.heads_ref, bf16[320,1280]{1,0:T(8,128)(2,1)S(1)} %collective-permute-done.got_ref, bf16[160,1280]{1,0:T(8,128)(2,1)S(1)} %collective-permute-done.1.pair_ref), custom_call_target="tpu_custom_call" | custom-call | tf_op jit(solution)/shard_map/pallas_call | solution.py:32
  64.6 0.9 %all-to-all-done.1.pn_ref = bf16[4,688,128]{2,1,0:T(8,128)(2,1)S(1)} async-done(((bf16[4,688,128]{2,1,0:T(8,128)(2,1)}), bf16[4,688,128]{2,1,0:T(8,128)(2,1)S(1)}, u32[]{:S(2)}, u32[]{:S(2)}) %all-to-all-start.1) | async-done | bytes 704544 | tf_op jit(solution)/shard_map/all_to_all | solution.py:303
  65.6 1.0 %shard_map.141 = bf16[128,2,1152]{2,1,0:T(2,128)(2,1)S(1)} custom-call(bf16[4,688,128]{2,1,0:T(8,128)(2,1)S(1)} %all-to-all-done.1.pn_ref, f32[136,128]{1,0:T(8,128)S(1)} %get-tuple-element.29.stat_ref, bf16[1408,128]{1,0:T(8,128)(2,1)S(1)} %get-tuple-element.30.heads_ref, bf16[256,1152]{1,0:T(8,128)(2,1)S(1)} %shard_map.140.wg_ref), custom_call_target="tpu_custom_call" | custom-call | tf_op jit(solution)/shard_map/pallas_call | solution.py:32
  66.5 26.6 %all_to_all.16.b_ref = bf16[128,2,1152]{2,1,0:T(2,128)(2,1)S(1)} all-to-all(bf16[128,2,1152]{2,1,0:T(2,128)(2,1)S(1)} %shard_map.141), channel_id=1, replica_groups=mesh['dp'=128,'zero'=4] {'dp'}, dimensions={0} | all-to-all | bytes 1179648 | tf_op jit(solution)/shard_map/all_to_all | solution.py:313
  93.2 1.1 %shard_map.142 = (bf16[320,128]{1,0:T(8,128)(2,1)}, bf16[320,128]{1,0:T(8,128)(2,1)}, f32[10,3,2,80]{3,2,1,0:T(2,128)}, f32[10,2,80]{2,1,0:T(2,128)}, f32[1,10]{1,0:T(1,128)}, /*index=5*/f32[1,10]{1,0:T(1,128)}) custom-call(bf16[128,256]{1,0:T(8,128)(2,1)S(1)} %get-tuple-element.22.odd_ref, bf16[128,2,1152]{2,1,0:T(2,128)(2,1)S(1)} %all_to_all.16.b_ref), custom_call_target="tpu_custom_call" | custom-call | tf_op jit(solution)/shard_map/pallas_call | solution.py:32
Async XLA Ops:
  0.6 1.2 %copy-start.2 = (bf16[2,80,1280]{2,1,0:T(8,128)(2,1)S(1)}, bf16[2,80,1280]{2,1,0:T(8,128)(2,1)}, u32[]{:S(2)}) copy-start(bf16[2,80,1280]{2,1,0:T(8,128)(2,1)} %param.17) | copy-start | bytes 1228804
  0.6 1.2 %copy-start.4 = (f32[1280]{0:T(1024)S(1)}, f32[1280]{0:T(1024)}, u32[]{:S(2)}) copy-start(f32[1280]{0:T(1024)} %bias_ref.1) | copy-start | bytes 15364
  0.7 1.2 %copy-start.3 = (f32[1280]{0:T(1024)S(1)}, f32[1280]{0:T(1024)}, u32[]{:S(2)}) copy-start(f32[1280]{0:T(1024)} %gain_ref.1) | copy-start | bytes 15364
  0.7 1.2 %copy-start.7 = (s32[1,128]{1,0:T(1,128)S(1)}, s32[1,128]{1,0:T(1,128)}, u32[]{:S(2)}) copy-start(s32[1,128]{1,0:T(1,128)} %seg_ref.1) | copy-start | bytes 1540
  0.7 1.2 %copy-start.6 = (s32[1,128]{1,0:T(1,128)S(1)}, s32[1,128]{1,0:T(1,128)}, u32[]{:S(2)}) copy-start(s32[1,128]{1,0:T(1,128)} %recv_ref.1) | copy-start | bytes 1540
  0.7 1.2 %copy-start.5 = (s32[1,128]{1,0:T(1,128)S(1)}, s32[1,128]{1,0:T(1,128)}, u32[]{:S(2)}) copy-start(s32[1,128]{1,0:T(1,128)} %send_ref.1) | copy-start | bytes 1540
  1.9 41.2 %copy-start = (bf16[1280,2,3,80]{0,3,2,1:T(8,128)(2,1)S(1)}, bf16[1280,2,3,80]{0,3,2,1:T(8,128)(2,1)}, u32[]{:S(2)}) copy-start(bf16[1280,2,3,80]{0,3,2,1:T(8,128)(2,1)} %param.16) | copy-start | bytes 3686404
  46.1 4.2 %copy-start.1 = (bf16[4,688,128]{2,1,0:T(8,128)(2,1)}, bf16[4,688,128]{2,1,0:T(8,128)(2,1)S(1)}, u32[]{:S(2)}) copy-start(bf16[4,688,128]{2,1,0:T(8,128)(2,1)S(1)} %get-tuple-element.28) | copy-start | bytes 2113540
  46.5 7.8 %collective-permute-start = (bf16[320,1280]{1,0:T(8,128)(2,1)S(1)}, bf16[320,1280]{1,0:T(8,128)(2,1)S(1)}, u32[]{:S(2)}, u32[]{:S(2)}) collective-permute-start(bf16[320,1280]{1,0:T(8,128)(2,1)S(1)} %shard_map.138), channel_id=1, source_target_pairs={{0,4},{4,0},{8,12},{12,8},{16,20},{20,16},{24,28},{28,24},{32,36},... | collective-permute-start | bytes 2457608 | tf_op jit(solution)/shard_map/ppermute | solution.py:282
  50.3 15.3 %all-to-all-start.1 = ((bf16[4,688,128]{2,1,0:T(8,128)(2,1)}), bf16[4,688,128]{2,1,0:T(8,128)(2,1)S(1)}, u32[]{:S(2)}, u32[]{:S(2)}) async-start(bf16[4,688,128]{2,1,0:T(8,128)(2,1)} %copy-done.1), calls=%async_computation.1 | async-start | bytes 1409024 | tf_op jit(solution)/shard_map/all_to_all | solution.py:303
  54.6 9.0 %collective-permute-start.1 = (bf16[160,1280]{1,0:T(8,128)(2,1)S(1)}, bf16[160,1280]{1,0:T(8,128)(2,1)S(1)}, u32[]{:S(2)}, u32[]{:S(2)}) collective-permute-start(bf16[160,1280]{1,0:T(8,128)(2,1)S(1)} %shard_map.139), channel_id=1, source_target_pairs={{0,8},{4,68},{8,0},{12,76},{16,24},{20,84},{24,16},{28,92},{32,40}... | collective-permute-start | bytes 1228808 | tf_op jit(solution)/shard_map/ppermute | solution.py:282

commit v10 on v9

--- a/solution.py
+++ b/solution.py
@@ -108,6 +108,7 @@
     x = dg(one_hot(at == 0), xg, 1, 0)
     g32 = dg(one_hot(at == 1), xg, 1, 0)
     g = g32.astype(BF)
+    dh = dg(wo_ref[...], g, 1, 1).astype(BF)
     ng_ref[R:, :] = g
     mean, inv, xh = norm_stats(x)
     normed = (xh * gain_ref[...] + bias_ref[...]).astype(BF)
@@ -126,26 +127,26 @@
                 stat_ref[R + t : R + t + 1] = line[:, t * R : (t + 1) * R]
 
     stat_ref[:R] = jnp.where(lane((R, R)) < 64, mean, inv)
-    dh = dg(wo_ref[...], g, 1, 1).astype(BF)
     qkv = dg(wq_ref[...], normed, 1, 1).astype(BF)
     same = same_ref[...] > 0.5
-    rows = []
-    for h in range(HG):
-        q = qkv[h * 3 * HD : h * 3 * HD + HD]
-        k = qkv[h * 3 * HD + HD : h * 3 * HD + 2 * HD]
-        v = qkv[h * 3 * HD + 2 * HD : (h + 1) * 3 * HD]
-        dhh = dh[h * HD : (h + 1) * HD]
-        s = jnp.where(same, dg(q, k, 0, 0) * (HD**-0.5), -1e30)
-        e = jnp.exp(s - jnp.max(s, axis=1, keepdims=True))
-        w = e / jnp.sum(e, axis=1, keepdims=True)
-        w16 = w.astype(BF)
-        pg = dg(dhh, v, 0, 0)
-        delta = jnp.sum(pg * w, axis=1, keepdims=True)
-        sg = (w * (pg - delta) * (HD**-0.5)).astype(BF)
-        rows.append(dg(k, sg, 1, 1).astype(BF))
-        rows.append(dg(q, sg, 1, 0).astype(BF))
-        rows.append(dg(dhh, w16, 1, 0).astype(BF))
-        rows.append(dg(v, w16, 1, 1).astype(BF))
+    heads = range(HG)
+    q = [qkv[h * 3 * HD : h * 3 * HD + HD] for h in heads]
+    k = [qkv[h * 3 * HD + HD : h * 3 * HD + 2 * HD] for h in heads]
+    v = [qkv[h * 3 * HD + 2 * HD : (h + 1) * 3 * HD] for h in heads]
+    dhh = [dh[h * HD : (h + 1) * HD] for h in heads]
+    s = [dg(q[h], k[h], 0, 0) for h in heads]
+    pg = [dg(dhh[h], v[h], 0, 0) for h in heads]
+    s = [jnp.where(same, s[h] * (HD**-0.5), -1e30) for h in heads]
+    e = [jnp.exp(s[h] - jnp.max(s[h], axis=1, keepdims=True)) for h in heads]
+    w = [e[h] / jnp.sum(e[h], axis=1, keepdims=True) for h in heads]
+    w16 = [w[h].astype(BF) for h in heads]
+    delta = [jnp.sum(pg[h] * w[h], axis=1, keepdims=True) for h in heads]
+    sg = [(w[h] * (pg[h] - delta[h]) * (HD**-0.5)).astype(BF) for h in heads]
+    ho = [dg(v[h], w16[h], 1, 1).astype(BF) for h in heads]
+    dv = [dg(dhh[h], w16[h], 1, 0).astype(BF) for h in heads]
+    dq = [dg(k[h], sg[h], 1, 1).astype(BF) for h in heads]
+    dk = [dg(q[h], sg[h], 1, 0).astype(BF) for h in heads]
+    rows = [part for h in heads for part in (dq[h], dk[h], dv[h], ho[h])]
     heads_ref[: 8 * HD] = jnp.concatenate(rows, axis=0)
     qg = jnp.concatenate(rows[0:3] + rows[4:7], axis=0)
     ho = jnp.concatenate([rows[3], rows[7]], axis=0)

time: 94.6 us -> 94.2 us (level)
  no operation moved by 1% of the time
where the time goes in v10:
time: 94.2 us; the launch traced here: 93.9 us
  blocking collectives  67.2 us (71%)
  starting transfers between devices  10.3 us (11%)
  waiting for transfers between devices  7.39 us (8%)
  Pallas kernels  6.97 us (7%)
  other arithmetic  1.16 us (1%)
    all_to_all x1, blocking collectives, local(): xg = lax.all_to_all(xg, 'dp', 0, 0, tiled=True)  40.6 us
    all_to_all x1, blocking collectives, local(): back = lax.all_to_all(back, 'dp', 0, 0, tiled=True)  26.6 us
    pallas_call x7, Pallas kernels, call(): pl.pallas_call(body, out_shape=tuple((jax.ShapeDtypeStruct(s, d) for s, d...  6.97 us
    ppermute x2, waiting for transfers between devices, swap(): return lax.ppermute(a, 'dp', [(i, other(i)) for i in range(128)])  6.45 us
    ppermute x2, starting transfers between devices, swap(): return lax.ppermute(a, 'dp', [(i, other(i)) for i in range(128)])  6.33 us
    all_to_all x1, starting transfers between devices, local(): pn = lax.all_to_all(pn, 'zero', 0, 0, tiled=True)  4.01 us
  transfers between devices with their start and end apart: 3, of which 2 were waited for; matrix products, arithmetic and copies ran while one was open for 0% of the time, Pallas kernels for 1%

profile of v10, /device:TPU:1, one launch (start us, length us, event | category | flops | bytes accessed | tf_op | source)
XLA Modules:
  0.0 93.9 jit_solution(17106076191649407715)
XLA Ops:
  0.6 0.0 copy-start.2
  0.6 0.0 copy-start.4
  0.7 0.0 copy-start.3
  0.7 0.0 copy-start.7
  0.7 0.0 copy-start.6
  0.7 0.0 copy-start.5
  0.7 1.2 %pad_maximum_fusion.xg_ref = bf16[256,1280]{1,0:T(8,128)(2,1)S(1)} fusion(bf16[128,1280]{1,0:T(8,128)(2,1)} %param.10, bf16[128,1280]{1,0:T(8,128)(2,1)} %param.9), kind=kLoop, calls=%fused_computation | loop fusion | flops 1310720 | bytes 1310720 | tf_op jit(solution)/shard_map/concatenate | solution.py:285
  1.9 0.0 copy-start
  1.9 0.0 copy-done.2
  1.9 0.0 copy-done.4
  1.9 0.0 copy-done.3
  1.9 0.0 copy-done.7
  1.9 0.0 copy-done.6
  1.9 0.0 copy-done.5
  1.9 0.6 shard_map.136
  2.5 40.6 %all_to_all.15.xg_ref = bf16[128,2,1280]{2,1,0:T(2,128)(2,1)S(1)} all-to-all(bf16[128,2,1280]{2,1,0:T(2,128)(2,1)S(1)} %get-tuple-element.23), channel_id=1, replica_groups=mesh['dp'=128,'zero'=4] {'dp'}, dimensions={0} | all-to-all | bytes 1310720 | tf_op jit(solution)/shard_map/all_to_all | solution.py:291
  43.0 0.0 copy-done
  43.0 2.7 %shard_map.137 = (bf16[4,688,128]{2,1,0:T(8,128)(2,1)S(1)}, bf16[256,1280]{1,0:T(8,128)(2,1)S(1)}, bf16[1408,128]{1,0:T(8,128)(2,1)S(1)}, f32[136,128]{1,0:T(8,128)S(1)}) custom-call(bf16[128,2,1280]{2,1,0:T(2,128)(2,1)S(1)} %all_to_all.15.xg_ref, f32[128,128]{1,0:T(8,128)S(1)} %get-tuple-element.24.same_ref, f32[1,1280]{1,0:T(1,128)S(1)} %get-tuple-element.25.gain_ref, ...), custom_call_target="tpu_custom_call" | custom-call | tf_op jit(solution)/shard_map/pallas_call | solution.py:32
  45.7 0.0 copy-start.1
  45.7 0.4 shard_map.138
  46.1 3.8 %collective-permute-start = (bf16[320,1280]{1,0:T(8,128)(2,1)S(1)}, bf16[320,1280]{1,0:T(8,128)(2,1)S(1)}, u32[]{:S(2)}, u32[]{:S(2)}) collective-permute-start(bf16[320,1280]{1,0:T(8,128)(2,1)S(1)} %shard_map.138), channel_id=1, source_target_pairs={{0,4},{4,0},{8,12},{12,8},{16,20},{20,16},{24,28},{28,24},{32,36},... | collective-permute-start | bytes 2457608 | tf_op jit(solution)/shard_map/ppermute | solution.py:283
  49.9 0.0 copy-done.1
  49.9 4.0 %all-to-all-start.1 = ((bf16[4,688,128]{2,1,0:T(8,128)(2,1)}), bf16[4,688,128]{2,1,0:T(8,128)(2,1)S(1)}, u32[]{:S(2)}, u32[]{:S(2)}) async-start(bf16[4,688,128]{2,1,0:T(8,128)(2,1)} %copy-done.1), calls=%async_computation.1 | async-start | bytes 1409024 | tf_op jit(solution)/shard_map/all_to_all | solution.py:304
  53.9 0.0 collective-permute-done.got_ref
  53.9 0.3 shard_map.139
  54.2 2.5 %collective-permute-start.1 = (bf16[160,1280]{1,0:T(8,128)(2,1)S(1)}, bf16[160,1280]{1,0:T(8,128)(2,1)S(1)}, u32[]{:S(2)}, u32[]{:S(2)}) collective-permute-start(bf16[160,1280]{1,0:T(8,128)(2,1)S(1)} %shard_map.139), channel_id=1, source_target_pairs={{0,8},{4,68},{8,0},{12,76},{16,24},{20,84},{24,16},{28,92},{32,40}... | collective-permute-start | bytes 1228808 | tf_op jit(solution)/shard_map/ppermute | solution.py:283
  56.8 6.4 %collective-permute-done.1.pair_ref = bf16[160,1280]{1,0:T(8,128)(2,1)S(1)} collective-permute-done((bf16[160,1280]{1,0:T(8,128)(2,1)S(1)}, bf16[160,1280]{1,0:T(8,128)(2,1)S(1)}, u32[]{:S(2)}, u32[]{:S(2)}) %collective-permute-start.1) | collective-permute-done | bytes 409632 | tf_op jit(solution)/shard_map/ppermute | solution.py:283
  63.2 1.0 %shard_map.140.wg_ref = bf16[256,1152]{1,0:T(8,128)(2,1)S(1)} custom-call(bf16[256,1280]{1,0:T(8,128)(2,1)S(1)} %get-tuple-element.31.ng_ref, bf16[1408,128]{1,0:T(8,128)(2,1)S(1)} %get-tuple-element.30.heads_ref, bf16[320,1280]{1,0:T(8,128)(2,1)S(1)} %collective-permute-done.got_ref, bf16[160,1280]{1,0:T(8,128)(2,1)S(1)} %collective-permute-done.1.pair_ref), custom_call_target="tpu_custom_call" | custom-call | tf_op jit(solution)/shard_map/pallas_call | solution.py:32
  64.2 0.9 %all-to-all-done.1.pn_ref = bf16[4,688,128]{2,1,0:T(8,128)(2,1)S(1)} async-done(((bf16[4,688,128]{2,1,0:T(8,128)(2,1)}), bf16[4,688,128]{2,1,0:T(8,128)(2,1)S(1)}, u32[]{:S(2)}, u32[]{:S(2)}) %all-to-all-start.1) | async-done | bytes 704544 | tf_op jit(solution)/shard_map/all_to_all | solution.py:304
  65.2 1.0 %shard_map.141 = bf16[128,2,1152]{2,1,0:T(2,128)(2,1)S(1)} custom-call(bf16[4,688,128]{2,1,0:T(8,128)(2,1)S(1)} %all-to-all-done.1.pn_ref, f32[136,128]{1,0:T(8,128)S(1)} %get-tuple-element.29.stat_ref, bf16[1408,128]{1,0:T(8,128)(2,1)S(1)} %get-tuple-element.30.heads_ref, bf16[256,1152]{1,0:T(8,128)(2,1)S(1)} %shard_map.140.wg_ref), custom_call_target="tpu_custom_call" | custom-call | tf_op jit(solution)/shard_map/pallas_call | solution.py:32
  66.1 26.6 %all_to_all.16.b_ref = bf16[128,2,1152]{2,1,0:T(2,128)(2,1)S(1)} all-to-all(bf16[128,2,1152]{2,1,0:T(2,128)(2,1)S(1)} %shard_map.141), channel_id=1, replica_groups=mesh['dp'=128,'zero'=4] {'dp'}, dimensions={0} | all-to-all | bytes 1179648 | tf_op jit(solution)/shard_map/all_to_all | solution.py:314
  92.8 1.1 %shard_map.142 = (bf16[320,128]{1,0:T(8,128)(2,1)}, bf16[320,128]{1,0:T(8,128)(2,1)}, f32[10,3,2,80]{3,2,1,0:T(2,128)}, f32[10,2,80]{2,1,0:T(2,128)}, f32[1,10]{1,0:T(1,128)}, /*index=5*/f32[1,10]{1,0:T(1,128)}) custom-call(bf16[128,256]{1,0:T(8,128)(2,1)S(1)} %get-tuple-element.22.odd_ref, bf16[128,2,1152]{2,1,0:T(2,128)(2,1)S(1)} %all_to_all.16.b_ref), custom_call_target="tpu_custom_call" | custom-call | tf_op jit(solution)/shard_map/pallas_call | solution.py:32
Async XLA Ops:
  0.6 1.2 %copy-start.2 = (bf16[2,80,1280]{2,1,0:T(8,128)(2,1)S(1)}, bf16[2,80,1280]{2,1,0:T(8,128)(2,1)}, u32[]{:S(2)}) copy-start(bf16[2,80,1280]{2,1,0:T(8,128)(2,1)} %param.17) | copy-start | bytes 1228804
  0.6 1.2 %copy-start.4 = (f32[1280]{0:T(1024)S(1)}, f32[1280]{0:T(1024)}, u32[]{:S(2)}) copy-start(f32[1280]{0:T(1024)} %bias_ref.1) | copy-start | bytes 15364
  0.7 1.2 %copy-start.3 = (f32[1280]{0:T(1024)S(1)}, f32[1280]{0:T(1024)}, u32[]{:S(2)}) copy-start(f32[1280]{0:T(1024)} %gain_ref.1) | copy-start | bytes 15364
  0.7 1.2 %copy-start.7 = (s32[1,128]{1,0:T(1,128)S(1)}, s32[1,128]{1,0:T(1,128)}, u32[]{:S(2)}) copy-start(s32[1,128]{1,0:T(1,128)} %seg_ref.1) | copy-start | bytes 1540
  0.7 1.2 %copy-start.6 = (s32[1,128]{1,0:T(1,128)S(1)}, s32[1,128]{1,0:T(1,128)}, u32[]{:S(2)}) copy-start(s32[1,128]{1,0:T(1,128)} %recv_ref.1) | copy-start | bytes 1540
  0.7 1.2 %copy-start.5 = (s32[1,128]{1,0:T(1,128)S(1)}, s32[1,128]{1,0:T(1,128)}, u32[]{:S(2)}) copy-start(s32[1,128]{1,0:T(1,128)} %send_ref.1) | copy-start | bytes 1540
  1.9 41.2 %copy-start = (bf16[1280,2,3,80]{0,3,2,1:T(8,128)(2,1)S(1)}, bf16[1280,2,3,80]{0,3,2,1:T(8,128)(2,1)}, u32[]{:S(2)}) copy-start(bf16[1280,2,3,80]{0,3,2,1:T(8,128)(2,1)} %param.16) | copy-start | bytes 3686404
  45.7 4.2 %copy-start.1 = (bf16[4,688,128]{2,1,0:T(8,128)(2,1)}, bf16[4,688,128]{2,1,0:T(8,128)(2,1)S(1)}, u32[]{:S(2)}) copy-start(bf16[4,688,128]{2,1,0:T(8,128)(2,1)S(1)} %get-tuple-element.28) | copy-start | bytes 2113540
  46.1 7.8 %collective-permute-start = (bf16[320,1280]{1,0:T(8,128)(2,1)S(1)}, bf16[320,1280]{1,0:T(8,128)(2,1)S(1)}, u32[]{:S(2)}, u32[]{:S(2)}) collective-permute-start(bf16[320,1280]{1,0:T(8,128)(2,1)S(1)} %shard_map.138), channel_id=1, source_target_pairs={{0,4},{4,0},{8,12},{12,8},{16,20},{20,16},{24,28},{28,24},{32,36},... | collective-permute-start | bytes 2457608 | tf_op jit(solution)/shard_map/ppermute | solution.py:283
  49.9 15.3 %all-to-all-start.1 = ((bf16[4,688,128]{2,1,0:T(8,128)(2,1)}), bf16[4,688,128]{2,1,0:T(8,128)(2,1)S(1)}, u32[]{:S(2)}, u32[]{:S(2)}) async-start(bf16[4,688,128]{2,1,0:T(8,128)(2,1)} %copy-done.1), calls=%async_computation.1 | async-start | bytes 1409024 | tf_op jit(solution)/shard_map/all_to_all | solution.py:304
  54.2 9.0 %collective-permute-start.1 = (bf16[160,1280]{1,0:T(8,128)(2,1)S(1)}, bf16[160,1280]{1,0:T(8,128)(2,1)S(1)}, u32[]{:S(2)}, u32[]{:S(2)}) collective-permute-start(bf16[160,1280]{1,0:T(8,128)(2,1)S(1)} %shard_map.139), channel_id=1, source_target_pairs={{0,8},{4,68},{8,0},{12,76},{16,24},{20,84},{24,16},{28,92},{32,40}... | collective-permute-start | bytes 1228808 | tf_op jit(solution)/shard_map/ppermute | solution.py:283

commit v11 on v10

--- a/solution.py
+++ b/solution.py
@@ -200,9 +200,13 @@
     send_ref[...] = half_rows(c, 1 - half, ng_ref, heads_ref, got_ref).astype(BF)
 
 
-def weights_body(ng_ref, heads_ref, got_ref, pair_ref, o_ref, first_ref, second_ref):
+def own_body(ng_ref, heads_ref, got_ref, own_ref):
     c, half = place_bits()
-    wg = half_rows(c, half, ng_ref, heads_ref, got_ref) + pair_ref[...].astype(F32)
+    own_ref[...] = half_rows(c, half, ng_ref, heads_ref, got_ref)
+
+
+def weights_body(own_ref, pair_ref, o_ref, first_ref, second_ref):
+    wg = own_ref[...] + pair_ref[...].astype(F32)
     first_ref[:, :HD] = wg[:HD].T
     second_ref[:, :HD] = wg[HD:].T
     slabs = []
@@ -304,9 +308,10 @@
     pn = lax.all_to_all(pn, "zero", 0, 0, tiled=True)
     (pair,) = call(pair_body, [((2 * HD, D), BF)], ng, heads, got)
     pair = swap(pair, partner)
+    (own,) = call(own_body, [((2 * HD, D), F32)], ng, heads, got)
     scratch = pltpu.VMEM((D, R), F32)
     (wg,) = call(
-        weights_body, [((2 * R, HALF), BF)], ng, heads, got, pair, scratch=[scratch] * 2
+        weights_body, [((2 * R, HALF), BF)], own, pair, scratch=[scratch] * 2
     )
     (back,) = call(
         post_body, [((R, 2, HALF), BF)], pn, stat, heads, wg, scratch=[scratch]

time: 94.2 us -> 94.2 us (level)
    pallas_call x7 -> x8, Pallas kernels: 6.97 us -> 7.11 us  [call(): pl.pallas_call(body, out_shape=tuple((jax.ShapeDtypeStruct(s, d) for s, d...]
  transfers between devices with their start and end apart: 3 -> 3, of which waited for: 2 -> 2; matrix products, arithmetic and copies ran while one was open for 0% -> 0% of each run, Pallas kernels for 1% -> 2%
where the time goes in v11:
time: 94.2 us; the launch traced here: 93.9 us
  blocking collectives  67.2 us (71%)
  starting transfers between devices  10.4 us (11%)
  waiting for transfers between devices  7.24 us (8%)
  Pallas kernels  7.11 us (8%)
  other arithmetic  1.16 us (1%)
    all_to_all x1, blocking collectives, local(): xg = lax.all_to_all(xg, 'dp', 0, 0, tiled=True)  40.6 us
    all_to_all x1, blocking collectives, local(): back = lax.all_to_all(back, 'dp', 0, 0, tiled=True)  26.6 us
    pallas_call x8, Pallas kernels, call(): pl.pallas_call(body, out_shape=tuple((jax.ShapeDtypeStruct(s, d) for s, d...  7.11 us
    ppermute x2, starting transfers between devices, swap(): return lax.ppermute(a, 'dp', [(i, other(i)) for i in range(128)])  6.33 us
    ppermute x2, waiting for transfers between devices, swap(): return lax.ppermute(a, 'dp', [(i, other(i)) for i in range(128)])  6.16 us
    all_to_all x1, starting transfers between devices, local(): pn = lax.all_to_all(pn, 'zero', 0, 0, tiled=True)  4.02 us
  transfers between devices with their start and end apart: 3, of which 2 were waited for; matrix products, arithmetic and copies ran while one was open for 0% of the time, Pallas kernels for 2%

profile of v11, /device:TPU:1, one launch (start us, length us, event | category | flops | bytes accessed | tf_op | source)
XLA Modules:
  0.0 93.9 jit_solution(9973545349454208642)
XLA Ops:
  0.6 0.0 copy-start.2
  0.6 0.0 copy-start.4
  0.7 0.0 copy-start.3
  0.7 0.0 copy-start.7
  0.7 0.0 copy-start.6
  0.7 0.0 copy-start.5
  0.7 1.2 %pad_maximum_fusion.xg_ref = bf16[256,1280]{1,0:T(8,128)(2,1)S(1)} fusion(bf16[128,1280]{1,0:T(8,128)(2,1)} %param.10, bf16[128,1280]{1,0:T(8,128)(2,1)} %param.9), kind=kLoop, calls=%fused_computation | loop fusion | flops 1310720 | bytes 1310720 | tf_op jit(solution)/shard_map/concatenate | solution.py:289
  1.9 0.0 copy-start
  1.9 0.0 copy-done.2
  1.9 0.0 copy-done.4
  1.9 0.0 copy-done.3
  1.9 0.0 copy-done.7
  1.9 0.0 copy-done.6
  1.9 0.0 copy-done.5
  1.9 0.6 shard_map.136
  2.5 40.6 %all_to_all.15.xg_ref = bf16[128,2,1280]{2,1,0:T(2,128)(2,1)S(1)} all-to-all(bf16[128,2,1280]{2,1,0:T(2,128)(2,1)S(1)} %get-tuple-element.23), channel_id=1, replica_groups=mesh['dp'=128,'zero'=4] {'dp'}, dimensions={0} | all-to-all | bytes 1310720 | tf_op jit(solution)/shard_map/all_to_all | solution.py:295
  43.0 0.0 copy-done
  43.0 2.7 %shard_map.137 = (bf16[4,688,128]{2,1,0:T(8,128)(2,1)S(1)}, bf16[256,1280]{1,0:T(8,128)(2,1)S(1)}, bf16[1408,128]{1,0:T(8,128)(2,1)S(1)}, f32[136,128]{1,0:T(8,128)S(1)}) custom-call(bf16[128,2,1280]{2,1,0:T(2,128)(2,1)S(1)} %all_to_all.15.xg_ref, f32[128,128]{1,0:T(8,128)S(1)} %get-tuple-element.24.same_ref, f32[1,1280]{1,0:T(1,128)S(1)} %get-tuple-element.25.gain_ref, ...), custom_call_target="tpu_custom_call" | custom-call | tf_op jit(solution)/shard_map/pallas_call | solution.py:32
  45.7 0.0 copy-start.1
  45.7 0.4 shard_map.138
  46.1 3.8 %collective-permute-start = (bf16[320,1280]{1,0:T(8,128)(2,1)S(1)}, bf16[320,1280]{1,0:T(8,128)(2,1)S(1)}, u32[]{:S(2)}, u32[]{:S(2)}) collective-permute-start(bf16[320,1280]{1,0:T(8,128)(2,1)S(1)} %shard_map.138), channel_id=1, source_target_pairs={{0,4},{4,0},{8,12},{12,8},{16,20},{20,16},{24,28},{28,24},{32,36},... | collective-permute-start | bytes 2457608 | tf_op jit(solution)/shard_map/ppermute | solution.py:287
  49.9 0.0 copy-done.1
  49.9 4.0 %all-to-all-start.1 = ((bf16[4,688,128]{2,1,0:T(8,128)(2,1)}), bf16[4,688,128]{2,1,0:T(8,128)(2,1)S(1)}, u32[]{:S(2)}, u32[]{:S(2)}) async-start(bf16[4,688,128]{2,1,0:T(8,128)(2,1)} %copy-done.1), calls=%async_computation.1 | async-start | bytes 1409024 | tf_op jit(solution)/shard_map/all_to_all | solution.py:308
  53.9 0.0 collective-permute-done.got_ref
  53.9 0.3 shard_map.140
  54.2 2.5 %collective-permute-start.1 = (bf16[160,1280]{1,0:T(8,128)(2,1)S(1)}, bf16[160,1280]{1,0:T(8,128)(2,1)S(1)}, u32[]{:S(2)}, u32[]{:S(2)}) collective-permute-start(bf16[160,1280]{1,0:T(8,128)(2,1)S(1)} %shard_map.140), channel_id=1, source_target_pairs={{0,8},{4,68},{8,0},{12,76},{16,24},{20,84},{24,16},{28,92},{32,40}... | collective-permute-start | bytes 1228808 | tf_op jit(solution)/shard_map/ppermute | solution.py:287
  56.8 0.3 shard_map.139.own_ref
  57.1 6.2 %collective-permute-done.1.pair_ref = bf16[160,1280]{1,0:T(8,128)(2,1)S(1)} collective-permute-done((bf16[160,1280]{1,0:T(8,128)(2,1)S(1)}, bf16[160,1280]{1,0:T(8,128)(2,1)S(1)}, u32[]{:S(2)}, u32[]{:S(2)}) %collective-permute-start.1) | collective-permute-done | bytes 409632 | tf_op jit(solution)/shard_map/ppermute | solution.py:287
  63.2 0.9 shard_map.141.wg_ref
  64.1 1.1 %all-to-all-done.1.pn_ref = bf16[4,688,128]{2,1,0:T(8,128)(2,1)S(1)} async-done(((bf16[4,688,128]{2,1,0:T(8,128)(2,1)}), bf16[4,688,128]{2,1,0:T(8,128)(2,1)S(1)}, u32[]{:S(2)}, u32[]{:S(2)}) %all-to-all-start.1) | async-done | bytes 704544 | tf_op jit(solution)/shard_map/all_to_all | solution.py:308
  65.2 1.0 %shard_map.142 = bf16[128,2,1152]{2,1,0:T(2,128)(2,1)S(1)} custom-call(bf16[4,688,128]{2,1,0:T(8,128)(2,1)S(1)} %all-to-all-done.1.pn_ref, f32[136,128]{1,0:T(8,128)S(1)} %get-tuple-element.29.stat_ref, bf16[1408,128]{1,0:T(8,128)(2,1)S(1)} %get-tuple-element.30.heads_ref, bf16[256,1152]{1,0:T(8,128)(2,1)S(1)} %shard_map.141.wg_ref), custom_call_target="tpu_custom_call" | custom-call | tf_op jit(solution)/shard_map/pallas_call | solution.py:32
  66.2 26.6 %all_to_all.16.b_ref = bf16[128,2,1152]{2,1,0:T(2,128)(2,1)S(1)} all-to-all(bf16[128,2,1152]{2,1,0:T(2,128)(2,1)S(1)} %shard_map.142), channel_id=1, replica_groups=mesh['dp'=128,'zero'=4] {'dp'}, dimensions={0} | all-to-all | bytes 1179648 | tf_op jit(solution)/shard_map/all_to_all | solution.py:319
  92.8 1.1 %shard_map.143 = (bf16[320,128]{1,0:T(8,128)(2,1)}, bf16[320,128]{1,0:T(8,128)(2,1)}, f32[10,3,2,80]{3,2,1,0:T(2,128)}, f32[10,2,80]{2,1,0:T(2,128)}, f32[1,10]{1,0:T(1,128)}, /*index=5*/f32[1,10]{1,0:T(1,128)}) custom-call(bf16[128,256]{1,0:T(8,128)(2,1)S(1)} %get-tuple-element.22.odd_ref, bf16[128,2,1152]{2,1,0:T(2,128)(2,1)S(1)} %all_to_all.16.b_ref), custom_call_target="tpu_custom_call" | custom-call | tf_op jit(solution)/shard_map/pallas_call | solution.py:32
Async XLA Ops:
  0.6 1.2 %copy-start.2 = (bf16[2,80,1280]{2,1,0:T(8,128)(2,1)S(1)}, bf16[2,80,1280]{2,1,0:T(8,128)(2,1)}, u32[]{:S(2)}) copy-start(bf16[2,80,1280]{2,1,0:T(8,128)(2,1)} %param.17) | copy-start | bytes 1228804
  0.6 1.2 %copy-start.4 = (f32[1280]{0:T(1024)S(1)}, f32[1280]{0:T(1024)}, u32[]{:S(2)}) copy-start(f32[1280]{0:T(1024)} %bias_ref.1) | copy-start | bytes 15364
  0.7 1.2 %copy-start.3 = (f32[1280]{0:T(1024)S(1)}, f32[1280]{0:T(1024)}, u32[]{:S(2)}) copy-start(f32[1280]{0:T(1024)} %gain_ref.1) | copy-start | bytes 15364
  0.7 1.2 %copy-start.7 = (s32[1,128]{1,0:T(1,128)S(1)}, s32[1,128]{1,0:T(1,128)}, u32[]{:S(2)}) copy-start(s32[1,128]{1,0:T(1,128)} %seg_ref.1) | copy-start | bytes 1540
  0.7 1.2 %copy-start.6 = (s32[1,128]{1,0:T(1,128)S(1)}, s32[1,128]{1,0:T(1,128)}, u32[]{:S(2)}) copy-start(s32[1,128]{1,0:T(1,128)} %recv_ref.1) | copy-start | bytes 1540
  0.7 1.2 %copy-start.5 = (s32[1,128]{1,0:T(1,128)S(1)}, s32[1,128]{1,0:T(1,128)}, u32[]{:S(2)}) copy-start(s32[1,128]{1,0:T(1,128)} %send_ref.1) | copy-start | bytes 1540
  1.9 41.2 %copy-start = (bf16[1280,2,3,80]{0,3,2,1:T(8,128)(2,1)S(1)}, bf16[1280,2,3,80]{0,3,2,1:T(8,128)(2,1)}, u32[]{:S(2)}) copy-start(bf16[1280,2,3,80]{0,3,2,1:T(8,128)(2,1)} %param.16) | copy-start | bytes 3686404
  45.7 4.2 %copy-start.1 = (bf16[4,688,128]{2,1,0:T(8,128)(2,1)}, bf16[4,688,128]{2,1,0:T(8,128)(2,1)S(1)}, u32[]{:S(2)}) copy-start(bf16[4,688,128]{2,1,0:T(8,128)(2,1)S(1)} %get-tuple-element.28) | copy-start | bytes 2113540
  46.1 7.8 %collective-permute-start = (bf16[320,1280]{1,0:T(8,128)(2,1)S(1)}, bf16[320,1280]{1,0:T(8,128)(2,1)S(1)}, u32[]{:S(2)}, u32[]{:S(2)}) collective-permute-start(bf16[320,1280]{1,0:T(8,128)(2,1)S(1)} %shard_map.138), channel_id=1, source_target_pairs={{0,4},{4,0},{8,12},{12,8},{16,20},{20,16},{24,28},{28,24},{32,36},... | collective-permute-start | bytes 2457608 | tf_op jit(solution)/shard_map/ppermute | solution.py:287
  49.9 15.3 %all-to-all-start.1 = ((bf16[4,688,128]{2,1,0:T(8,128)(2,1)}), bf16[4,688,128]{2,1,0:T(8,128)(2,1)S(1)}, u32[]{:S(2)}, u32[]{:S(2)}) async-start(bf16[4,688,128]{2,1,0:T(8,128)(2,1)} %copy-done.1), calls=%async_computation.1 | async-start | bytes 1409024 | tf_op jit(solution)/shard_map/all_to_all | solution.py:308
  54.2 9.0 %collective-permute-start.1 = (bf16[160,1280]{1,0:T(8,128)(2,1)S(1)}, bf16[160,1280]{1,0:T(8,128)(2,1)S(1)}, u32[]{:S(2)}, u32[]{:S(2)}) collective-permute-start(bf16[160,1280]{1,0:T(8,128)(2,1)S(1)} %shard_map.140), channel_id=1, source_target_pairs={{0,8},{4,68},{8,0},{12,76},{16,24},{20,84},{24,16},{28,92},{32,40}... | collective-permute-start | bytes 1228808 | tf_op jit(solution)/shard_map/ppermute | solution.py:287

commit v12 on v10

--- a/solution.py
+++ b/solution.py
@@ -200,11 +200,17 @@
     send_ref[...] = half_rows(c, 1 - half, ng_ref, heads_ref, got_ref).astype(BF)
 
 
-def weights_body(ng_ref, heads_ref, got_ref, pair_ref, o_ref, first_ref, second_ref):
+def own_body(ng_ref, heads_ref, got_ref, first_ref, second_ref):
     c, half = place_bits()
-    wg = half_rows(c, half, ng_ref, heads_ref, got_ref) + pair_ref[...].astype(F32)
-    first_ref[:, :HD] = wg[:HD].T
-    second_ref[:, :HD] = wg[HD:].T
+    own = half_rows(c, half, ng_ref, heads_ref, got_ref)
+    first_ref[:, :HD] = own[:HD].T
+    second_ref[:, :HD] = own[HD:].T
+
+
+def weights_body(own_first, own_second, pair_ref, o_ref, first_ref, second_ref):
+    pair = pair_ref[...].astype(F32)
+    first_ref[:, :HD] = own_first[:, :HD] + pair[:HD].T
+    second_ref[:, :HD] = own_second[:, :HD] + pair[HD:].T
     slabs = []
     for i in range(10):
         rows = pl.ds(i, R, stride=10)
@@ -304,9 +310,10 @@
     pn = lax.all_to_all(pn, "zero", 0, 0, tiled=True)
     (pair,) = call(pair_body, [((2 * HD, D), BF)], ng, heads, got)
     pair = swap(pair, partner)
+    own = call(own_body, [((D, R), F32)] * 2, ng, heads, got)
     scratch = pltpu.VMEM((D, R), F32)
     (wg,) = call(
-        weights_body, [((2 * R, HALF), BF)], ng, heads, got, pair, scratch=[scratch] * 2
+        weights_body, [((2 * R, HALF), BF)], *own, pair, scratch=[scratch] * 2
     )
     (back,) = call(
         post_body, [((R, 2, HALF), BF)], pn, stat, heads, wg, scratch=[scratch]

time: 94.2 us -> 94.3 us (level)
    pallas_call x7 -> x8, Pallas kernels: 6.97 us -> 7.26 us  [call(): pl.pallas_call(body, out_shape=tuple((jax.ShapeDtypeStruct(s, d) for s, d...]
  transfers between devices with their start and end apart: 3 -> 3, of which waited for: 2 -> 2; matrix products, arithmetic and copies ran while one was open for 0% -> 0% of each run, Pallas kernels for 1% -> 2%
where the time goes in v12:
time: 94.3 us; the launch traced here: 93.9 us
  blocking collectives  67.2 us (71%)
  starting transfers between devices  10.4 us (11%)
  Pallas kernels  7.26 us (8%)
  waiting for transfers between devices  7.09 us (8%)
  other arithmetic  1.17 us (1%)
    all_to_all x1, blocking collectives, local(): xg = lax.all_to_all(xg, 'dp', 0, 0, tiled=True)  40.6 us
    all_to_all x1, blocking collectives, local(): back = lax.all_to_all(back, 'dp', 0, 0, tiled=True)  26.6 us
    pallas_call x8, Pallas kernels, call(): pl.pallas_call(body, out_shape=tuple((jax.ShapeDtypeStruct(s, d) for s, d...  7.26 us
    ppermute x2, starting transfers between devices, swap(): return lax.ppermute(a, 'dp', [(i, other(i)) for i in range(128)])  6.33 us
    ppermute x2, waiting for transfers between devices, swap(): return lax.ppermute(a, 'dp', [(i, other(i)) for i in range(128)])  5.86 us
    all_to_all x1, starting transfers between devices, local(): pn = lax.all_to_all(pn, 'zero', 0, 0, tiled=True)  4.03 us
  transfers between devices with their start and end apart: 3, of which 2 were waited for; matrix products, arithmetic and copies ran while one was open for 0% of the time, Pallas kernels for 2%

profile of v12, /device:TPU:1, one launch (start us, length us, event | category | flops | bytes accessed | tf_op | source)
XLA Modules:
  0.0 93.9 jit_solution(5190161656519641677)
XLA Ops:
  0.6 0.0 copy-start.5
  0.6 0.0 copy-start.6
  0.7 0.0 copy-start.7
  0.7 0.0 copy-start.3
  0.7 0.0 copy-start.4
  0.7 0.0 copy-start.2
  0.7 1.2 %pad_maximum_fusion.xg_ref = bf16[256,1280]{1,0:T(8,128)(2,1)S(1)} fusion(bf16[128,1280]{1,0:T(8,128)(2,1)} %param.10, bf16[128,1280]{1,0:T(8,128)(2,1)} %param.9), kind=kLoop, calls=%fused_computation | loop fusion | flops 1310720 | bytes 1310720 | tf_op jit(solution)/shard_map/concatenate | solution.py:291
  1.9 0.0 copy-start
  1.9 0.0 copy-done.5
  1.9 0.0 copy-done.6
  1.9 0.0 copy-done.7
  1.9 0.0 copy-done.3
  1.9 0.0 copy-done.4
  1.9 0.0 copy-done.2
  1.9 0.6 shard_map.136
  2.5 40.6 %all_to_all.15.xg_ref = bf16[128,2,1280]{2,1,0:T(2,128)(2,1)S(1)} all-to-all(bf16[128,2,1280]{2,1,0:T(2,128)(2,1)S(1)} %get-tuple-element.25), channel_id=1, replica_groups=mesh['dp'=128,'zero'=4] {'dp'}, dimensions={0} | all-to-all | bytes 1310720 | tf_op jit(solution)/shard_map/all_to_all | solution.py:297
  43.1 0.0 copy-done
  43.1 2.7 %shard_map.137 = (bf16[4,688,128]{2,1,0:T(8,128)(2,1)S(1)}, bf16[256,1280]{1,0:T(8,128)(2,1)S(1)}, bf16[1408,128]{1,0:T(8,128)(2,1)S(1)}, f32[136,128]{1,0:T(8,128)S(1)}) custom-call(bf16[128,2,1280]{2,1,0:T(2,128)(2,1)S(1)} %all_to_all.15.xg_ref, f32[128,128]{1,0:T(8,128)S(1)} %get-tuple-element.26.same_ref, f32[1,1280]{1,0:T(1,128)S(1)} %get-tuple-element.27.gain_ref, ...), custom_call_target="tpu_custom_call" | custom-call | tf_op jit(solution)/shard_map/pallas_call | solution.py:32
  45.7 0.0 copy-start.1
  45.7 0.4 shard_map.138
  46.1 3.8 %collective-permute-start = (bf16[320,1280]{1,0:T(8,128)(2,1)S(1)}, bf16[320,1280]{1,0:T(8,128)(2,1)S(1)}, u32[]{:S(2)}, u32[]{:S(2)}) collective-permute-start(bf16[320,1280]{1,0:T(8,128)(2,1)S(1)} %shard_map.138), channel_id=1, source_target_pairs={{0,4},{4,0},{8,12},{12,8},{16,20},{20,16},{24,28},{28,24},{32,36},... | collective-permute-start | bytes 2457608 | tf_op jit(solution)/shard_map/ppermute | solution.py:289
  49.9 0.0 copy-done.1
  49.9 4.0 %all-to-all-start.1 = ((bf16[4,688,128]{2,1,0:T(8,128)(2,1)}), bf16[4,688,128]{2,1,0:T(8,128)(2,1)S(1)}, u32[]{:S(2)}, u32[]{:S(2)}) async-start(bf16[4,688,128]{2,1,0:T(8,128)(2,1)} %copy-done.1), calls=%async_computation.1 | async-start | bytes 1409024 | tf_op jit(solution)/shard_map/all_to_all | solution.py:310
  54.0 0.0 collective-permute-done.got_ref
  54.0 0.3 shard_map.140
  54.2 2.5 %collective-permute-start.1 = (bf16[160,1280]{1,0:T(8,128)(2,1)S(1)}, bf16[160,1280]{1,0:T(8,128)(2,1)S(1)}, u32[]{:S(2)}, u32[]{:S(2)}) collective-permute-start(bf16[160,1280]{1,0:T(8,128)(2,1)S(1)} %shard_map.140), channel_id=1, source_target_pairs={{0,8},{4,68},{8,0},{12,76},{16,24},{20,84},{24,16},{28,92},{32,40}... | collective-permute-start | bytes 1228808 | tf_op jit(solution)/shard_map/ppermute | solution.py:289
  56.8 0.6 shard_map.139
  57.4 5.9 %collective-permute-done.1.pair_ref = bf16[160,1280]{1,0:T(8,128)(2,1)S(1)} collective-permute-done((bf16[160,1280]{1,0:T(8,128)(2,1)S(1)}, bf16[160,1280]{1,0:T(8,128)(2,1)S(1)}, u32[]{:S(2)}, u32[]{:S(2)}) %collective-permute-start.1) | collective-permute-done | bytes 409632 | tf_op jit(solution)/shard_map/ppermute | solution.py:289
  63.2 0.7 shard_map.141.wg_ref
  64.0 1.2 %all-to-all-done.1.pn_ref = bf16[4,688,128]{2,1,0:T(8,128)(2,1)S(1)} async-done(((bf16[4,688,128]{2,1,0:T(8,128)(2,1)}), bf16[4,688,128]{2,1,0:T(8,128)(2,1)S(1)}, u32[]{:S(2)}, u32[]{:S(2)}) %all-to-all-start.1) | async-done | bytes 704544 | tf_op jit(solution)/shard_map/all_to_all | solution.py:310
  65.2 1.0 %shard_map.142 = bf16[128,2,1152]{2,1,0:T(2,128)(2,1)S(1)} custom-call(bf16[4,688,128]{2,1,0:T(8,128)(2,1)S(1)} %all-to-all-done.1.pn_ref, f32[136,128]{1,0:T(8,128)S(1)} %get-tuple-element.31.stat_ref, bf16[1408,128]{1,0:T(8,128)(2,1)S(1)} %get-tuple-element.32.heads_ref, bf16[256,1152]{1,0:T(8,128)(2,1)S(1)} %shard_map.141.wg_ref), custom_call_target="tpu_custom_call" | custom-call | tf_op jit(solution)/shard_map/pallas_call | solution.py:32
  66.2 26.6 %all_to_all.16.b_ref = bf16[128,2,1152]{2,1,0:T(2,128)(2,1)S(1)} all-to-all(bf16[128,2,1152]{2,1,0:T(2,128)(2,1)S(1)} %shard_map.142), channel_id=1, replica_groups=mesh['dp'=128,'zero'=4] {'dp'}, dimensions={0} | all-to-all | bytes 1179648 | tf_op jit(solution)/shard_map/all_to_all | solution.py:321
  92.8 1.1 %shard_map.143 = (bf16[320,128]{1,0:T(8,128)(2,1)}, bf16[320,128]{1,0:T(8,128)(2,1)}, f32[10,3,2,80]{3,2,1,0:T(2,128)}, f32[10,2,80]{2,1,0:T(2,128)}, f32[1,10]{1,0:T(1,128)}, /*index=5*/f32[1,10]{1,0:T(1,128)}) custom-call(bf16[128,256]{1,0:T(8,128)(2,1)S(1)} %get-tuple-element.24.odd_ref, bf16[128,2,1152]{2,1,0:T(2,128)(2,1)S(1)} %all_to_all.16.b_ref), custom_call_target="tpu_custom_call" | custom-call | tf_op jit(solution)/shard_map/pallas_call | solution.py:32
Async XLA Ops:
  0.6 1.2 %copy-start.5 = (s32[1,128]{1,0:T(1,128)S(1)}, s32[1,128]{1,0:T(1,128)}, u32[]{:S(2)}) copy-start(s32[1,128]{1,0:T(1,128)} %send_ref.1) | copy-start | bytes 1540
  0.6 1.2 %copy-start.6 = (s32[1,128]{1,0:T(1,128)S(1)}, s32[1,128]{1,0:T(1,128)}, u32[]{:S(2)}) copy-start(s32[1,128]{1,0:T(1,128)} %recv_ref.1) | copy-start | bytes 1540
  0.7 1.2 %copy-start.7 = (s32[1,128]{1,0:T(1,128)S(1)}, s32[1,128]{1,0:T(1,128)}, u32[]{:S(2)}) copy-start(s32[1,128]{1,0:T(1,128)} %seg_ref.1) | copy-start | bytes 1540
  0.7 1.2 %copy-start.3 = (f32[1280]{0:T(1024)S(1)}, f32[1280]{0:T(1024)}, u32[]{:S(2)}) copy-start(f32[1280]{0:T(1024)} %gain_ref.1) | copy-start | bytes 15364
  0.7 1.2 %copy-start.4 = (f32[1280]{0:T(1024)S(1)}, f32[1280]{0:T(1024)}, u32[]{:S(2)}) copy-start(f32[1280]{0:T(1024)} %bias_ref.1) | copy-start | bytes 15364
  0.7 1.2 %copy-start.2 = (bf16[2,80,1280]{2,1,0:T(8,128)(2,1)S(1)}, bf16[2,80,1280]{2,1,0:T(8,128)(2,1)}, u32[]{:S(2)}) copy-start(bf16[2,80,1280]{2,1,0:T(8,128)(2,1)} %param.17) | copy-start | bytes 1228804
  1.9 41.2 %copy-start = (bf16[1280,2,3,80]{0,3,2,1:T(8,128)(2,1)S(1)}, bf16[1280,2,3,80]{0,3,2,1:T(8,128)(2,1)}, u32[]{:S(2)}) copy-start(bf16[1280,2,3,80]{0,3,2,1:T(8,128)(2,1)} %param.16) | copy-start | bytes 3686404
  45.7 4.2 %copy-start.1 = (bf16[4,688,128]{2,1,0:T(8,128)(2,1)}, bf16[4,688,128]{2,1,0:T(8,128)(2,1)S(1)}, u32[]{:S(2)}) copy-start(bf16[4,688,128]{2,1,0:T(8,128)(2,1)S(1)} %get-tuple-element.30) | copy-start | bytes 2113540
  46.1 7.8 %collective-permute-start = (bf16[320,1280]{1,0:T(8,128)(2,1)S(1)}, bf16[320,1280]{1,0:T(8,128)(2,1)S(1)}, u32[]{:S(2)}, u32[]{:S(2)}) collective-permute-start(bf16[320,1280]{1,0:T(8,128)(2,1)S(1)} %shard_map.138), channel_id=1, source_target_pairs={{0,4},{4,0},{8,12},{12,8},{16,20},{20,16},{24,28},{28,24},{32,36},... | collective-permute-start | bytes 2457608 | tf_op jit(solution)/shard_map/ppermute | solution.py:289
  49.9 15.3 %all-to-all-start.1 = ((bf16[4,688,128]{2,1,0:T(8,128)(2,1)}), bf16[4,688,128]{2,1,0:T(8,128)(2,1)S(1)}, u32[]{:S(2)}, u32[]{:S(2)}) async-start(bf16[4,688,128]{2,1,0:T(8,128)(2,1)} %copy-done.1), calls=%async_computation.1 | async-start | bytes 1409024 | tf_op jit(solution)/shard_map/all_to_all | solution.py:310
  54.2 9.0 %collective-permute-start.1 = (bf16[160,1280]{1,0:T(8,128)(2,1)S(1)}, bf16[160,1280]{1,0:T(8,128)(2,1)S(1)}, u32[]{:S(2)}, u32[]{:S(2)}) collective-permute-start(bf16[160,1280]{1,0:T(8,128)(2,1)S(1)} %shard_map.140), channel_id=1, source_target_pairs={{0,8},{4,68},{8,0},{12,76},{16,24},{20,84},{24,16},{28,92},{32,40}... | collective-permute-start | bytes 1228808 | tf_op jit(solution)/shard_map/ppermute | solution.py:289
